TPU v7x, 32 devices: a whole 2x2x4 slice. The times are simulated.
32 devices in a mesh: sec: 4 (over z), blk: 8 (over y, x, core).
Axes of the slice: x: 2, y: 2, z: 4, core: 2. Of those that a mesh axis runs over, the one named last changes fastest.
Arguments:
- wavefunction: bfloat16 [4, 96, 128, 128], P('sec', 'blk')
- left_env: bfloat16 [4, 20, 96, 128, 128], P('sec', None, 'blk')
- right_env: bfloat16 [4, 20, 96, 128, 128], P('sec', None, 'blk')
- row_offset: int32 [4, 12], P('sec'), may hold values from 0 to 7, as said below
- sector_dims: int32 [4, 96, 2], P('sec', 'blk'), may hold values from 64 to 128
- trunc_ranks: int32 [4, 96], P('sec', 'blk'), may hold values from 32 to 128
Outputs:
- state_new: bfloat16 [4, 96, 128, 128], P('sec', 'blk')
- hstate_new: bfloat16 [4, 96, 128, 128], P('sec', 'blk')
- energy: float32 [4], P('sec')
- next_left: bfloat16 [4, 20, 96, 128, 128], P('sec', None, 'blk')
Inputs may be any that keep to these rules, and one draw needn't show every extreme that they name: The sector with up-charge u and down-charge e is stored in slot u of device (e + row_offset[u]) mod 8; in every section the offsets of some two adjacent up-charges differ by 8 / 2 modulo 8.
All inputs are finite; a program needn't handle non-finite values.
Results may differ from a plain program's by a relative error of at most 0.0067.
Values may be sent and summed in bfloat16 or wider, within the bound.
No kernel may reach another device: no remote copies, remote signals or barrier semaphores. Data moves between devices by JAX's collectives and lax.ppermute only.
A program may use at most 128 MiB of HBM per device.

v0:
```python
import functools

import jax
import jax.numpy as jnp
from jax import lax
from jax.experimental import pallas as pl
from jax.experimental.pallas import tpu as pltpu
from jax.sharding import PartitionSpec as P

GROUPS = 5
EXTRA = 16
SLACK = 128
HAM_STEP = 4
PACK_STEP = 2
UNPACK_STEP = 2
EARLY_STEP = 1
VMEM = 40 * 1024 * 1024
F32 = jnp.float32
BF16 = jnp.bfloat16


def params():
    return pltpu.CompilerParams(vmem_limit_bytes=VMEM)


def shares(kinds):
    first = tuple((c, 0, 1) for c in range(GROUPS))
    then = ((0, 1, kinds), (1, 1, 2))
    return first, then, ((1, 2, kinds), (2, 1, kinds), (3, 1, kinds), (4, 1, kinds))


def exchange(value, bit):
    length = lax.axis_size("blk")
    return lax.ppermute(value, "blk", [(i, i ^ bit) for i in range(length)])


def onward(value):
    length = lax.axis_size("sec")
    return lax.ppermute(value, "sec", [(i, i + 1) for i in range(length - 1)])


def in_hbm(value):
    return pltpu.with_memory_space_constraint(value, pltpu.HBM)


def gathered(value):
    nblk = lax.axis_size("blk")
    if nblk == 8:
        rows = value.shape[0]
        half = rows // 2 // 16 * 16
        four, two, one = exchange(value, 4), exchange(value, 2), exchange(value, 1)
        six_a, six_b = exchange(two[:half], 4), exchange(four[half:], 2)
        three, five = exchange(two, 1), exchange(four, 1)
        seven_a, seven_b = exchange(six_a, 1), exchange(six_b, 1)
        return [
            (value, 0, 0), (one, 1, 0), (two, 2, 0), (three, 3, 0), (four, 4, 0), (five, 5, 0),
            (six_a, 6, 0), (six_b, 6, half), (seven_a, 7, 0), (seven_b, 7, half),
        ]
    held = {0: value}
    bit = 1
    while bit < nblk:
        held.update({place | bit: exchange(rows, bit) for place, rows in list(held.items())})
        bit *= 2
    return [(held[place], place, 0) for place in range(nblk)]


def extras_of(pieces, nblk, body):
    found = [None] * nblk
    for rows, place, first in pieces:
        if first + rows.shape[0] == body + EXTRA:
            found[place] = rows[rows.shape[0] - EXTRA :]
    return jnp.stack(found)


def start_pieces(places, refs, scratch, sem):
    copies = []
    for (place, first), ref in zip(places, refs):
        copies.append(
            pltpu.make_async_copy(ref, scratch.at[place, pl.ds(first, ref.shape[0])], sem.at[len(copies)])
        )
        copies[-1].start()
    return copies


def source_of(c, t, offsets, device, count, nblk):
    mine = device[0]
    down = (mine - offsets[t]) & (nblk - 1)
    if c == 0:
        return 0, t, None
    if c in (1, 2):
        slot = jnp.maximum(t - 1, 0) if c == 1 else jnp.minimum(t + 1, count - 1)
        holder = (down + offsets[slot]) & (nblk - 1)
        return holder ^ mine, slot, (t >= 1) if c == 1 else (t <= count - 2)
    if c == 3:
        return ((mine - 1) & (nblk - 1)) ^ mine, t, down >= 1
    return ((mine + 1) & (nblk - 1)) ^ mine, t, down <= nblk - 2


def block_of(scratch, place, slot, width):
    return scratch[place, pl.ds(pl.multiple_of(slot * width, width), width), :]


def only(on, block):
    return block if on is None else jnp.where(on, block, jnp.zeros_like(block))


def ham_sum(x, t, lref, rref):
    kinds = lref.shape[0] // GROUPS
    zero = jnp.zeros_like(x[0])
    width = zero.shape[0]
    inner = [None] * lref.shape[0]
    for c0, c1 in ((0, 1), (2, 3)):
        both = jnp.concatenate(
            [jnp.concatenate([x[c0], zero], 1), jnp.concatenate([zero, x[c1]], 1)], 0
        )
        left = jnp.concatenate(
            [
                jnp.concatenate([lref[GROUPS * k + c0, t], lref[GROUPS * k + c1, t]], 1)
                for k in range(kinds)
            ],
            0,
        )
        pair = jnp.dot(left, both, preferred_element_type=F32).astype(BF16)
        for k in range(kinds):
            inner[GROUPS * k + c0] = pair[width * k : width * (k + 1), :width]
            inner[GROUPS * k + c1] = pair[width * k : width * (k + 1), width:]
    left = jnp.concatenate([lref[GROUPS * k + 4, t] for k in range(kinds)], 0)
    last = jnp.dot(left, x[4], preferred_element_type=F32).astype(BF16)
    for k in range(kinds):
        inner[GROUPS * k + 4] = last[width * k : width * (k + 1)]
    right = jnp.concatenate([rref[w, t] for w in range(lref.shape[0])], 1)
    return lax.dot_general(
        jnp.concatenate(inner, 1), right, (((1,), (1,)), ((), ())), preferred_element_type=F32
    )


def step_of(count, most):
    return max(p for p in range(1, most + 1) if count % p == 0)


def over_slots(count, body, most, before=None, after=None):
    per = step_of(count, most)

    def step(i, carry):
        if before is not None:
            before(i)
        for p in range(per):
            body(i * per + p)
        if after is not None:
            after(i)
        return carry

    lax.fori_loop(0, count // per, step, 0)


def env_copies(envs, count, i):
    per = step_of(count, HAM_STEP)
    span = pl.ds(i * per, per)
    return [pltpu.make_async_copy(far.at[:, span], near.at[:, span], sem.at[i]) for far, near, sem in envs]


def bring_in(envs, count, copies):
    for copy in env_copies(envs, count, 0):
        copy.start()
    for copy in copies:
        copy.wait()
    for i in range(1, count // step_of(count, HAM_STEP)):
        for copy in env_copies(envs, count, i):
            copy.start()


def arrival(envs, count):
    def before(i):
        for copy in env_copies(envs, count, i):
            copy.wait()

    return before


def inside(rows, cols, shape):
    row = lax.broadcasted_iota(jnp.int32, shape, 0)
    col = lax.broadcasted_iota(jnp.int32, shape, 1)
    return (row < rows) & (col < cols)


def total_of(value):
    return jnp.sum(jnp.sum(value, axis=0, keepdims=True), axis=1, keepdims=True)


def first_kernel(places, count, then, offsets, device, dims, *refs):
    pieces = refs[: len(places)]
    lfar, rfar, href, payload, sent, held, lref, rref, ext, sem, lsem, rsem, out_sem = refs[len(places) :]
    width = href.shape[1]
    nblk = held.shape[0]
    envs = ((lfar, lref, lsem), (rfar, rref, rsem))
    channels = [GROUPS * k + c for c, low, end in then for k in range(low, end)]
    outgoing = [pltpu.make_async_copy(lref.at[w], sent.at[i], out_sem.at[i]) for i, w in enumerate(channels)]
    ext[...] = jnp.zeros_like(ext)
    bring_in(envs, count, start_pieces(places, pieces, held, sem))
    row = lax.broadcasted_iota(jnp.int32, ext.shape, 0)
    lane = lax.broadcasted_iota(jnp.int32, ext.shape, 1)

    def slot(t):
        x = []
        for c in range(GROUPS):
            place, at, on = source_of(c, t, offsets, device, count, nblk)
            x.append(only(on, block_of(held, place, at, width)))
        h = jnp.where(inside(dims[t, 0], dims[t, 1], (width, width)), ham_sum(x, t, lref, rref), 0.0)
        href[t] = h
        v = x[0].astype(F32)
        norm, num = total_of(v * v), total_of(v * h)
        alpha = jnp.where(norm > 1e-30, num / jnp.maximum(norm, 1e-30), 0.0).astype(BF16).astype(F32)
        payload[pl.ds(pl.multiple_of(t * width, width), width), :] = (h - alpha * v).astype(BF16)
        now = jnp.where(row == t, alpha, ext[...])
        ext[...] = now + jnp.where(row == count, norm, 0.0) + jnp.where(row == count + 1, num, 0.0)

    def before(i):
        arrival(envs, count)(i)

        @pl.when(i == count // step_of(count, HAM_STEP) - 1)
        def _():
            for copy in outgoing:
                copy.start()

    over_slots(count, slot, HAM_STEP, before)
    now = ext[...]
    high = now.astype(BF16).astype(F32)
    rest = now - high
    mid = rest.astype(BF16).astype(F32)
    low = rest - mid
    split = jnp.where(lane == 0, high, jnp.where(lane == 1, mid, jnp.where(lane == 2, low, 0.0)))
    payload[pl.ds(count * width, EXTRA), :] = jnp.where(row < count, now, split).astype(BF16)
    for copy in outgoing:
        copy.wait()


def second_kernel(places, count, cells, used, offsets, device, dims, *refs):
    n = len(places)
    vpieces, rpieces = refs[:n], refs[n : 2 * n]
    lfar, rfar, gref, sums, vsrc, wsrc, vheld, rheld, lref, rref, ext, vsem, hsem, lsem, rsem = refs[2 * n :]
    width = gref.shape[1]
    nblk = vheld.shape[0]
    srow = lax.broadcasted_iota(jnp.int32, sums.shape, 0)
    envs = ((lfar, lref, lsem), (rfar, rref, rsem))
    copies = start_pieces(places, rpieces, rheld, hsem) + start_pieces(places, vpieces, vheld, vsem)
    bring_in(envs, count, copies)
    both = jnp.zeros((EXTRA, 128), F32)
    for place in range(nblk):
        part = rheld[place, pl.ds(count * width, EXTRA), :].astype(F32)
        ext[pl.ds(place * EXTRA, EXTRA), :] = part
        both = both + part
    both = jnp.sum(both, axis=1, keepdims=True)
    norm, num = both[count : count + 1], both[count + 1 : count + 2]
    sums[...] = jnp.where(srow == 2, num / norm, jnp.where(srow == 3, jnp.sqrt(cells / norm), 0.0))
    a_zero, scale = sums[2:3, :], sums[3:4, :]

    def slot(t):
        x = []
        squares = None
        for c in range(GROUPS):
            place, at, on = source_of(c, t, offsets, device, count, nblk)
            v = only(on, block_of(vheld, place, at, width))
            r = block_of(rheld, place, at, width).astype(F32)
            alpha = ext[pl.ds(place * EXTRA + at, 1), :]
            w = scale * (r + (alpha - a_zero) * v.astype(F32))
            if c == 0:
                squares = total_of(w * w)
            w = only(on, w).astype(BF16)
            x.append(w)
            if c in used:
                vsrc[used.index(c), t] = v
                wsrc[used.index(c), t] = w
        g = jnp.where(inside(dims[t, 0], dims[t, 1], (width, width)), ham_sum(x, t, lref, rref), 0.0)
        gref[t] = g
        num = total_of(x[0].astype(F32) * g)
        sums[...] += jnp.where(srow == 0, squares, jnp.where(srow == 1, num, 0.0))

    over_slots(count, slot, HAM_STEP, arrival(envs, count))


def ritz_kernel(count, cells, ranks, parts, vsrc, wsrc, facts, passed, coefs):
    width = vsrc.shape[2]
    both = parts[0]
    for i in range(1, parts.shape[0]):
        both = both + parts[i]
    squares, num = both[0:1, :] / cells, both[1:2, :] / cells
    a_zero, scale = parts[0, 2:3, :], parts[0, 3:4, :]
    beta = jnp.sqrt(squares + 1e-06)
    a_one = num / (beta * beta)
    half_gap = (a_zero - a_one) / 2.0
    ritz = (a_zero + a_one) / 2.0 - jnp.sqrt(half_gap * half_gap + beta * beta)
    gap_val = ritz - a_zero
    length = jnp.sqrt(beta * beta + gap_val * gap_val)
    from_v, from_w = beta / length * scale, gap_val / length / beta
    row = lax.broadcasted_iota(jnp.int32, coefs.shape, 0)
    coefs[...] = jnp.where(row == 0, from_v, jnp.where(row == 1, from_w, ritz))
    lane = lax.broadcasted_iota(jnp.int32, (width, width), 1)
    passed[pl.ds(count * width, EXTRA), :] = facts[...]

    def slot(t):
        state = from_v * vsrc[0, t].astype(F32) + from_w * wsrc[0, t].astype(F32)
        kept = jnp.where(lane < ranks[t], state, 0.0).astype(BF16)
        passed[pl.ds(pl.multiple_of(t * width, width), width), :] = kept

    over_slots(count, slot, 2)


def stacked(blocks):
    width = blocks.shape[1]
    return jnp.concatenate([blocks[width * k : width * (k + 1)] for k in range(blocks.shape[0] // width)], 1)


def pack_kernel(count, late, used, caps, src_caps, starts, coefs, vsrc, wsrc, far, out, lref, accs, sem):
    width = vsrc.shape[2]
    per = accs.shape[0]
    lane = lax.broadcasted_iota(jnp.int32, (width, width), 1)
    from_v, from_w = coefs[0:1, :], coefs[1:2, :]

    def envs(g):
        span, first, copies = pl.ds(g * per, per), 0, []
        for i, (c, low, end) in enumerate(late):
            copies.append(
                pltpu.make_async_copy(
                    far.at[pl.ds(low, end - low), c, span], lref.at[pl.ds(first, end - low), span], sem.at[i, g]
                )
            )
            first += end - low
        return copies

    for g in range(count // per):
        for copy in envs(g):
            copy.start()

    def kept_block(c, t, cap):
        i = used.index(c)
        state = from_v * vsrc[i, t].astype(F32) + from_w * wsrc[i, t].astype(F32)
        return jnp.where(lane < cap, state, 0.0)

    def slot(t, acc):
        own = kept_block(0, t, caps[t]).T.astype(BF16)
        at, first = jnp.int32(0), 0
        for c, low, end in late:
            cap = src_caps[c, t]
            left = jnp.concatenate([lref[first + k, t] for k in range(end - low)], 0)
            inner = jnp.dot(left, kept_block(c, t, cap).astype(BF16), preferred_element_type=F32).astype(BF16)
            update = jnp.dot(own, stacked(inner), preferred_element_type=F32)
            for k in range(end - low):
                tile = at // width
                lead = at - tile * width
                turned = pltpu.roll(update[:, width * k : width * (k + 1)], lead, 1)
                acc[tile] = jnp.where(lane >= lead, turned, acc[tile])
                acc[tile + 1] = turned
                at = at + cap
            first += end - low
        return (at + width - 1) // width

    def step(g, carry):
        for copy in envs(g):
            copy.wait()
        tiles = [slot(g * per + p, accs.at[p]) for p in range(per)]
        for p in range(per):
            t = g * per + p
            high = (caps[t] + 15) // 16 * 16

            def flush(tile, c, t=t, p=p, high=high):
                first = jnp.minimum(starts[t] + tile * high, out.shape[0] - width)
                out[pl.ds(pl.multiple_of(first, 16), width), :] = accs[p, tile].astype(BF16)
                return c

            lax.fori_loop(0, tiles[p], flush, 0)
        return carry

    lax.fori_loop(0, count // per, step, 0)


def made_copies(share, out, made, sem, span, at):
    copies, first = [], 0
    for i, (c, low, end) in enumerate(share):
        copies.append(
            (made.at[pl.ds(first, end - low), span], out.at[pl.ds(low, end - low), c, span], sem.at[len(share) * at + i])
        )
        first += end - low
    return copies


def own_left(share, lenv, out, made, sem, count):
    every = pl.ds(0, count)
    into = [pltpu.make_async_copy(b, a, s) for a, b, s in made_copies(share, lenv, made, sem, every, 0)]
    for copy in into:
        copy.start()
    for copy in into:
        copy.wait()
    back = [pltpu.make_async_copy(a, b, s) for a, b, s in made_copies(share, out, made, sem, every, 0)]
    for copy in back:
        copy.start()
    for copy in back:
        copy.wait()


def send_out(share, out, made, sem, per):
    def after(g):
        for a, b, s in made_copies(share, out, made, sem, pl.ds(g * per, per), g):
            pltpu.make_async_copy(a, b, s).start()

    return after


def wait_out(share, out, made, sem, count, per):
    def wait(g, carry):
        for a, b, s in made_copies(share, out, made, sem, pl.ds(g * per, per), g):
            pltpu.make_async_copy(a, b, s).wait()
        return carry

    lax.fori_loop(0, count // per, wait, 0)


def unpack_kernel(count, late, caps, src_caps, starts, first_sec, packed, lenv, so_far, out, made, sem):
    del so_far
    width = packed.shape[1]

    @pl.when(first_sec[0] == 1)
    def _():
        own_left(late, lenv, out, made, sem, count)

    @pl.when(first_sec[0] == 0)
    def _():
        lane = lax.broadcasted_iota(jnp.int32, (width, width), 1)

        def slot(t):
            high = (caps[t] + 15) // 16 * 16
            at, first = jnp.int32(0), 0
            for c, low, end in late:
                mine = src_caps[c, t]
                valid = inside(caps[t], mine, (width, width))
                for k in range(end - low):
                    tile = jnp.where(mine > 0, at // width, 0)
                    lead = at - at // width * width
                    near = packed[pl.ds(pl.multiple_of(starts[t] + tile * high, 16), width), :]
                    next_one = packed[pl.ds(pl.multiple_of(starts[t] + (tile + 1) * high, 16), width), :]
                    both = jnp.where(lane >= lead, near.astype(F32), next_one.astype(F32))
                    both = pltpu.roll(both, width - lead, 1)
                    made[first + k, t] = jnp.where(valid, both, 0.0).astype(BF16)
                    at = at + mine
                first += end - low

        per = step_of(count, UNPACK_STEP)
        over_slots(count, slot, UNPACK_STEP, None, send_out(late, out, made, sem, per))
        wait_out(late, out, made, sem, count, per)


def early_kernel(places, count, early, offsets, device, first_sec, *refs):
    pieces = refs[: len(places)]
    one, two, lenv, out, held, sent, made, sem, far_sem, out_sem = refs[len(places) :]
    width = made.shape[2]
    nblk = held.shape[0]

    @pl.when(first_sec[0] == 1)
    def _():
        own_left(early, lenv, out, made, out_sem, count)

    @pl.when(first_sec[0] == 0)
    def _():
        copies = start_pieces(places, pieces, held, sem)
        m = one.shape[0]
        copies.append(pltpu.make_async_copy(one, sent.at[pl.ds(0, m)], far_sem.at[0]))
        copies.append(pltpu.make_async_copy(two, sent.at[pl.ds(m, two.shape[0])], far_sem.at[1]))
        for copy in copies[-2:]:
            copy.start()
        for copy in copies:
            copy.wait()

        def slot(t):
            own = block_of(held, 0, t, width).astype(F32).T.astype(BF16)
            first = 0
            for c, low, end in early:
                place, at, on = source_of(c, t, offsets, device, count, nblk)
                kept = only(on, block_of(held, place, at, width))
                left = jnp.concatenate([sent[first + k, t] for k in range(end - low)], 0)
                inner = jnp.dot(left, kept, preferred_element_type=F32).astype(BF16)
                update = jnp.dot(own, stacked(inner), preferred_element_type=F32).astype(BF16)
                for k in range(end - low):
                    made[first + k, t] = update[:, width * k : width * (k + 1)]
                first += end - low

        per = step_of(count, EARLY_STEP)
        over_slots(count, slot, EARLY_STEP, None, send_out(early, out, made, out_sem, per))
        wait_out(early, out, made, out_sem, count, per)


def shards(wavefunction, left_env, right_env, row_offset, sector_dims, trunc_ranks):
    start, lenv, renv = wavefunction[0], left_env[0], right_env[0]
    offsets, dims, ranks = row_offset[0], sector_dims[0], trunc_ranks[0]
    count, width = start.shape[0], start.shape[1]
    channels = lenv.shape[0]
    kinds = channels // GROUPS
    nblk, device = lax.axis_size("blk"), lax.axis_index("blk")
    body = count * width
    cells = float(count * nblk * width * width)
    lines = jnp.arange(width, dtype=jnp.int32)
    first_sec = jnp.reshape((lax.axis_index("sec") == 0).astype(jnp.int32), (1,))
    mine = jnp.reshape(device.astype(jnp.int32), (1,))
    by_group = lenv.reshape((kinds, GROUPS, count, width, width))
    at_once, then, late = shares(kinds)
    early = at_once + then
    used = (0,) + tuple(c for c, _, _ in late)
    n_then, n_late = (sum(end - low for _, low, end in share) for share in (then, late))
    n_early = channels - n_late

    mask_on = (lines[None, :, None] < dims[:, 0][:, None, None]) & (
        lines[None, None, :] < dims[:, 1][:, None, None]
    )
    vzero = jnp.where(mask_on, start, jnp.zeros_like(start))
    caps = jnp.minimum(dims[:, 1], ranks)
    meta = jnp.zeros((EXTRA, width), BF16).at[0, :count].set(caps.astype(BF16))
    vpieces = gathered(jnp.concatenate([vzero.reshape((body, width)), meta]))
    sent_one = onward(lenv[:GROUPS])
    places = tuple((place, first) for _, place, first in vpieces)
    n = len(places)
    vrows = [in_hbm(rows) for rows, _, _ in vpieces]
    anywhere = pl.BlockSpec(memory_space=pl.ANY)
    far = pl.BlockSpec(memory_space=pltpu.HBM)
    near = pl.BlockSpec(memory_space=pltpu.VMEM)
    scalars = pl.BlockSpec(memory_space=pltpu.SMEM)
    held = pltpu.VMEM((nblk, body + EXTRA, width), BF16)
    env = pltpu.VMEM(lenv.shape, BF16)
    wide_shape = jax.ShapeDtypeStruct((count, width, width), F32)
    pay_shape = jax.ShapeDtypeStruct((body + EXTRA, width), BF16)
    row_shape = jax.ShapeDtypeStruct((8, 128), F32)
    used_shape = jax.ShapeDtypeStruct((len(used), count, width, width), BF16)
    steps = count // step_of(count, HAM_STEP)

    def dma(*shape):
        return pltpu.SemaphoreType.DMA(shape)

    def call(kernel, name, in_specs, out_specs, out_shape, scratch=(), aliases=None, moved=1):
        return pl.pallas_call(
            kernel,
            in_specs=in_specs,
            out_specs=out_specs,
            out_shape=out_shape,
            scratch_shapes=list(scratch),
            input_output_aliases=aliases or {},
            compiler_params=params(),
            cost_estimate=pl.CostEstimate(flops=1, bytes_accessed=moved, transcendentals=0),
            name=name,
        )

    hzero, rpay, sent_two = call(
        functools.partial(first_kernel, places, count, then),
        "ham_first",
        [scalars] * 3 + [anywhere] * n + [far] * 2,
        [near, near, far],
        [wide_shape, pay_shape, jax.ShapeDtypeStruct((n_then, count, width, width), BF16)],
        [held, env, env, pltpu.VMEM((EXTRA, 128), F32), dma(n), dma(steps), dma(steps), dma(n_then)],
    )(offsets, mine, dims, *vrows, in_hbm(lenv), in_hbm(renv))

    rpieces = gathered(rpay)
    gone, sums, vsrc, wsrc = call(
        functools.partial(second_kernel, places, count, cells, used),
        "ham_second",
        [scalars] * 3 + [anywhere] * (2 * n) + [far] * 2,
        [near] * 4,
        [wide_shape, row_shape, used_shape, used_shape],
        [
            held, held, env, env, pltpu.VMEM((nblk * EXTRA, 128), F32),
            dma(n), dma(n), dma(steps), dma(steps),
        ],
    )(offsets, mine, dims, *vrows, *[rows for rows, _, _ in rpieces], in_hbm(lenv), in_hbm(renv))

    offsets, caps, hzero = lax.optimization_barrier((offsets, caps, hzero))
    all_caps = extras_of(vpieces, nblk, body)[:, 0, :count].astype(jnp.int32).reshape((-1,))
    up_val = jnp.arange(count, dtype=jnp.int32)

    def layout(caps, src_caps):
        high = (caps + 15) // 16 * 16
        wide = (sum((end - low) * src_caps[c] for c, low, end in late) + width - 1) // width
        ends = jnp.cumsum(high * wide)
        return ends - high * wide, ends[-1]

    def used_by(holder):
        down_val = (holder - offsets) % nblk
        holders = [
            jnp.broadcast_to(holder, (count,)),
            (down_val + jnp.roll(offsets, 1)) % nblk,
            (down_val + jnp.roll(offsets, -1)) % nblk,
            jnp.broadcast_to((holder - 1) % nblk, (count,)),
            jnp.broadcast_to((holder + 1) % nblk, (count,)),
        ]
        slots = [up_val, jnp.maximum(up_val - 1, 0), jnp.minimum(up_val + 1, count - 1), up_val, up_val]
        there = [up_val >= 0, up_val >= 1, up_val <= count - 2, down_val >= 1, down_val <= nblk - 2]
        entries = (jnp.stack(holders) ^ device) * count + jnp.stack(slots)
        match = entries[..., None] == jnp.arange(all_caps.shape[0], dtype=jnp.int32)
        found = jnp.sum(jnp.where(match, all_caps, 0), axis=-1)
        found = jnp.where(jnp.stack(there), found, 0).astype(jnp.int32)
        return found, *layout(found[0], found)

    src_caps, starts, _ = used_by(device)
    needed = jnp.max(jax.vmap(lambda holder: used_by(holder)[2])(jnp.arange(nblk, dtype=jnp.int32)))
    length = lax.axis_size("sec")
    needed = jnp.where(lax.axis_index("sec") == length - 1, 0, needed).astype(F32)
    needed, sums = lax.optimization_barrier((needed, sums))
    needed = jnp.full((8, 128), needed)
    most_needed = needed
    for shift in range(1, length):
        turn = [(i, (i + shift) % length) for i in range(length)]
        most_needed = jnp.maximum(most_needed, lax.ppermute(needed, "sec", turn))
    sent_two = onward(sent_two)
    most_needed = most_needed[0, 0].astype(jnp.int32)

    parts = lax.all_gather(sums, "blk", axis=0)
    facts = jnp.concatenate([caps[None], src_caps, offsets[None]], axis=0).astype(BF16)
    facts = jnp.zeros((EXTRA, width), BF16).at[: facts.shape[0], :count].set(facts)

    most = count * n_late * width + SLACK
    out_shape = jax.ShapeDtypeStruct(by_group.shape, BF16)
    per = step_of(count, PACK_STEP)

    def finish(rows):
        def branch(parts, hzero, gone, vsrc, wsrc, sent_one, sent_two):
            passed, coefs = call(
                functools.partial(ritz_kernel, count, cells),
                "ritz",
                [scalars] + [near] * 4,
                [near] * 2,
                [pay_shape, row_shape],
            )(ranks, parts, vsrc, wsrc, facts)
            passed = onward(passed)
            packed = call(
                functools.partial(pack_kernel, count, late, used),
                "pack_update",
                [scalars] * 3 + [near] * 3 + [far],
                near,
                jax.ShapeDtypeStruct((rows, width), BF16),
                [
                    pltpu.VMEM((n_late, count, width, width), BF16),
                    pltpu.VMEM((per, n_late + 2, width, width), F32),
                    dma(len(late), count // per),
                ],
                moved=20 * 1024 * 1024,
            )(caps, src_caps, starts, coefs, vsrc, wsrc, in_hbm(by_group))
            packed, passed = lax.optimization_barrier((packed, passed))
            arrived = onward(packed)
            kpieces = gathered(passed)
            rows_last, coefs = lax.optimization_barrier((kpieces[-1][0], coefs))
            kpieces[-1] = (rows_last, *kpieces[-1][1:])
            from_v, from_w, ritz = coefs[0, 0], coefs[1, 0], coefs[2, 0]
            state_new = (from_v * vsrc[0].astype(F32) + from_w * wsrc[0].astype(F32)).astype(BF16)
            hstate_new = (from_v * hzero + from_w * gone).astype(BF16)
            facts_in = passed[body:, :count].astype(jnp.int32)
            prev_caps, prev_src, prev_offsets = facts_in[0], facts_in[1 : 1 + GROUPS], facts_in[1 + GROUPS]
            prev_starts, _ = layout(prev_caps, prev_src)
            so_far = call(
                functools.partial(early_kernel, places, count, early),
                "early_update",
                [scalars] * 3 + [anywhere] * n + [far] * 3,
                far,
                out_shape,
                [
                    held,
                    pltpu.VMEM((n_early, count, width, width), BF16),
                    pltpu.VMEM((n_early, count, width, width), BF16),
                    dma(n),
                    dma(2),
                    dma(len(early) * count),
                ],
            )(prev_offsets, mine, first_sec, *[r for r, _, _ in kpieces], in_hbm(sent_one), in_hbm(sent_two), in_hbm(by_group))
            next_left = call(
                functools.partial(unpack_kernel, count, late),
                "unpack_update",
                [scalars] * 4 + [near] + [far] * 2,
                far,
                out_shape,
                [pltpu.VMEM((n_late, count, width, width), BF16), dma(len(late) * count)],
                {6: 0},
            )(prev_caps, prev_src, prev_starts, first_sec, arrived, in_hbm(by_group), in_hbm(so_far))
            return state_new, hstate_new, ritz, next_left

        return branch

    sizes = [most * part // 64 // 16 * 16 for part in (20, 24, 26, 27, 28, 30, 36)] + [most]
    tier = sum((most_needed + SLACK > size).astype(jnp.int32) for size in sizes[:-1])
    state_new, hstate_new, ritz, next_left = lax.switch(
        tier, [finish(size) for size in sizes], parts, hzero, gone, vsrc, wsrc, sent_one, sent_two
    )
    next_left = next_left.reshape((channels, count, width, width))
    return (state_new[None], hstate_new[None], jnp.reshape(ritz, (1,)), next_left[None])


def solution(mesh):
    placed = (
        P("sec", "blk", None, None),
        P("sec", None, "blk", None, None),
        P("sec", None, "blk", None, None),
        P("sec", None),
        P("sec", "blk", None),
        P("sec", "blk"),
    )
    return jax.shard_map(
        shards,
        mesh=mesh,
        in_specs=placed,
        out_specs=(
            P("sec", "blk", None, None),
            P("sec", "blk", None, None),
            P("sec"),
            P("sec", None, "blk", None, None),
        ),
        check_vma=False,
    )
```

profile of v0, /device:TPU:8, one launch (start us, length us, event | category | flops | bytes accessed | tf_op | source)
XLA Modules:
  0.0 166.7 jit_solution(499090546290271265)
XLA Ops:
  0.6 0.8 slice_bitcast_fusion.25
  1.5 0.7 fusion.81
  2.3 1.3 fusion.48
  3.6 1.6 collective-permute-start.91
  5.2 1.5 collective-permute-start.89
  6.7 3.0 %slice_bitcast_fusion.16 = bf16[5,12,128,128]{3,2,1,0:T(8,128)(2,1)} fusion(bf16[1,20,12,128,128]{4,3,2,1,0:T(8,128)(2,1)} %param.19), kind=kLoop, calls=%fused_computation.352 | loop fusion | bytes 3932160 | tf_op jit(solution)/shard_map/slice | solution.py:516
  9.7 3.5 %collective-permute-start.109 = (bf16[5,12,128,128]{3,2,1,0:T(8,128)(2,1)}, bf16[5,12,128,128]{3,2,1,0:T(8,128)(2,1)}, u32[]{:S(2)}, u32[]{:S(2)}) collective-permute-start(bf16[5,12,128,128]{3,2,1,0:T(8,128)(2,1)} %slice_bitcast_fusion.16), channel_id=1, source_target_pairs={{0,8},{8,16},{16,24},{1,9},{9,17},{17,25},{2,10},{10,18},{18,26},{... | collective-permute-start | bytes 5898248 | tf_op jit(solution)/shard_map/ppermute | solution.py:39
  13.5 1.1 collective-permute-done.91.refs_4_
  14.6 1.6 collective-permute-start.94
  16.2 1.6 collective-permute-start.93
  18.3 3.6 %collective-permute-done.93.refs_6_ = bf16[768,128]{1,0:T(8,128)(2,1)S(1)} collective-permute-done((bf16[768,128]{1,0:T(8,128)(2,1)S(1)}, bf16[768,128]{1,0:T(8,128)(2,1)S(1)}, u32[]{:S(2)}, u32[]{:S(2)}) %collective-permute-start.93) | collective-permute-done | bytes 196640 | tf_op jit(solution)/shard_map/ppermute | solution.py:34
  22.5 0.9 collective-permute-done.95.refs_8_
  24.4 11.9 %ham_first.1 = (f32[12,128,128]{2,1,0:T(8,128)}, bf16[1552,128]{1,0:T(8,128)(2,1)S(1)}, bf16[4,12,128,128]{3,2,1,0:T(8,128)(2,1)S(1)}) custom-call(s32[12]{0:T(128)S(1)} %bitcast.498, s32[1]{0:T(128)} %bitcast.124.device, s32[12,2]{1,0:T(8,128)S(1)} %copy.25.dims, bf16[1552,128]{1,0:T(8,128)(2,1)} %copy-done.42, bf16[1552,128]{1,0:T(8,128)(2,1)} %copy-done.46, ...), custom_call_target="tpu_custom_call" | custom-call | flops 1 | bytes 1 | tf_op jit(solution)/shard_map/ham_first/pallas_call | solution.py:548
  36.2 1.1 copy-done.9
  38.1 1.5 collective-permute-start.100
  40.1 0.7 constant_dynamic-update-slice_fusion.10
  40.9 0.6 fusion.75
  41.6 0.7 fusion.74
  43.1 1.2 select_reduce_fusion
  44.4 3.5 %collective-permute-start.110 = (bf16[4,12,128,128]{3,2,1,0:T(8,128)(2,1)}, bf16[4,12,128,128]{3,2,1,0:T(8,128)(2,1)}, u32[]{:S(2)}, u32[]{:S(2)}) collective-permute-start(bf16[4,12,128,128]{3,2,1,0:T(8,128)(2,1)} %copy-done.9), channel_id=1, source_target_pairs={{0,8},{8,16},{16,24},{1,9},{9,17},{17,25},{2,10},{10,18},{18,26},{... | collective-permute-start | bytes 4718600 | tf_op jit(solution)/shard_map/ppermute | solution.py:39
  47.9 1.4 collective-permute-done.100.refs_14_
  49.4 1.2 collective-permute-start.103
  50.7 1.0 collective-permute-start.102
  51.6 5.1 %collective-permute-done.102.refs_16_ = bf16[768,128]{1,0:T(8,128)(2,1)S(1)} collective-permute-done((bf16[768,128]{1,0:T(8,128)(2,1)S(1)}, bf16[768,128]{1,0:T(8,128)(2,1)S(1)}, u32[]{:S(2)}, u32[]{:S(2)}) %collective-permute-start.102) | collective-permute-done | bytes 196640 | tf_op jit(solution)/shard_map/ppermute | solution.py:34
  58.9 1.3 collective-permute-done.105.refs_19_
  60.2 13.3 %ham_second.1 = (f32[12,128,128]{2,1,0:T(8,128)}, f32[8,128]{1,0:T(8,128)S(1)}, bf16[5,12,128,128]{3,2,1,0:T(8,128)(2,1)S(1)}, bf16[5,12,128,128]{3,2,1,0:T(8,128)(2,1)S(1)}) custom-call(s32[12]{0:T(128)S(1)} %bitcast.506, s32[1]{0:T(128)} %bitcast.124.device, s32[12,2]{1,0:T(8,128)S(1)} %copy.25.dims, bf16[1552,128]{1,0:T(8,128)(2,1)} %copy-done.42, ...), custom_call_target="tpu_custom_call" | custom-call | flops 1 | bytes 1 | tf_op jit(solution)/shard_map/ham_second/pallas_call | solution.py:558
  73.5 1.6 collective-permute-start.106
  75.1 2.0 %collective-permute-start.107 = (f32[8,128]{1,0:T(8,128)S(1)}, f32[8,128]{1,0:T(8,128)S(1)}, u32[]{:S(2)}, u32[]{:S(2)}) collective-permute-start(f32[8,128]{1,0:T(8,128)S(1)} %broadcast_in_dim.111), channel_id=1, source_target_pairs={{0,16},{8,24},{16,0},{24,8},{1,17},{9,25},{17,1},{25,9},{2,18},{10... | collective-permute-start | bytes 12296 | tf_op jit(solution)/shard_map/ppermute | solution.py:606
  77.2 1.0 collective-permute-start.108
  78.2 8.4 %all-gather = f32[64,128]{1,0:T(8,128)S(1)} all-gather(f32[8,128]{1,0:T(8,128)S(1)} %get-tuple-element.1180), channel_id=2, replica_groups=mesh['sec'=4,'blk'=8] {'blk'}, dimensions={0}, use_global_device_ids=true | all-gather | bytes 36864 | tf_op jit(solution)/shard_map/all_gather | solution.py:610
  86.6 4.4 %collective-permute-done.106 = f32[8,128]{1,0:T(8,128)S(1)} collective-permute-done((f32[8,128]{1,0:T(8,128)S(1)}, f32[8,128]{1,0:T(8,128)S(1)}, u32[]{:S(2)}, u32[]{:S(2)}) %collective-permute-start.106) | collective-permute-done | bytes 4128 | tf_op jit(solution)/shard_map/ppermute | solution.py:606
  92.3 73.3 %conditional.3 = (bf16[1,12,128,128]{3,2,1,0:T(8,128)(2,1)}, f32[1]{0:T(128)}, bf16[1,20,12,128,128]{4,3,2,1,0:T(8,128)(2,1)}, bf16[1,12,128,128]{3,2,1,0:T(8,128)(2,1)}) conditional(s32[]{:T(128)} %bitcast.143, (s32[12,1]{0,1:T(1,128)S(1)}, s32[12]{0:T(128)S(1)}, s32[12]{0:T(128)S(1)}, pred[12]{0:T(512)(128)(4,1)S(1)}, ...), branch_computations={%region_5.7_spmd, %region_7.9_spmd, %region_9.11_spmd, %region_11.... | conditional | flops 1967680 | bytes 77086360
  99.0 0.8 ritz.11
  99.8 3.6 %collective-permute-start.33 = (bf16[1552,128]{1,0:T(8,128)(2,1)S(1)}, bf16[1552,128]{1,0:T(8,128)(2,1)S(1)}, u32[]{:S(2)}, u32[]{:S(2)}) collective-permute-start(bf16[1552,128]{1,0:T(8,128)(2,1)S(1)} %get-tuple-element.1015), channel_id=1, source_target_pairs={{0,8},{8,16},{16,24},{1,9},{9,17},{17,25},{2,10},{10,18},{18,26},{... | collective-permute-start | bytes 1191944 | tf_op jit(solution)/shard_map/cond/branch_3_fun/ppermute | solution.py:39
  103.4 0.8 bitcast_subtract_fusion.7.starts
  104.2 9.7 %pack_update.11 = bf16[7168,128]{1,0:T(8,128)(2,1)} custom-call(s32[12]{0:T(128)S(1)} %copy-done.71, s32[5,12]{1,0:T(8,128)} %copy-done.54, s32[12]{0:T(128)S(1)} %bitcast_subtract_fusion.7.starts, f32[8,128]{1,0:T(8,128)S(1)} %get-tuple-element.1017.coefs, bf16[5,12,128,128]{3,2,1,0:T(8,128)(2,1)} %copy-done.13, ...), custom_call_target="tpu_custom_call" | custom-call | flops 1 | bytes 20971520 | tf_op jit(solution)/shard_map/cond/branch_3_fun/pack_update/pallas_call | solution.py:628
  114.0 3.4 %collective-permute-start.37 = (bf16[7168,128]{1,0:T(8,128)(2,1)}, bf16[7168,128]{1,0:T(8,128)(2,1)S(1)}, u32[]{:S(2)}, u32[]{:S(2)}) collective-permute-start(bf16[7168,128]{1,0:T(8,128)(2,1)} %pack_update.11), channel_id=1, source_target_pairs={{0,8},{8,16},{16,24},{1,9},{9,17},{17,25},{2,10},{10,18},{18,26},{... | collective-permute-start | bytes 5505032 | tf_op jit(solution)/shard_map/cond/branch_3_fun/ppermute | solution.py:39
  118.5 9.3 %collective-permute-done.34.refs_4_ = bf16[1552,128]{1,0:T(8,128)(2,1)S(1)} collective-permute-done((bf16[1552,128]{1,0:T(8,128)(2,1)S(1)}, bf16[1552,128]{1,0:T(8,128)(2,1)S(1)}, u32[]{:S(2)}, u32[]{:S(2)}) %collective-permute-start.34) | collective-permute-done | bytes 397344 | tf_op jit(solution)/shard_map/cond/branch_3_fun/ppermute | solution.py:34
  127.8 0.7 slice.598
  129.0 0.7 slice.606
  130.5 5.2 %collective-permute-done.42.refs_6_ = bf16[768,128]{1,0:T(8,128)(2,1)} collective-permute-done((bf16[768,128]{1,0:T(8,128)(2,1)}, bf16[768,128]{1,0:T(8,128)(2,1)}, u32[]{:S(2)}, u32[]{:S(2)}) %collective-permute-start.42) | collective-permute-done | bytes 196640 | tf_op jit(solution)/shard_map/cond/branch_3_fun/ppermute | solution.py:34
  136.2 1.5 collective-permute-done.36.refs_9_
  138.0 1.4 collective-permute-done.43.refs_8_
  139.4 11.2 %early_update.11.so_far = bf16[4,5,12,128,128]{4,3,2,1,0:T(8,128)(2,1)} custom-call(s32[12]{0:T(128)S(1)} %get-tuple-element.1324.offsets, s32[1]{0:T(128)} %get-tuple-element.1022.device, s32[1]{0:T(128)} %bitcast.57.first_sec, bf16[1552,128]{1,0:T(8,128)(2,1)S(1)} %collective-permute-done.33.refs_0_, ...), custom_call_target="tpu_custom_call" | custom-call | flops 1 | bytes 1 | tf_op jit(solution)/shard_map/cond/branch_3_fun/early_update/pallas_call | solution.py:652
  151.2 3.1 %add_convert_fusion.6 = bf16[1,12,128,128]{3,2,1,0:T(8,128)(2,1)} fusion(bf16[5,12,128,128]{3,2,1,0:T(8,128)(2,1)} %copy-done.21, f32[]{:T(128)} %bitcast.49, bf16[5,12,128,128]{3,2,1,0:T(8,128)(2,1)} %copy-done.13, f32[]{:T(128)} %bitcast.48), kind=kLoop, calls=%fused_computation.132 | loop fusion | flops 1179648 | bytes 1179656 | tf_op jit(solution)/shard_map/cond/branch_0_fun/convert_element_type | solution.py:647
  154.3 2.0 %fusion.18 = bf16[1,12,128,128]{3,2,1,0:T(8,128)(2,1)} fusion(f32[12,128,128]{2,1,0:T(8,128)S(1)} %copy-done.37, f32[12,128,128]{2,1,0:T(8,128)S(1)} %copy-done.29, f32[]{:T(128)} %bitcast.49, f32[]{:T(128)} %bitcast.48), kind=kLoop, calls=%fused_computation.134 | loop fusion | flops 786432 | bytes 1966088 | tf_op jit(solution)/shard_map/broadcast_in_dim | solution.py:686
  156.2 1.2 collective-permute-done.37.packed
  157.4 4.1 %unpack_update.11 = bf16[4,5,12,128,128]{4,3,2,1,0:T(8,128)(2,1)} custom-call(s32[12]{0:T(128)S(1)} %get-tuple-element.1325.caps, s32[5,12]{1,0:T(8,128)S(1)} %slice.600.src_caps, s32[12]{0:T(128)S(1)} %bitcast_subtract_fusion.6.starts, s32[1]{0:T(128)} %bitcast.57.first_sec, ...), custom_call_target="tpu_custom_call", output_to_operand_aliasing={{}: (6, {})} | custom-call | flops 1 | bytes 1 | tf_op jit(solution)/shard_map/cond/branch_3_fun/unpack_update/pallas_call | solution.py:667
  (165 shorter events, 10.9 us)
Async XLA Ops:
  3.6 6.2 %copy-start.42 = (bf16[1552,128]{1,0:T(8,128)(2,1)}, bf16[1552,128]{1,0:T(8,128)(2,1)S(1)}, u32[]{:S(2)}) copy-start(bf16[1552,128]{1,0:T(8,128)(2,1)S(1)} %pad_maximum_fusion.refs_0_) | copy-start | bytes 1191940
  3.6 9.7 %copy-start.77 = (s32[1,12,2]{1,2,0:T(2,128)S(1)}, s32[1,12,2]{1,2,0:T(2,128)}, u32[]{:S(2)}) copy-start(s32[1,12,2]{1,2,0:T(2,128)} %param.22) | copy-start | bytes 292
  3.6 9.9 %copy-start.72 = (s32[1,12]{1,0:T(1,128)S(1)}, s32[1,12]{1,0:T(1,128)}, u32[]{:S(2)}) copy-start(s32[1,12]{1,0:T(1,128)} %param.23) | copy-start | bytes 148
  3.6 20.8 %copy-start.8 = (s32[1,12]{1,0:T(1,128)S(1)}, s32[1,12]{1,0:T(1,128)}, u32[]{:S(2)}) copy-start(s32[1,12]{1,0:T(1,128)} %param.21) | copy-start | bytes 148
  3.6 11.0 %collective-permute-start.91 = (bf16[1552,128]{1,0:T(8,128)(2,1)S(1)}, bf16[1552,128]{1,0:T(8,128)(2,1)S(1)}, u32[]{:S(2)}, u32[]{:S(2)}) collective-permute-start(bf16[1552,128]{1,0:T(8,128)(2,1)S(1)} %pad_maximum_fusion.refs_0_), channel_id=1, source_target_pairs={{0,4},{1,5},{2,6},{3,7},{4,0},{5,1},{6,2},{7,3},{8,12},{9,13},{10,... | collective-permute-start | bytes 1191944 | tf_op jit(solution)/shard_map/ppermute | solution.py:34
  5.2 11.0 %collective-permute-start.89 = (bf16[1552,128]{1,0:T(8,128)(2,1)S(1)}, bf16[1552,128]{1,0:T(8,128)(2,1)S(1)}, u32[]{:S(2)}, u32[]{:S(2)}) collective-permute-start(bf16[1552,128]{1,0:T(8,128)(2,1)S(1)} %pad_maximum_fusion.refs_0_), channel_id=1, source_target_pairs={{0,2},{1,3},{2,0},{3,1},{4,6},{5,7},{6,4},{7,5},{8,10},{9,11},{10,... | collective-permute-start | bytes 1191944 | tf_op jit(solution)/shard_map/ppermute | solution.py:34
  6.7 11.1 %collective-permute-start.88 = (bf16[1552,128]{1,0:T(8,128)(2,1)S(1)}, bf16[1552,128]{1,0:T(8,128)(2,1)S(1)}, u32[]{:S(2)}, u32[]{:S(2)}) collective-permute-start(bf16[1552,128]{1,0:T(8,128)(2,1)S(1)} %pad_maximum_fusion.refs_0_), channel_id=1, source_target_pairs={{0,1},{1,0},{2,3},{3,2},{4,5},{5,4},{6,7},{7,6},{8,9},{9,8},{10,11... | collective-permute-start | bytes 1191944 | tf_op jit(solution)/shard_map/ppermute | solution.py:34
  9.7 82.5 %collective-permute-start.109 = (bf16[5,12,128,128]{3,2,1,0:T(8,128)(2,1)}, bf16[5,12,128,128]{3,2,1,0:T(8,128)(2,1)}, u32[]{:S(2)}, u32[]{:S(2)}) collective-permute-start(bf16[5,12,128,128]{3,2,1,0:T(8,128)(2,1)} %slice_bitcast_fusion.16), channel_id=1, source_target_pairs={{0,8},{8,16},{16,24},{1,9},{9,17},{17,25},{2,10},{10,18},{18,26},{... | collective-permute-start | bytes 5898248 | tf_op jit(solution)/shard_map/ppermute | solution.py:39
  14.6 9.1 %copy-start.44 = (bf16[1552,128]{1,0:T(8,128)(2,1)}, bf16[1552,128]{1,0:T(8,128)(2,1)S(1)}, u32[]{:S(2)}) copy-start(bf16[1552,128]{1,0:T(8,128)(2,1)S(1)} %collective-permute-done.91.refs_4_) | copy-start | bytes 1191940
  14.6 7.3 %collective-permute-start.94 = (bf16[784,128]{1,0:T(8,128)(2,1)S(1)}, bf16[784,128]{1,0:T(8,128)(2,1)S(1)}, u32[]{:S(2)}, u32[]{:S(2)}) collective-permute-start(bf16[784,128]{1,0:T(8,128)(2,1)S(1)} %slice.644), channel_id=1, source_target_pairs={{0,2},{1,3},{2,0},{3,1},{4,6},{5,7},{6,4},{7,5},{8,10},{9,11},{10,... | collective-permute-start | bytes 602120 | tf_op jit(solution)/shard_map/ppermute | solution.py:34
  16.2 7.5 %copy-start.45 = (bf16[1552,128]{1,0:T(8,128)(2,1)}, bf16[1552,128]{1,0:T(8,128)(2,1)S(1)}, u32[]{:S(2)}) copy-start(bf16[1552,128]{1,0:T(8,128)(2,1)S(1)} %collective-permute-done.89.refs_2_) | copy-start | bytes 1191940
  16.2 5.7 %collective-permute-start.93 = (bf16[768,128]{1,0:T(8,128)(2,1)S(1)}, bf16[768,128]{1,0:T(8,128)(2,1)S(1)}, u32[]{:S(2)}, u32[]{:S(2)}) collective-permute-start(bf16[768,128]{1,0:T(8,128)(2,1)S(1)} %slice.643), channel_id=1, source_target_pairs={{0,4},{1,5},{2,6},{3,7},{4,0},{5,1},{6,2},{7,3},{8,12},{9,13},{10,... | collective-permute-start | bytes 589832 | tf_op jit(solution)/shard_map/ppermute | solution.py:34
  17.8 4.7 %collective-permute-start.90 = (bf16[1552,128]{1,0:T(8,128)(2,1)S(1)}, bf16[1552,128]{1,0:T(8,128)(2,1)S(1)}, u32[]{:S(2)}, u32[]{:S(2)}) collective-permute-start(bf16[1552,128]{1,0:T(8,128)(2,1)S(1)} %collective-permute-done.89.refs_2_), channel_id=1, source_target_pairs={{0,1},{1,0},{2,3},{3,2},{4,5},{5,4},{6,7},{7,6},{8,9},{9,8},{10,11... | collective-permute-start | bytes 1191944 | tf_op jit(solution)/shard_map/ppermute | solution.py:34
  17.8 5.9 %copy-start.46 = (bf16[1552,128]{1,0:T(8,128)(2,1)}, bf16[1552,128]{1,0:T(8,128)(2,1)S(1)}, u32[]{:S(2)}) copy-start(bf16[1552,128]{1,0:T(8,128)(2,1)S(1)} %collective-permute-done.88.refs_1_) | copy-start | bytes 1191940
  17.8 4.7 %collective-permute-start.92 = (bf16[1552,128]{1,0:T(8,128)(2,1)S(1)}, bf16[1552,128]{1,0:T(8,128)(2,1)S(1)}, u32[]{:S(2)}, u32[]{:S(2)}) collective-permute-start(bf16[1552,128]{1,0:T(8,128)(2,1)S(1)} %collective-permute-done.91.refs_4_), channel_id=1, source_target_pairs={{0,1},{1,0},{2,3},{3,2},{4,5},{5,4},{6,7},{7,6},{8,9},{9,8},{10,11... | collective-permute-start | bytes 1191944 | tf_op jit(solution)/shard_map/ppermute | solution.py:34
  22.0 1.7 %copy-start.51 = (bf16[768,128]{1,0:T(8,128)(2,1)}, bf16[768,128]{1,0:T(8,128)(2,1)S(1)}, u32[]{:S(2)}) copy-start(bf16[768,128]{1,0:T(8,128)(2,1)S(1)} %collective-permute-done.93.refs_6_) | copy-start | bytes 589828
  22.0 1.4 collective-permute-start.95
  22.0 1.7 %copy-start.49 = (bf16[784,128]{1,0:T(8,128)(2,1)}, bf16[784,128]{1,0:T(8,128)(2,1)S(1)}, u32[]{:S(2)}) copy-start(bf16[784,128]{1,0:T(8,128)(2,1)S(1)} %collective-permute-done.94.refs_7_) | copy-start | bytes 602116
  22.0 1.7 %collective-permute-start.96 = (bf16[784,128]{1,0:T(8,128)(2,1)S(1)}, bf16[784,128]{1,0:T(8,128)(2,1)S(1)}, u32[]{:S(2)}, u32[]{:S(2)}) collective-permute-start(bf16[784,128]{1,0:T(8,128)(2,1)S(1)} %collective-permute-done.94.refs_7_), channel_id=1, source_target_pairs={{0,1},{1,0},{2,3},{3,2},{4,5},{5,4},{6,7},{7,6},{8,9},{9,8},{10,11... | collective-permute-start | bytes 602120 | tf_op jit(solution)/shard_map/ppermute | solution.py:34
  38.1 11.3 %collective-permute-start.100 = (bf16[1552,128]{1,0:T(8,128)(2,1)S(1)}, bf16[1552,128]{1,0:T(8,128)(2,1)S(1)}, u32[]{:S(2)}, u32[]{:S(2)}) collective-permute-start(bf16[1552,128]{1,0:T(8,128)(2,1)S(1)} %get-tuple-element.1176.refs_10_), channel_id=1, source_target_pairs={{0,4},{1,5},{2,6},{3,7},{4,0},{5,1},{6,2},{7,3},{8,12},{9,13},{10,... | collective-permute-start | bytes 1191944 | tf_op jit(solution)/shard_map/ppermute | solution.py:34
  39.6 11.1 %collective-permute-start.98 = (bf16[1552,128]{1,0:T(8,128)(2,1)S(1)}, bf16[1552,128]{1,0:T(8,128)(2,1)S(1)}, u32[]{:S(2)}, u32[]{:S(2)}) collective-permute-start(bf16[1552,128]{1,0:T(8,128)(2,1)S(1)} %get-tuple-element.1176.refs_10_), channel_id=1, source_target_pairs={{0,2},{1,3},{2,0},{3,1},{4,6},{5,7},{6,4},{7,5},{8,10},{9,11},{10,... | collective-permute-start | bytes 1191944 | tf_op jit(solution)/shard_map/ppermute | solution.py:34
  40.1 11.5 %collective-permute-start.97 = (bf16[1552,128]{1,0:T(8,128)(2,1)S(1)}, bf16[1552,128]{1,0:T(8,128)(2,1)S(1)}, u32[]{:S(2)}, u32[]{:S(2)}) collective-permute-start(bf16[1552,128]{1,0:T(8,128)(2,1)S(1)} %get-tuple-element.1176.refs_10_), channel_id=1, source_target_pairs={{0,1},{1,0},{2,3},{3,2},{4,5},{5,4},{6,7},{7,6},{8,9},{9,8},{10,11... | collective-permute-start | bytes 1191944 | tf_op jit(solution)/shard_map/ppermute | solution.py:34
  44.4 47.8 %collective-permute-start.110 = (bf16[4,12,128,128]{3,2,1,0:T(8,128)(2,1)}, bf16[4,12,128,128]{3,2,1,0:T(8,128)(2,1)}, u32[]{:S(2)}, u32[]{:S(2)}) collective-permute-start(bf16[4,12,128,128]{3,2,1,0:T(8,128)(2,1)} %copy-done.9), channel_id=1, source_target_pairs={{0,8},{8,16},{16,24},{1,9},{9,17},{17,25},{2,10},{10,18},{18,26},{... | collective-permute-start | bytes 4718600 | tf_op jit(solution)/shard_map/ppermute | solution.py:39
  49.4 7.4 %collective-permute-start.103 = (bf16[784,128]{1,0:T(8,128)(2,1)S(1)}, bf16[784,128]{1,0:T(8,128)(2,1)S(1)}, u32[]{:S(2)}, u32[]{:S(2)}) collective-permute-start(bf16[784,128]{1,0:T(8,128)(2,1)S(1)} %slice.659), channel_id=1, source_target_pairs={{0,2},{1,3},{2,0},{3,1},{4,6},{5,7},{6,4},{7,5},{8,10},{9,11},{10,... | collective-permute-start | bytes 602120 | tf_op jit(solution)/shard_map/ppermute | solution.py:34
  50.7 6.1 %collective-permute-start.102 = (bf16[768,128]{1,0:T(8,128)(2,1)S(1)}, bf16[768,128]{1,0:T(8,128)(2,1)S(1)}, u32[]{:S(2)}, u32[]{:S(2)}) collective-permute-start(bf16[768,128]{1,0:T(8,128)(2,1)S(1)} %slice.658), channel_id=1, source_target_pairs={{0,4},{1,5},{2,6},{3,7},{4,0},{5,1},{6,2},{7,3},{8,12},{9,13},{10,... | collective-permute-start | bytes 589832 | tf_op jit(solution)/shard_map/ppermute | solution.py:34
  51.6 7.3 %collective-permute-start.101 = (bf16[1552,128]{1,0:T(8,128)(2,1)S(1)}, bf16[1552,128]{1,0:T(8,128)(2,1)S(1)}, u32[]{:S(2)}, u32[]{:S(2)}) collective-permute-start(bf16[1552,128]{1,0:T(8,128)(2,1)S(1)} %collective-permute-done.100.refs_14_), channel_id=1, source_target_pairs={{0,1},{1,0},{2,3},{3,2},{4,5},{5,4},{6,7},{7,6},{8,9},{9,8},{10,11... | collective-permute-start | bytes 1191944 | tf_op jit(solution)/shard_map/ppermute | solution.py:34
  56.8 2.2 %collective-permute-start.99 = (bf16[1552,128]{1,0:T(8,128)(2,1)S(1)}, bf16[1552,128]{1,0:T(8,128)(2,1)S(1)}, u32[]{:S(2)}, u32[]{:S(2)}) collective-permute-start(bf16[1552,128]{1,0:T(8,128)(2,1)S(1)} %collective-permute-done.98.refs_12_), channel_id=1, source_target_pairs={{0,1},{1,0},{2,3},{3,2},{4,5},{5,4},{6,7},{7,6},{8,9},{9,8},{10,11... | collective-permute-start | bytes 1191944 | tf_op jit(solution)/shard_map/ppermute | solution.py:34
  56.8 2.0 %collective-permute-start.104 = (bf16[768,128]{1,0:T(8,128)(2,1)S(1)}, bf16[768,128]{1,0:T(8,128)(2,1)S(1)}, u32[]{:S(2)}, u32[]{:S(2)}) collective-permute-start(bf16[768,128]{1,0:T(8,128)(2,1)S(1)} %collective-permute-done.102.refs_16_), channel_id=1, source_target_pairs={{0,1},{1,0},{2,3},{3,2},{4,5},{5,4},{6,7},{7,6},{8,9},{9,8},{10,11... | collective-permute-start | bytes 589832 | tf_op jit(solution)/shard_map/ppermute | solution.py:34
  58.8 1.5 collective-permute-start.105
  73.5 17.5 %collective-permute-start.106 = (f32[8,128]{1,0:T(8,128)S(1)}, f32[8,128]{1,0:T(8,128)S(1)}, u32[]{:S(2)}, u32[]{:S(2)}) collective-permute-start(f32[8,128]{1,0:T(8,128)S(1)} %broadcast_in_dim.111), channel_id=1, source_target_pairs={{0,8},{8,16},{16,24},{24,0},{1,9},{9,17},{17,25},{25,1},{2,10},{10... | collective-permute-start | bytes 12296 | tf_op jit(solution)/shard_map/ppermute | solution.py:606
  75.1 15.9 %collective-permute-start.107 = (f32[8,128]{1,0:T(8,128)S(1)}, f32[8,128]{1,0:T(8,128)S(1)}, u32[]{:S(2)}, u32[]{:S(2)}) collective-permute-start(f32[8,128]{1,0:T(8,128)S(1)} %broadcast_in_dim.111), channel_id=1, source_target_pairs={{0,16},{8,24},{16,0},{24,8},{1,17},{9,25},{17,1},{25,9},{2,18},{10... | collective-permute-start | bytes 12296 | tf_op jit(solution)/shard_map/ppermute | solution.py:606
  77.2 13.9 %collective-permute-start.108 = (f32[8,128]{1,0:T(8,128)S(1)}, f32[8,128]{1,0:T(8,128)S(1)}, u32[]{:S(2)}, u32[]{:S(2)}) collective-permute-start(f32[8,128]{1,0:T(8,128)S(1)} %broadcast_in_dim.111), channel_id=1, source_target_pairs={{0,24},{8,0},{16,8},{24,16},{1,25},{9,1},{17,9},{25,17},{2,26},{10... | collective-permute-start | bytes 12296 | tf_op jit(solution)/shard_map/ppermute | solution.py:606
  98.5 1.3 copy-start.13
  98.5 5.7 %copy-start.21 = (bf16[5,12,128,128]{3,2,1,0:T(8,128)(2,1)}, bf16[5,12,128,128]{3,2,1,0:T(8,128)(2,1)S(1)}, u32[]{:S(2)}) copy-start(bf16[5,12,128,128]{3,2,1,0:T(8,128)(2,1)S(1)} %get-tuple-element.1011.wsrc) | copy-start | bytes 5898244
  99.0 5.3 %copy-start.71 = (s32[12]{0:T(128)S(1)}, s32[12]{0:T(128)}, u32[]{:S(2)}) copy-start(s32[12]{0:T(128)} %copy-done.70) | copy-start | bytes 148
  99.8 14.2 %collective-permute-start.33 = (bf16[1552,128]{1,0:T(8,128)(2,1)S(1)}, bf16[1552,128]{1,0:T(8,128)(2,1)S(1)}, u32[]{:S(2)}, u32[]{:S(2)}) collective-permute-start(bf16[1552,128]{1,0:T(8,128)(2,1)S(1)} %get-tuple-element.1015), channel_id=1, source_target_pairs={{0,8},{8,16},{16,24},{1,9},{9,17},{17,25},{2,10},{10,18},{18,26},{... | collective-permute-start | bytes 1191944 | tf_op jit(solution)/shard_map/cond/branch_3_fun/ppermute | solution.py:39
  114.0 43.4 %collective-permute-start.37 = (bf16[7168,128]{1,0:T(8,128)(2,1)}, bf16[7168,128]{1,0:T(8,128)(2,1)S(1)}, u32[]{:S(2)}, u32[]{:S(2)}) collective-permute-start(bf16[7168,128]{1,0:T(8,128)(2,1)} %pack_update.11), channel_id=1, source_target_pairs={{0,8},{8,16},{16,24},{1,9},{9,17},{17,25},{2,10},{10,18},{18,26},{... | collective-permute-start | bytes 5505032 | tf_op jit(solution)/shard_map/cond/branch_3_fun/ppermute | solution.py:39
  117.4 10.4 %collective-permute-start.34 = (bf16[1552,128]{1,0:T(8,128)(2,1)S(1)}, bf16[1552,128]{1,0:T(8,128)(2,1)S(1)}, u32[]{:S(2)}, u32[]{:S(2)}) collective-permute-start(bf16[1552,128]{1,0:T(8,128)(2,1)S(1)} %collective-permute-done.33.refs_0_), channel_id=1, source_target_pairs={{0,4},{1,5},{2,6},{3,7},{4,0},{5,1},{6,2},{7,3},{8,12},{9,13},{10,... | collective-permute-start | bytes 1191944 | tf_op jit(solution)/shard_map/cond/branch_3_fun/ppermute | solution.py:34
  118.0 11.0 %collective-permute-start.39 = (bf16[1552,128]{1,0:T(8,128)(2,1)S(1)}, bf16[1552,128]{1,0:T(8,128)(2,1)S(1)}, u32[]{:S(2)}, u32[]{:S(2)}) collective-permute-start(bf16[1552,128]{1,0:T(8,128)(2,1)S(1)} %collective-permute-done.33.refs_0_), channel_id=1, source_target_pairs={{0,2},{1,3},{2,0},{3,1},{4,6},{5,7},{6,4},{7,5},{8,10},{9,11},{10,... | collective-permute-start | bytes 1191944 | tf_op jit(solution)/shard_map/cond/branch_3_fun/ppermute | solution.py:34
  118.5 19.4 %collective-permute-start.38 = (bf16[1552,128]{1,0:T(8,128)(2,1)S(1)}, bf16[1552,128]{1,0:T(8,128)(2,1)S(1)}, u32[]{:S(2)}, u32[]{:S(2)}) collective-permute-start(bf16[1552,128]{1,0:T(8,128)(2,1)S(1)} %collective-permute-done.33.refs_0_), channel_id=1, source_target_pairs={{0,1},{1,0},{2,3},{3,2},{4,5},{5,4},{6,7},{7,6},{8,9},{9,8},{10,11... | collective-permute-start | bytes 1191944 | tf_op jit(solution)/shard_map/cond/branch_3_fun/ppermute | solution.py:34
  128.5 7.2 %collective-permute-start.35 = (bf16[784,128]{1,0:T(8,128)(2,1)}, bf16[784,128]{1,0:T(8,128)(2,1)}, u32[]{:S(2)}, u32[]{:S(2)}) collective-permute-start(bf16[784,128]{1,0:T(8,128)(2,1)} %slice.598), channel_id=1, source_target_pairs={{0,2},{1,3},{2,0},{3,1},{4,6},{5,7},{6,4},{7,5},{8,10},{9,11},{10,... | collective-permute-start | bytes 602120 | tf_op jit(solution)/shard_map/cond/branch_3_fun/ppermute | solution.py:34
  129.7 6.0 %collective-permute-start.42 = (bf16[768,128]{1,0:T(8,128)(2,1)}, bf16[768,128]{1,0:T(8,128)(2,1)}, u32[]{:S(2)}, u32[]{:S(2)}) collective-permute-start(bf16[768,128]{1,0:T(8,128)(2,1)} %slice.606), channel_id=1, source_target_pairs={{0,4},{1,5},{2,6},{3,7},{4,0},{5,1},{6,2},{7,3},{8,12},{9,13},{10,... | collective-permute-start | bytes 589832 | tf_op jit(solution)/shard_map/cond/branch_3_fun/ppermute | solution.py:34
  130.5 8.9 %collective-permute-start.40 = (bf16[1552,128]{1,0:T(8,128)(2,1)S(1)}, bf16[1552,128]{1,0:T(8,128)(2,1)S(1)}, u32[]{:S(2)}, u32[]{:S(2)}) collective-permute-start(bf16[1552,128]{1,0:T(8,128)(2,1)S(1)} %collective-permute-done.39.refs_2_), channel_id=1, source_target_pairs={{0,1},{1,0},{2,3},{3,2},{4,5},{5,4},{6,7},{7,6},{8,9},{9,8},{10,11... | collective-permute-start | bytes 1191944 | tf_op jit(solution)/shard_map/cond/branch_3_fun/ppermute | solution.py:34
  135.7 3.7 %collective-permute-start.41 = (bf16[1552,128]{1,0:T(8,128)(2,1)S(1)}, bf16[1552,128]{1,0:T(8,128)(2,1)S(1)}, u32[]{:S(2)}, u32[]{:S(2)}) collective-permute-start(bf16[1552,128]{1,0:T(8,128)(2,1)S(1)} %collective-permute-done.34.refs_4_), channel_id=1, source_target_pairs={{0,1},{1,0},{2,3},{3,2},{4,5},{5,4},{6,7},{7,6},{8,9},{9,8},{10,11... | collective-permute-start | bytes 1191944 | tf_op jit(solution)/shard_map/cond/branch_3_fun/ppermute | solution.py:34
  135.7 2.0 %collective-permute-start.36 = (bf16[784,128]{1,0:T(8,128)(2,1)}, bf16[784,128]{1,0:T(8,128)(2,1)S(1)}, u32[]{:S(2)}, u32[]{:S(2)}) collective-permute-start(bf16[784,128]{1,0:T(8,128)(2,1)} %collective-permute-done.35.refs_7_), channel_id=1, source_target_pairs={{0,1},{1,0},{2,3},{3,2},{4,5},{5,4},{6,7},{7,6},{8,9},{9,8},{10,11... | collective-permute-start | bytes 602120 | tf_op jit(solution)/shard_map/cond/branch_3_fun/ppermute | solution.py:34
  137.7 1.7 collective-permute-start.43
  139.4 14.9 %copy-start.29 = (f32[12,128,128]{2,1,0:T(8,128)S(1)}, f32[12,128,128]{2,1,0:T(8,128)}, u32[]{:S(2)}) copy-start(f32[12,128,128]{2,1,0:T(8,128)} %get-tuple-element.1018) | copy-start | bytes 2359300
  139.4 14.9 %copy-start.37 = (f32[12,128,128]{2,1,0:T(8,128)S(1)}, f32[12,128,128]{2,1,0:T(8,128)}, u32[]{:S(2)}) copy-start(f32[12,128,128]{2,1,0:T(8,128)} %get-tuple-element.1019) | copy-start | bytes 2359300
  (11 other events, 12.0 us)
where the time goes:
time: 168 us; the launch traced here: 167 us
  Pallas kernels  50.9 us (30%)
  waiting for transfers between devices  36.9 us (22%)
  starting transfers between devices  33.6 us (20%)
  other arithmetic  12.4 us (7%)
  local copies, waits for them, and re-layouts  10.4 us (6%)
  loops' own time  10.4 us (6%)
  blocking collectives  8.45 us (5%)
  between operations  3.55 us (2%)
    ppermute x27, waiting for transfers between devices, exchange(): return lax.ppermute(value, 'blk', [(i, i ^ bit) for i in range(length)])  31.3 us
    ppermute x27, starting transfers between devices, exchange(): return lax.ppermute(value, 'blk', [(i, i ^ bit) for i in range(length)])  15 us
    ppermute x4, starting transfers between devices, onward(): return lax.ppermute(value, 'sec', [(i, i + 1) for i in range(length - 1)])  14 us
    pallas_call x1, Pallas kernels, shards(): call(functools.partial(second_kernel, places, count, cells, used), 'ham_s...  13.3 us
    pallas_call x1, Pallas kernels, shards(): call(functools.partial(first_kernel, places, count, then), 'ham_first', [...  11.9 us
    pallas_call x1, Pallas kernels, branch(): call(functools.partial(early_kernel, places, count, early), 'early_update...  11.2 us
    unnamed x1, loops' own time  10.4 us
    pallas_call x1, Pallas kernels, branch(): call(functools.partial(pack_kernel, count, late, used), 'pack_update', [s...  9.73 us
  transfers between devices with their start and end apart: 34, of which 14 were waited for; matrix products, arithmetic and copies ran while one was open for 11% of the time, Pallas kernels for 28%

commit v1 on v0

--- a/solution.py
+++ b/solution.py
@@ -25,8 +25,8 @@
 
 def shares(kinds):
     first = tuple((c, 0, 1) for c in range(GROUPS))
-    then = ((0, 1, kinds), (1, 1, 2))
-    return first, then, ((1, 2, kinds), (2, 1, kinds), (3, 1, kinds), (4, 1, kinds))
+    then = ((0, 1, kinds),)
+    return first, then, ((1, 1, kinds), (2, 1, kinds), (3, 1, kinds), (4, 1, kinds))
 
 
 def exchange(value, bit):
@@ -64,14 +64,6 @@
     return [(held[place], place, 0) for place in range(nblk)]
 
 
-def extras_of(pieces, nblk, body):
-    found = [None] * nblk
-    for rows, place, first in pieces:
-        if first + rows.shape[0] == body + EXTRA:
-            found[place] = rows[rows.shape[0] - EXTRA :]
-    return jnp.stack(found)
-
-
 def start_pieces(places, refs, scratch, sem):
     copies = []
     for (place, first), ref in zip(places, refs):
@@ -84,12 +76,12 @@
 
 def source_of(c, t, offsets, device, count, nblk):
     mine = device[0]
-    down = (mine - offsets[t]) & (nblk - 1)
+    down = (mine - offsets(t)) & (nblk - 1)
     if c == 0:
         return 0, t, None
     if c in (1, 2):
         slot = jnp.maximum(t - 1, 0) if c == 1 else jnp.minimum(t + 1, count - 1)
-        holder = (down + offsets[slot]) & (nblk - 1)
+        holder = (down + offsets(slot)) & (nblk - 1)
         return holder ^ mine, slot, (t >= 1) if c == 1 else (t <= count - 2)
     if c == 3:
         return ((mine - 1) & (nblk - 1)) ^ mine, t, down >= 1
@@ -187,7 +179,7 @@
     return jnp.sum(jnp.sum(value, axis=0, keepdims=True), axis=1, keepdims=True)
 
 
-def first_kernel(places, count, then, offsets, device, dims, *refs):
+def first_kernel(places, count, then, offsets, device, dims, table, *refs):
     pieces = refs[: len(places)]
     lfar, rfar, href, payload, sent, held, lref, rref, ext, sem, lsem, rsem, out_sem = refs[len(places) :]
     width = href.shape[1]
@@ -203,7 +195,7 @@
     def slot(t):
         x = []
         for c in range(GROUPS):
-            place, at, on = source_of(c, t, offsets, device, count, nblk)
+            place, at, on = source_of(c, t, lambda i: offsets[i], device, count, nblk)
             x.append(only(on, block_of(held, place, at, width)))
         h = jnp.where(inside(dims[t, 0], dims[t, 1], (width, width)), ham_sum(x, t, lref, rref), 0.0)
         href[t] = h
@@ -229,15 +221,70 @@
     mid = rest.astype(BF16).astype(F32)
     low = rest - mid
     split = jnp.where(lane == 0, high, jnp.where(lane == 1, mid, jnp.where(lane == 2, low, 0.0)))
-    payload[pl.ds(count * width, EXTRA), :] = jnp.where(row < count, now, split).astype(BF16)
+    extra = jnp.where(row < count, now, split)
+    extra = jnp.where(row == count + 2, table[0:1, :], jnp.where(row == count + 3, table[1:2, :], extra))
+    payload[pl.ds(count * width, EXTRA), :] = extra.astype(BF16)
     for copy in outgoing:
         copy.wait()
 
 
-def second_kernel(places, count, cells, used, offsets, device, dims, *refs):
+def layout_of(caps, offsets, device, sec, count, secs, late):
+    nblk = caps.shape[0]
+    row = lax.broadcasted_iota(jnp.int32, caps.shape, 0)
+    lane = lax.broadcasted_iota(jnp.int32, caps.shape, 1)
+    sec_of = sum((lane >= count * k).astype(jnp.int32) for k in range(1, secs))
+    up = lane - count * sec_of
+    down = ((row ^ device) - offsets) & (nblk - 1)
+
+    def by_sector(value):
+        rows = [jnp.sum(jnp.where(down == e, value, 0.0), axis=0, keepdims=True) for e in range(nblk)]
+        return jnp.concatenate(rows, 0)
+
+    def by_place(value):
+        return sum(jnp.where(down == e, value[e : e + 1], 0.0) for e in range(nblk))
+
+    own = by_sector(caps)
+    none = jnp.zeros_like(own[:1])
+    groups = [
+        own,
+        jnp.where(up >= 1, pltpu.roll(own, 1, 1), 0.0),
+        jnp.where(up <= count - 2, pltpu.roll(own, 127, 1), 0.0),
+        jnp.concatenate([none, own[:-1]], 0),
+        jnp.concatenate([own[1:], none], 0),
+    ]
+    wide = sum((end - low) * groups[c] for c, low, end in late)
+    used = jnp.floor((own + 15.0) / 16.0) * 16.0 * jnp.floor((wide + 127.0) / 128.0)
+    groups = [by_place(value) for value in groups]
+    used = by_place(used)
+    most = jnp.zeros((1, 1), F32)
+    for s in range(secs - 1):
+        rows = jnp.sum(jnp.where(sec_of == s, used, 0.0), axis=1, keepdims=True)
+        most = jnp.maximum(most, jnp.max(rows, axis=0, keepdims=True))
+    line = lax.broadcasted_iota(jnp.int32, (8, 128), 0)
+    place = lax.broadcasted_iota(jnp.int32, (8, 128), 1)
+    tables = []
+    for s in (sec, jnp.maximum(sec - 1, 0)):
+
+        def mine(value, s=s):
+            value = jnp.broadcast_to(value[:1], (8, 128))
+            return jnp.where(place < count, pltpu.roll(value, (128 - count * s) & 127, 1), 0.0)
+
+        rows = mine(used)
+        ends = rows
+        for shift in (1, 2, 4, 8):
+            ends = ends + jnp.where(place >= shift, pltpu.roll(ends, shift, 1), 0.0)
+        lines = [groups[0], *groups, offsets.astype(F32)]
+        table = ends - rows
+        for i, value in enumerate(lines):
+            table = jnp.where(line == i, mine(value), table)
+        tables.append(table.astype(jnp.int32))
+    return most, tables
+
+
+def second_kernel(places, count, cells, secs, late, used, offsets, device, dims, *refs):
     n = len(places)
     vpieces, rpieces = refs[:n], refs[n : 2 * n]
-    lfar, rfar, gref, sums, vsrc, wsrc, vheld, rheld, lref, rref, ext, vsem, hsem, lsem, rsem = refs[2 * n :]
+    lfar, rfar, gref, sums, tables, vsrc, wsrc, vheld, rheld, lref, rref, ext, vsem, hsem, lsem, rsem = refs[2 * n :]
     width = gref.shape[1]
     nblk = vheld.shape[0]
     srow = lax.broadcasted_iota(jnp.int32, sums.shape, 0)
@@ -245,20 +292,28 @@
     copies = start_pieces(places, rpieces, rheld, hsem) + start_pieces(places, vpieces, vheld, vsem)
     bring_in(envs, count, copies)
     both = jnp.zeros((EXTRA, 128), F32)
+    caps = []
     for place in range(nblk):
         part = rheld[place, pl.ds(count * width, EXTRA), :].astype(F32)
         ext[pl.ds(place * EXTRA, EXTRA), :] = part
+        caps.append(part[count + 2 : count + 3])
         both = both + part
+    turns = part[count + 3 : count + 4].astype(jnp.int32)
+    most, (table, table_before) = layout_of(
+        jnp.concatenate(caps, 0), turns, device[0], device[1], count, secs, late
+    )
+    tables[0], tables[1] = table, table_before
     both = jnp.sum(both, axis=1, keepdims=True)
     norm, num = both[count : count + 1], both[count + 1 : count + 2]
-    sums[...] = jnp.where(srow == 2, num / norm, jnp.where(srow == 3, jnp.sqrt(cells / norm), 0.0))
+    firsts = jnp.where(srow == 2, num / norm, jnp.where(srow == 3, jnp.sqrt(cells / norm), 0.0))
+    sums[...] = jnp.where(srow == 4, most, firsts)
     a_zero, scale = sums[2:3, :], sums[3:4, :]
 
     def slot(t):
         x = []
         squares = None
         for c in range(GROUPS):
-            place, at, on = source_of(c, t, offsets, device, count, nblk)
+            place, at, on = source_of(c, t, lambda i: offsets[i], device, count, nblk)
             v = only(on, block_of(vheld, place, at, width))
             r = block_of(rheld, place, at, width).astype(F32)
             alpha = ext[pl.ds(place * EXTRA + at, 1), :]
@@ -278,7 +333,7 @@
     over_slots(count, slot, HAM_STEP, arrival(envs, count))
 
 
-def ritz_kernel(count, cells, ranks, parts, vsrc, wsrc, facts, passed, coefs):
+def ritz_kernel(count, cells, ranks, parts, vsrc, wsrc, passed, coefs):
     width = vsrc.shape[2]
     both = parts[0]
     for i in range(1, parts.shape[0]):
@@ -295,7 +350,6 @@
     row = lax.broadcasted_iota(jnp.int32, coefs.shape, 0)
     coefs[...] = jnp.where(row == 0, from_v, jnp.where(row == 1, from_w, ritz))
     lane = lax.broadcasted_iota(jnp.int32, (width, width), 1)
-    passed[pl.ds(count * width, EXTRA), :] = facts[...]
 
     def slot(t):
         state = from_v * vsrc[0, t].astype(F32) + from_w * wsrc[0, t].astype(F32)
@@ -310,7 +364,7 @@
     return jnp.concatenate([blocks[width * k : width * (k + 1)] for k in range(blocks.shape[0] // width)], 1)
 
 
-def pack_kernel(count, late, used, caps, src_caps, starts, coefs, vsrc, wsrc, far, out, lref, accs, sem):
+def pack_kernel(count, late, used, table, coefs, vsrc, wsrc, far, out, lref, accs, sem):
     width = vsrc.shape[2]
     per = accs.shape[0]
     lane = lax.broadcasted_iota(jnp.int32, (width, width), 1)
@@ -337,10 +391,10 @@
         return jnp.where(lane < cap, state, 0.0)
 
     def slot(t, acc):
-        own = kept_block(0, t, caps[t]).T.astype(BF16)
+        own = kept_block(0, t, table[0, t]).T.astype(BF16)
         at, first = jnp.int32(0), 0
         for c, low, end in late:
-            cap = src_caps[c, t]
+            cap = table[1 + c, t]
             left = jnp.concatenate([lref[first + k, t] for k in range(end - low)], 0)
             inner = jnp.dot(left, kept_block(c, t, cap).astype(BF16), preferred_element_type=F32).astype(BF16)
             update = jnp.dot(own, stacked(inner), preferred_element_type=F32)
@@ -360,10 +414,10 @@
         tiles = [slot(g * per + p, accs.at[p]) for p in range(per)]
         for p in range(per):
             t = g * per + p
-            high = (caps[t] + 15) // 16 * 16
+            high = (table[0, t] + 15) // 16 * 16
 
             def flush(tile, c, t=t, p=p, high=high):
-                first = jnp.minimum(starts[t] + tile * high, out.shape[0] - width)
+                first = jnp.minimum(table[7, t] + tile * high, out.shape[0] - width)
                 out[pl.ds(pl.multiple_of(first, 16), width), :] = accs[p, tile].astype(BF16)
                 return c
 
@@ -414,7 +468,7 @@
     lax.fori_loop(0, count // per, wait, 0)
 
 
-def unpack_kernel(count, late, caps, src_caps, starts, first_sec, packed, lenv, so_far, out, made, sem):
+def unpack_kernel(count, late, table, first_sec, packed, lenv, so_far, out, made, sem):
     del so_far
     width = packed.shape[1]
 
@@ -427,16 +481,16 @@
         lane = lax.broadcasted_iota(jnp.int32, (width, width), 1)
 
         def slot(t):
-            high = (caps[t] + 15) // 16 * 16
+            high = (table[0, t] + 15) // 16 * 16
             at, first = jnp.int32(0), 0
             for c, low, end in late:
-                mine = src_caps[c, t]
-                valid = inside(caps[t], mine, (width, width))
+                mine = table[1 + c, t]
+                valid = inside(table[0, t], mine, (width, width))
                 for k in range(end - low):
                     tile = jnp.where(mine > 0, at // width, 0)
                     lead = at - at // width * width
-                    near = packed[pl.ds(pl.multiple_of(starts[t] + tile * high, 16), width), :]
-                    next_one = packed[pl.ds(pl.multiple_of(starts[t] + (tile + 1) * high, 16), width), :]
+                    near = packed[pl.ds(pl.multiple_of(table[7, t] + tile * high, 16), width), :]
+                    next_one = packed[pl.ds(pl.multiple_of(table[7, t] + (tile + 1) * high, 16), width), :]
                     both = jnp.where(lane >= lead, near.astype(F32), next_one.astype(F32))
                     both = pltpu.roll(both, width - lead, 1)
                     made[first + k, t] = jnp.where(valid, both, 0.0).astype(BF16)
@@ -448,7 +502,7 @@
         wait_out(late, out, made, sem, count, per)
 
 
-def early_kernel(places, count, early, offsets, device, first_sec, *refs):
+def early_kernel(places, count, early, table, device, first_sec, *refs):
     pieces = refs[: len(places)]
     one, two, lenv, out, held, sent, made, sem, far_sem, out_sem = refs[len(places) :]
     width = made.shape[2]
@@ -473,7 +527,7 @@
             own = block_of(held, 0, t, width).astype(F32).T.astype(BF16)
             first = 0
             for c, low, end in early:
-                place, at, on = source_of(c, t, offsets, device, count, nblk)
+                place, at, on = source_of(c, t, lambda i: table[6, i], device, count, nblk)
                 kept = only(on, block_of(held, place, at, width))
                 left = jnp.concatenate([sent[first + k, t] for k in range(end - low)], 0)
                 inner = jnp.dot(left, kept, preferred_element_type=F32).astype(BF16)
@@ -498,11 +552,12 @@
     cells = float(count * nblk * width * width)
     lines = jnp.arange(width, dtype=jnp.int32)
     first_sec = jnp.reshape((lax.axis_index("sec") == 0).astype(jnp.int32), (1,))
-    mine = jnp.reshape(device.astype(jnp.int32), (1,))
+    sec, secs = lax.axis_index("sec"), lax.axis_size("sec")
+    mine = jnp.stack([device, sec]).astype(jnp.int32)
     by_group = lenv.reshape((kinds, GROUPS, count, width, width))
     at_once, then, late = shares(kinds)
     early = at_once + then
-    used = (0,) + tuple(c for c, _, _ in late)
+    used = (0,) + tuple(c for c, _, _ in late if c)
     n_then, n_late = (sum(end - low for _, low, end in share) for share in (then, late))
     n_early = channels - n_late
 
@@ -510,10 +565,15 @@
         lines[None, None, :] < dims[:, 1][:, None, None]
     )
     vzero = jnp.where(mask_on, start, jnp.zeros_like(start))
-    caps = jnp.minimum(dims[:, 1], ranks)
-    meta = jnp.zeros((EXTRA, width), BF16).at[0, :count].set(caps.astype(BF16))
-    vpieces = gathered(jnp.concatenate([vzero.reshape((body, width)), meta]))
-    sent_one = onward(lenv[:GROUPS])
+    both = jnp.stack([jnp.minimum(dims[:, 1], ranks), offsets]).astype(F32)
+    zero = jnp.zeros((), jnp.int32)
+    own_lanes = lax.dynamic_update_slice(jnp.zeros((8, 128), F32), both, (zero, (count * sec).astype(jnp.int32)))
+    table = own_lanes
+    for shift in range(1, secs):
+        table = table + lax.ppermute(own_lanes, "sec", [(i, (i + shift) % secs) for i in range(secs)])
+    vpieces = gathered(vzero.reshape((body, width)))
+    sent_one, table = lax.optimization_barrier((lenv[: len(at_once)], table))
+    sent_one = onward(sent_one)
     places = tuple((place, first) for _, place, first in vpieces)
     n = len(places)
     vrows = [in_hbm(rows) for rows, _, _ in vpieces]
@@ -548,87 +608,48 @@
     hzero, rpay, sent_two = call(
         functools.partial(first_kernel, places, count, then),
         "ham_first",
-        [scalars] * 3 + [anywhere] * n + [far] * 2,
+        [scalars] * 3 + [near] + [anywhere] * n + [far] * 2,
         [near, near, far],
         [wide_shape, pay_shape, jax.ShapeDtypeStruct((n_then, count, width, width), BF16)],
         [held, env, env, pltpu.VMEM((EXTRA, 128), F32), dma(n), dma(steps), dma(steps), dma(n_then)],
-    )(offsets, mine, dims, *vrows, in_hbm(lenv), in_hbm(renv))
+    )(offsets, mine, dims, table, *vrows, in_hbm(lenv), in_hbm(renv))
 
     rpieces = gathered(rpay)
-    gone, sums, vsrc, wsrc = call(
-        functools.partial(second_kernel, places, count, cells, used),
+    gone, sums, tables, vsrc, wsrc = call(
+        functools.partial(second_kernel, places, count, cells, secs, late, used),
         "ham_second",
         [scalars] * 3 + [anywhere] * (2 * n) + [far] * 2,
-        [near] * 4,
-        [wide_shape, row_shape, used_shape, used_shape],
+        [near] * 5,
+        [wide_shape, row_shape, jax.ShapeDtypeStruct((2, 8, 128), jnp.int32), used_shape, used_shape],
         [
             held, held, env, env, pltpu.VMEM((nblk * EXTRA, 128), F32),
             dma(n), dma(n), dma(steps), dma(steps),
         ],
     )(offsets, mine, dims, *vrows, *[rows for rows, _, _ in rpieces], in_hbm(lenv), in_hbm(renv))
 
-    offsets, caps, hzero = lax.optimization_barrier((offsets, caps, hzero))
-    all_caps = extras_of(vpieces, nblk, body)[:, 0, :count].astype(jnp.int32).reshape((-1,))
-    up_val = jnp.arange(count, dtype=jnp.int32)
-
-    def layout(caps, src_caps):
-        high = (caps + 15) // 16 * 16
-        wide = (sum((end - low) * src_caps[c] for c, low, end in late) + width - 1) // width
-        ends = jnp.cumsum(high * wide)
-        return ends - high * wide, ends[-1]
-
-    def used_by(holder):
-        down_val = (holder - offsets) % nblk
-        holders = [
-            jnp.broadcast_to(holder, (count,)),
-            (down_val + jnp.roll(offsets, 1)) % nblk,
-            (down_val + jnp.roll(offsets, -1)) % nblk,
-            jnp.broadcast_to((holder - 1) % nblk, (count,)),
-            jnp.broadcast_to((holder + 1) % nblk, (count,)),
-        ]
-        slots = [up_val, jnp.maximum(up_val - 1, 0), jnp.minimum(up_val + 1, count - 1), up_val, up_val]
-        there = [up_val >= 0, up_val >= 1, up_val <= count - 2, down_val >= 1, down_val <= nblk - 2]
-        entries = (jnp.stack(holders) ^ device) * count + jnp.stack(slots)
-        match = entries[..., None] == jnp.arange(all_caps.shape[0], dtype=jnp.int32)
-        found = jnp.sum(jnp.where(match, all_caps, 0), axis=-1)
-        found = jnp.where(jnp.stack(there), found, 0).astype(jnp.int32)
-        return found, *layout(found[0], found)
-
-    src_caps, starts, _ = used_by(device)
-    needed = jnp.max(jax.vmap(lambda holder: used_by(holder)[2])(jnp.arange(nblk, dtype=jnp.int32)))
-    length = lax.axis_size("sec")
-    needed = jnp.where(lax.axis_index("sec") == length - 1, 0, needed).astype(F32)
-    needed, sums = lax.optimization_barrier((needed, sums))
-    needed = jnp.full((8, 128), needed)
-    most_needed = needed
-    for shift in range(1, length):
-        turn = [(i, (i + shift) % length) for i in range(length)]
-        most_needed = jnp.maximum(most_needed, lax.ppermute(needed, "sec", turn))
     sent_two = onward(sent_two)
-    most_needed = most_needed[0, 0].astype(jnp.int32)
-
     parts = lax.all_gather(sums, "blk", axis=0)
-    facts = jnp.concatenate([caps[None], src_caps, offsets[None]], axis=0).astype(BF16)
-    facts = jnp.zeros((EXTRA, width), BF16).at[: facts.shape[0], :count].set(facts)
+    most_needed = sums[4, 0].astype(jnp.int32)
+    table, table_before = tables[0], tables[1]
 
     most = count * n_late * width + SLACK
     out_shape = jax.ShapeDtypeStruct(by_group.shape, BF16)
     per = step_of(count, PACK_STEP)
 
     def finish(rows):
-        def branch(parts, hzero, gone, vsrc, wsrc, sent_one, sent_two):
+        def branch(parts, hzero, gone, vsrc, wsrc, sent_one, sent_two, table, table_before):
             passed, coefs = call(
                 functools.partial(ritz_kernel, count, cells),
                 "ritz",
-                [scalars] + [near] * 4,
+                [scalars] + [near] * 3,
                 [near] * 2,
-                [pay_shape, row_shape],
-            )(ranks, parts, vsrc, wsrc, facts)
+                [jax.ShapeDtypeStruct((body, width), BF16), row_shape],
+            )(ranks, parts, vsrc, wsrc)
             passed = onward(passed)
             packed = call(
                 functools.partial(pack_kernel, count, late, used),
                 "pack_update",
-                [scalars] * 3 + [near] * 3 + [far],
+                [scalars] + [near] * 3 + [far],
                 near,
                 jax.ShapeDtypeStruct((rows, width), BF16),
                 [
@@ -637,18 +658,15 @@
                     dma(len(late), count // per),
                 ],
                 moved=20 * 1024 * 1024,
-            )(caps, src_caps, starts, coefs, vsrc, wsrc, in_hbm(by_group))
+            )(table, coefs, vsrc, wsrc, in_hbm(by_group))
             packed, passed = lax.optimization_barrier((packed, passed))
             arrived = onward(packed)
             kpieces = gathered(passed)
-            rows_last, coefs = lax.optimization_barrier((kpieces[-1][0], coefs))
-            kpieces[-1] = (rows_last, *kpieces[-1][1:])
+            rows_two, coefs = lax.optimization_barrier((kpieces[2][0], coefs))
+            kpieces[2] = (rows_two, *kpieces[2][1:])
             from_v, from_w, ritz = coefs[0, 0], coefs[1, 0], coefs[2, 0]
             state_new = (from_v * vsrc[0].astype(F32) + from_w * wsrc[0].astype(F32)).astype(BF16)
             hstate_new = (from_v * hzero + from_w * gone).astype(BF16)
-            facts_in = passed[body:, :count].astype(jnp.int32)
-            prev_caps, prev_src, prev_offsets = facts_in[0], facts_in[1 : 1 + GROUPS], facts_in[1 + GROUPS]
-            prev_starts, _ = layout(prev_caps, prev_src)
             so_far = call(
                 functools.partial(early_kernel, places, count, early),
                 "early_update",
@@ -663,24 +681,24 @@
                     dma(2),
                     dma(len(early) * count),
                 ],
-            )(prev_offsets, mine, first_sec, *[r for r, _, _ in kpieces], in_hbm(sent_one), in_hbm(sent_two), in_hbm(by_group))
+            )(table_before, mine, first_sec, *[r for r, _, _ in kpieces], in_hbm(sent_one), in_hbm(sent_two), in_hbm(by_group))
             next_left = call(
                 functools.partial(unpack_kernel, count, late),
                 "unpack_update",
-                [scalars] * 4 + [near] + [far] * 2,
+                [scalars] * 2 + [near] + [far] * 2,
                 far,
                 out_shape,
                 [pltpu.VMEM((n_late, count, width, width), BF16), dma(len(late) * count)],
-                {6: 0},
-            )(prev_caps, prev_src, prev_starts, first_sec, arrived, in_hbm(by_group), in_hbm(so_far))
+                {4: 0},
+            )(table_before, first_sec, arrived, in_hbm(by_group), in_hbm(so_far))
             return state_new, hstate_new, ritz, next_left
 
         return branch
 
-    sizes = [most * part // 64 // 16 * 16 for part in (20, 24, 26, 27, 28, 30, 36)] + [most]
+    sizes = [most * part // 64 // 16 * 16 for part in (28, 32)] + [most]
     tier = sum((most_needed + SLACK > size).astype(jnp.int32) for size in sizes[:-1])
     state_new, hstate_new, ritz, next_left = lax.switch(
-        tier, [finish(size) for size in sizes], parts, hzero, gone, vsrc, wsrc, sent_one, sent_two
+        tier, [finish(size) for size in sizes], parts, hzero, gone, vsrc, wsrc, sent_one, sent_two, table, table_before
     )
     next_left = next_left.reshape((channels, count, width, width))
     return (state_new[None], hstate_new[None], jnp.reshape(ritz, (1,)), next_left[None])

time: 168 us -> 158 us (0.940)
  waiting for transfers between devices: 36.9 us -> 53.6 us
  loops' own time: 10.4 us -> 0.35 us
  other arithmetic: 12.4 us -> 5.79 us
  starting transfers between devices: 33.6 us -> 29.2 us
  local copies, waits for them, and re-layouts: 10.4 us -> 7.72 us
  between operations: 3.55 us -> 1.54 us
  Pallas kernels: 50.9 us -> 49.2 us
    ppermute x4, waiting for transfers between devices: 1.19 us -> 19 us  [onward(): return lax.ppermute(value, 'sec', [(i, i + 1) for i in range(length - 1)])]
    unnamed x1, loops' own time: 10.4 us -> 0.35 us
    ppermute x4, starting transfers between devices: 14 us -> 8.78 us  [onward(): return lax.ppermute(value, 'sec', [(i, i + 1) for i in range(length - 1)])]
    ppermute x3, waiting for transfers between devices: 4.39 us -> 0.01 us  [shards(): lax.ppermute(own_lanes, 'sec', [(i, (i + shift) % secs) for i in range(se...]
    ppermute x27, waiting for transfers between devices: 31.3 us -> 34.5 us  [exchange(): return lax.ppermute(value, 'blk', [(i, i ^ bit) for i in range(length)])]
    convert_element_type x4 -> x1, other arithmetic: 3.85 us -> 0.66 us  [shards(): both = jnp.stack([jnp.minimum(dims[:, 1], ranks), offsets]).astype(F32)]
    another operation x7 -> x1, other arithmetic: 1.78 us -> 0.07 us  [shards(): mine = jnp.stack([device, sec]).astype(jnp.int32)]
    slice x5 -> x2, local copies, waits for them, and re-layouts: 4.22 us -> 3.56 us  [the longest x1 3.04 us: shards(): sent_one, table = lax.optimization_barrier((lenv[:len(at_once)], table))]
  transfers between devices with their start and end apart: 34 -> 34, of which waited for: 14 -> 15; matrix products, arithmetic and copies ran while one was open for 11% -> 6% of each run, Pallas kernels for 28% -> 28%
where the time goes in v1:
time: 158 us; the launch traced here: 155 us
  waiting for transfers between devices  53.6 us (34%)
  Pallas kernels  49.2 us (31%)
  starting transfers between devices  29.2 us (18%)
  blocking collectives  8.09 us (5%)
  local copies, waits for them, and re-layouts  7.72 us (5%)
  other arithmetic  5.79 us (4%)
    ppermute x27, waiting for transfers between devices, exchange(): return lax.ppermute(value, 'blk', [(i, i ^ bit) for i in range(length)])  34.5 us
    ppermute x4, waiting for transfers between devices, onward(): return lax.ppermute(value, 'sec', [(i, i + 1) for i in range(length - 1)])  19 us
    ppermute x27, starting transfers between devices, exchange(): return lax.ppermute(value, 'blk', [(i, i ^ bit) for i in range(length)])  15.7 us
    pallas_call x1, Pallas kernels, shards(): call(functools.partial(second_kernel, places, count, cells, secs, late, u...  12.9 us
    pallas_call x1, Pallas kernels, shards(): call(functools.partial(first_kernel, places, count, then), 'ham_first', [...  11.9 us
    pallas_call x1, Pallas kernels, branch(): call(functools.partial(early_kernel, places, count, early), 'early_update...  11.2 us
    ppermute x4, starting transfers between devices, onward(): return lax.ppermute(value, 'sec', [(i, i + 1) for i in range(length - 1)])  8.78 us
    all_gather x1, blocking collectives, shards(): parts = lax.all_gather(sums, 'blk', axis=0)  8.09 us
  transfers between devices with their start and end apart: 34, of which 15 were waited for; matrix products, arithmetic and copies ran while one was open for 6% of the time, Pallas kernels for 28%

profile of v1, /device:TPU:8, one launch (start us, length us, event | category | flops | bytes accessed | tf_op | source)
XLA Modules:
  0.0 155.4 jit_solution(8471916455551529230)
XLA Ops:
  0.6 0.7 bitcast_minimum_fusion
  1.3 0.7 add_convert_fusion.3
  2.5 1.6 %collective-permute-start.42 = (f32[8,128]{1,0:T(8,128)S(1)}, f32[8,128]{1,0:T(8,128)S(1)}, u32[]{:S(2)}, u32[]{:S(2)}) collective-permute-start(f32[8,128]{1,0:T(8,128)S(1)} %dynamic_update_slice.5), channel_id=1, source_target_pairs={{0,8},{8,16},{16,24},{24,0},{1,9},{9,17},{17,25},{25,1},{2,10},{10... | collective-permute-start | bytes 12296 | tf_op jit(solution)/shard_map/ppermute | solution.py:573
  4.1 1.1 collective-permute-start.43
  5.2 1.9 %collective-permute-start.44 = (f32[8,128]{1,0:T(8,128)S(1)}, f32[8,128]{1,0:T(8,128)S(1)}, u32[]{:S(2)}, u32[]{:S(2)}) collective-permute-start(f32[8,128]{1,0:T(8,128)S(1)} %dynamic_update_slice.5), channel_id=1, source_target_pairs={{0,24},{8,0},{16,8},{24,16},{1,25},{9,1},{17,9},{25,17},{2,26},{10... | collective-permute-start | bytes 12296 | tf_op jit(solution)/shard_map/ppermute | solution.py:573
  7.2 0.8 slice_bitcast_fusion.8
  8.1 1.3 fusion.3.refs_0_
  9.4 1.6 %collective-permute-start.34 = (bf16[1536,128]{1,0:T(8,128)(2,1)S(1)}, bf16[1536,128]{1,0:T(8,128)(2,1)S(1)}, u32[]{:S(2)}, u32[]{:S(2)}) collective-permute-start(bf16[1536,128]{1,0:T(8,128)(2,1)S(1)} %fusion.3.refs_0_), channel_id=1, source_target_pairs={{0,2},{1,3},{2,0},{3,1},{4,6},{5,7},{6,4},{7,5},{8,10},{9,11},{10,... | collective-permute-start | bytes 1179656 | tf_op jit(solution)/shard_map/ppermute | solution.py:34
  10.9 1.5 collective-permute-start.36
  12.5 3.0 %slice_bitcast_fusion.6 = bf16[5,12,128,128]{3,2,1,0:T(8,128)(2,1)} fusion(bf16[1,20,12,128,128]{4,3,2,1,0:T(8,128)(2,1)} %param.10), kind=kLoop, calls=%fused_computation.15 | loop fusion | bytes 3932160 | tf_op jit(solution)/shard_map/slice | solution.py:575
  16.1 2.0 %collective-permute-start.54 = (bf16[5,12,128,128]{3,2,1,0:T(8,128)(2,1)}, bf16[5,12,128,128]{3,2,1,0:T(8,128)(2,1)}, u32[]{:S(2)}, u32[]{:S(2)}) collective-permute-start(bf16[5,12,128,128]{3,2,1,0:T(8,128)(2,1)} %slice_bitcast_fusion.6), channel_id=1, source_target_pairs={{0,8},{8,16},{16,24},{1,9},{9,17},{17,25},{2,10},{10,18},{18,26},{... | collective-permute-start | bytes 5898248 | tf_op jit(solution)/shard_map/ppermute | solution.py:39
  18.1 1.4 collective-permute-done.34.refs_2_
  19.5 1.6 %collective-permute-start.38 = (bf16[768,128]{1,0:T(8,128)(2,1)S(1)}, bf16[768,128]{1,0:T(8,128)(2,1)S(1)}, u32[]{:S(2)}, u32[]{:S(2)}) collective-permute-start(bf16[768,128]{1,0:T(8,128)(2,1)S(1)} %slice.126), channel_id=1, source_target_pairs={{0,4},{1,5},{2,6},{3,7},{4,0},{5,1},{6,2},{7,3},{8,12},{9,13},{10,... | collective-permute-start | bytes 589832 | tf_op jit(solution)/shard_map/ppermute | solution.py:34
  21.1 1.6 %collective-permute-start.39 = (bf16[768,128]{1,0:T(8,128)(2,1)S(1)}, bf16[768,128]{1,0:T(8,128)(2,1)S(1)}, u32[]{:S(2)}, u32[]{:S(2)}) collective-permute-start(bf16[768,128]{1,0:T(8,128)(2,1)S(1)} %slice.127), channel_id=1, source_target_pairs={{0,2},{1,3},{2,0},{3,1},{4,6},{5,7},{6,4},{7,5},{8,10},{9,11},{10,... | collective-permute-start | bytes 589832 | tf_op jit(solution)/shard_map/ppermute | solution.py:34
  23.2 2.2 %collective-permute-done.38.refs_6_ = bf16[768,128]{1,0:T(8,128)(2,1)S(1)} collective-permute-done((bf16[768,128]{1,0:T(8,128)(2,1)S(1)}, bf16[768,128]{1,0:T(8,128)(2,1)S(1)}, u32[]{:S(2)}, u32[]{:S(2)}) %collective-permute-start.38) | collective-permute-done | bytes 196640 | tf_op jit(solution)/shard_map/ppermute | solution.py:34
  25.4 1.4 collective-permute-done.39.refs_7_
  27.0 1.3 collective-permute-done.41.refs_9_
  29.2 11.9 %ham_first.1 = (f32[12,128,128]{2,1,0:T(8,128)}, bf16[1552,128]{1,0:T(8,128)(2,1)S(1)}, bf16[3,12,128,128]{3,2,1,0:T(8,128)(2,1)}) custom-call(s32[12]{0:T(128)S(1)} %bitcast.63, s32[2]{0:T(128)S(1)} %pad_add_fusion.device, s32[12,2]{1,0:T(8,128)S(1)} %copy.14.dims, f32[8,128]{1,0:T(8,128)S(1)} %add_add_fusion.table, bf16[1536,128]{1,0:T(8,128)(2,1)} %copy-done.2, ...), custom_call_target="tpu_custom_call" | custom-call | flops 1 | bytes 1 | tf_op jit(solution)/shard_map/ham_first/pallas_call | solution.py:608
  41.1 2.3 %collective-permute-start.55 = (bf16[3,12,128,128]{3,2,1,0:T(8,128)(2,1)}, bf16[3,12,128,128]{3,2,1,0:T(8,128)(2,1)}, u32[]{:S(2)}, u32[]{:S(2)}) collective-permute-start(bf16[3,12,128,128]{3,2,1,0:T(8,128)(2,1)} %get-tuple-element.192), channel_id=1, source_target_pairs={{0,8},{8,16},{16,24},{1,9},{9,17},{17,25},{2,10},{10,18},{18,26},{... | collective-permute-start | bytes 3538952 | tf_op jit(solution)/shard_map/ppermute | solution.py:39
  43.4 1.3 collective-permute-start.48
  44.7 0.8 collective-permute-start.46
  45.5 9.0 %collective-permute-done.48.refs_14_ = bf16[1552,128]{1,0:T(8,128)(2,1)S(1)} collective-permute-done((bf16[1552,128]{1,0:T(8,128)(2,1)S(1)}, bf16[1552,128]{1,0:T(8,128)(2,1)S(1)}, u32[]{:S(2)}, u32[]{:S(2)}) %collective-permute-start.48) | collective-permute-done | bytes 397344 | tf_op jit(solution)/shard_map/ppermute | solution.py:34
  54.5 1.6 %collective-permute-start.51 = (bf16[784,128]{1,0:T(8,128)(2,1)S(1)}, bf16[784,128]{1,0:T(8,128)(2,1)S(1)}, u32[]{:S(2)}, u32[]{:S(2)}) collective-permute-start(bf16[784,128]{1,0:T(8,128)(2,1)S(1)} %slice.129), channel_id=1, source_target_pairs={{0,2},{1,3},{2,0},{3,1},{4,6},{5,7},{6,4},{7,5},{8,10},{9,11},{10,... | collective-permute-start | bytes 602120 | tf_op jit(solution)/shard_map/ppermute | solution.py:34
  56.6 5.2 %collective-permute-done.50.refs_16_ = bf16[768,128]{1,0:T(8,128)(2,1)S(1)} collective-permute-done((bf16[768,128]{1,0:T(8,128)(2,1)S(1)}, bf16[768,128]{1,0:T(8,128)(2,1)S(1)}, u32[]{:S(2)}, u32[]{:S(2)}) %collective-permute-start.50) | collective-permute-done | bytes 196640 | tf_op jit(solution)/shard_map/ppermute | solution.py:34
  62.3 1.5 collective-permute-done.52.refs_18_
  63.9 1.3 collective-permute-done.53.refs_19_
  65.2 12.9 %ham_second.1 = (f32[12,128,128]{2,1,0:T(8,128)S(1)}, f32[8,128]{1,0:T(8,128)S(1)}, s32[2,8,128]{2,1,0:T(8,128)S(1)}, bf16[5,12,128,128]{3,2,1,0:T(8,128)(2,1)S(1)}, bf16[5,12,128,128]{3,2,1,0:T(8,128)(2,1)S(1)}) custom-call(s32[12]{0:T(128)S(1)} %bitcast.64, s32[2]{0:T(128)S(1)} %pad_add_fusion.device, s32[12,2]{1,0:T(8,128)S(1)} %copy.14.dims, ...), custom_call_target="tpu_custom_call" | custom-call | flops 1 | bytes 1 | tf_op jit(solution)/shard_map/ham_second/pallas_call | solution.py:618
  79.3 8.1 %all-gather = f32[64,128]{1,0:T(8,128)S(1)} all-gather(f32[8,128]{1,0:T(8,128)S(1)} %get-tuple-element.185), channel_id=2, replica_groups=mesh['sec'=4,'blk'=8] {'blk'}, dimensions={0}, use_global_device_ids=true | all-gather | bytes 36864 | tf_op jit(solution)/shard_map/all_gather | solution.py:631
  87.4 1.4 collective-permute-done.55
  88.8 65.7 %conditional.4 = (bf16[1,12,128,128]{3,2,1,0:T(8,128)(2,1)S(1)}, f32[1]{0:T(128)}, bf16[1,20,12,128,128]{4,3,2,1,0:T(8,128)(2,1)}, bf16[1,12,128,128]{3,2,1,0:T(8,128)(2,1)S(1)}) conditional(s32[]{:T(128)} %bitcast.43, (s32[2,8,128]{2,1,0:T(8,128)S(1)}, s32[1,12]{1,0:T(1,128)S(1)}, f32[8,8,128]{2,1,0:T(8,128)S(1)}, ...), branch_computations={%region_0.1_spmd, %region_1.2_spmd, %region_2.3_spmd} | conditional | flops 1966084 | bytes 56508928
  88.8 0.8 ritz.3
  89.6 2.2 %collective-permute-start = (bf16[1536,128]{1,0:T(8,128)(2,1)S(1)}, bf16[1536,128]{1,0:T(8,128)(2,1)S(1)}, u32[]{:S(2)}, u32[]{:S(2)}) collective-permute-start(bf16[1536,128]{1,0:T(8,128)(2,1)S(1)} %get-tuple-element.118), channel_id=1, source_target_pairs={{0,8},{8,16},{16,24},{1,9},{9,17},{17,25},{2,10},{10,18},{18,26},{... | collective-permute-start | bytes 1179656 | tf_op jit(solution)/shard_map/cond/branch_0_fun/ppermute | solution.py:39
  91.8 8.1 %pack_update.3 = bf16[8112,128]{1,0:T(8,128)(2,1)S(1)} custom-call(s32[8,128]{1,0:T(8,128)S(1)} %get-tuple-element.204.table, f32[8,128]{1,0:T(8,128)S(1)} %get-tuple-element.120.coefs, bf16[5,12,128,128]{3,2,1,0:T(8,128)(2,1)S(1)} %get-tuple-element.114.vsrc, bf16[5,12,128,128]{3,2,1,0:T(8,128)(2,1)S(1)} %get-tuple-element.115.wsrc, ...), custom_call_target="tpu_custom_call" | custom-call | flops 1 | bytes 20971520 | tf_op jit(solution)/shard_map/cond/branch_0_fun/pack_update/pallas_call | solution.py:649
  99.9 2.3 %collective-permute-done.refs_0_ = bf16[1536,128]{1,0:T(8,128)(2,1)S(1)} collective-permute-done((bf16[1536,128]{1,0:T(8,128)(2,1)S(1)}, bf16[1536,128]{1,0:T(8,128)(2,1)S(1)}, u32[]{:S(2)}, u32[]{:S(2)}) %collective-permute-start) | collective-permute-done | bytes 393248 | tf_op jit(solution)/shard_map/cond/branch_0_fun/ppermute | solution.py:39
  102.2 2.3 %collective-permute-start.2 = (bf16[8112,128]{1,0:T(8,128)(2,1)S(1)}, bf16[8112,128]{1,0:T(8,128)(2,1)S(1)}, u32[]{:S(2)}, u32[]{:S(2)}) collective-permute-start(bf16[8112,128]{1,0:T(8,128)(2,1)S(1)} %pack_update.3), channel_id=1, source_target_pairs={{0,8},{8,16},{16,24},{1,9},{9,17},{17,25},{2,10},{10,18},{18,26},{... | collective-permute-start | bytes 6230024 | tf_op jit(solution)/shard_map/cond/branch_0_fun/ppermute | solution.py:39
  104.6 0.9 collective-permute-start.1
  106.1 8.3 %collective-permute-done.1.refs_2_ = bf16[1536,128]{1,0:T(8,128)(2,1)S(1)} collective-permute-done((bf16[1536,128]{1,0:T(8,128)(2,1)S(1)}, bf16[1536,128]{1,0:T(8,128)(2,1)S(1)}, u32[]{:S(2)}, u32[]{:S(2)}) %collective-permute-start.1) | collective-permute-done | bytes 393248 | tf_op jit(solution)/shard_map/cond/branch_0_fun/ppermute | solution.py:34
  114.4 1.0 collective-permute-done.5.refs_4_
  115.4 0.8 collective-permute-start.8
  116.2 1.4 collective-permute-start.7
  118.6 1.4 fusion
  120.0 1.1 collective-permute-done.8.refs_7_
  121.1 0.8 collective-permute-done.7.refs_6_
  122.0 1.4 multiply_add_fusion
  123.5 11.2 %early_update.3.so_far = bf16[4,5,12,128,128]{4,3,2,1,0:T(8,128)(2,1)} custom-call(s32[8,128]{1,0:T(8,128)S(1)} %get-tuple-element.203.table, s32[2]{0:T(128)S(1)} %get-tuple-element.125.device, s32[1]{0:T(128)} %bitcast.8.first_sec, bf16[1536,128]{1,0:T(8,128)(2,1)S(1)} %collective-permute-done.refs_0_, ...), custom_call_target="tpu_custom_call" | custom-call | flops 1 | bytes 1 | tf_op jit(solution)/shard_map/cond/branch_0_fun/early_update/pallas_call | solution.py:670
  134.7 15.4 %collective-permute-done.2.packed = bf16[8112,128]{1,0:T(8,128)(2,1)S(1)} collective-permute-done((bf16[8112,128]{1,0:T(8,128)(2,1)S(1)}, bf16[8112,128]{1,0:T(8,128)(2,1)S(1)}, u32[]{:S(2)}, u32[]{:S(2)}) %collective-permute-start.2) | collective-permute-done | bytes 2076704 | tf_op jit(solution)/shard_map/cond/branch_0_fun/ppermute | solution.py:39
  150.1 4.3 %unpack_update.3 = bf16[4,5,12,128,128]{4,3,2,1,0:T(8,128)(2,1)} custom-call(s32[8,128]{1,0:T(8,128)S(1)} %get-tuple-element.203.table, s32[1]{0:T(128)} %bitcast.8.first_sec, bf16[8112,128]{1,0:T(8,128)(2,1)S(1)} %collective-permute-done.2.packed, bf16[4,5,12,128,128]{4,3,2,1,0:T(8,128)(2,1)} %bitcast.69, ...), custom_call_target="tpu_custom_call", output_to_operand_aliasing={{}: (4, {})} | custom-call | flops 1 | bytes 1 | tf_op jit(solution)/shard_map/cond/branch_0_fun/unpack_update/pallas_call | solution.py:685
  154.6 0.7 copy-done.12
  (85 shorter events, 6.3 us)
Async XLA Ops:
  2.5 13.0 %collective-permute-start.42 = (f32[8,128]{1,0:T(8,128)S(1)}, f32[8,128]{1,0:T(8,128)S(1)}, u32[]{:S(2)}, u32[]{:S(2)}) collective-permute-start(f32[8,128]{1,0:T(8,128)S(1)} %dynamic_update_slice.5), channel_id=1, source_target_pairs={{0,8},{8,16},{16,24},{24,0},{1,9},{9,17},{17,25},{25,1},{2,10},{10... | collective-permute-start | bytes 12296 | tf_op jit(solution)/shard_map/ppermute | solution.py:573
  4.1 11.9 %collective-permute-start.43 = (f32[8,128]{1,0:T(8,128)S(1)}, f32[8,128]{1,0:T(8,128)S(1)}, u32[]{:S(2)}, u32[]{:S(2)}) collective-permute-start(f32[8,128]{1,0:T(8,128)S(1)} %dynamic_update_slice.5), channel_id=1, source_target_pairs={{0,16},{8,24},{16,0},{24,8},{1,17},{9,25},{17,1},{25,9},{2,18},{10... | collective-permute-start | bytes 12296 | tf_op jit(solution)/shard_map/ppermute | solution.py:573
  5.2 10.8 %collective-permute-start.44 = (f32[8,128]{1,0:T(8,128)S(1)}, f32[8,128]{1,0:T(8,128)S(1)}, u32[]{:S(2)}, u32[]{:S(2)}) collective-permute-start(f32[8,128]{1,0:T(8,128)S(1)} %dynamic_update_slice.5), channel_id=1, source_target_pairs={{0,24},{8,0},{16,8},{24,16},{1,25},{9,1},{17,9},{25,17},{2,26},{10... | collective-permute-start | bytes 12296 | tf_op jit(solution)/shard_map/ppermute | solution.py:573
  9.4 10.1 %copy-start.2 = (bf16[1536,128]{1,0:T(8,128)(2,1)}, bf16[1536,128]{1,0:T(8,128)(2,1)S(1)}, u32[]{:S(2)}) copy-start(bf16[1536,128]{1,0:T(8,128)(2,1)S(1)} %fusion.3.refs_0_) | copy-start | bytes 1179652
  9.4 6.2 %copy-start = (s32[1,12]{1,0:T(1,128)S(1)}, s32[1,12]{1,0:T(1,128)}, u32[]{:S(2)}) copy-start(s32[1,12]{1,0:T(1,128)} %param.12) | copy-start | bytes 148
  9.4 17.5 %copy-start.15 = (s32[1,12,2]{1,2,0:T(2,128)S(1)}, s32[1,12,2]{1,2,0:T(2,128)}, u32[]{:S(2)}) copy-start(s32[1,12,2]{1,2,0:T(2,128)} %param.13) | copy-start | bytes 292
  9.4 10.1 %collective-permute-start.34 = (bf16[1536,128]{1,0:T(8,128)(2,1)S(1)}, bf16[1536,128]{1,0:T(8,128)(2,1)S(1)}, u32[]{:S(2)}, u32[]{:S(2)}) collective-permute-start(bf16[1536,128]{1,0:T(8,128)(2,1)S(1)} %fusion.3.refs_0_), channel_id=1, source_target_pairs={{0,2},{1,3},{2,0},{3,1},{4,6},{5,7},{6,4},{7,5},{8,10},{9,11},{10,... | collective-permute-start | bytes 1179656 | tf_op jit(solution)/shard_map/ppermute | solution.py:34
  10.9 10.1 %collective-permute-start.36 = (bf16[1536,128]{1,0:T(8,128)(2,1)S(1)}, bf16[1536,128]{1,0:T(8,128)(2,1)S(1)}, u32[]{:S(2)}, u32[]{:S(2)}) collective-permute-start(bf16[1536,128]{1,0:T(8,128)(2,1)S(1)} %fusion.3.refs_0_), channel_id=1, source_target_pairs={{0,4},{1,5},{2,6},{3,7},{4,0},{5,1},{6,2},{7,3},{8,12},{9,13},{10,... | collective-permute-start | bytes 1179656 | tf_op jit(solution)/shard_map/ppermute | solution.py:34
  15.5 7.2 %collective-permute-start.33 = (bf16[1536,128]{1,0:T(8,128)(2,1)S(1)}, bf16[1536,128]{1,0:T(8,128)(2,1)S(1)}, u32[]{:S(2)}, u32[]{:S(2)}) collective-permute-start(bf16[1536,128]{1,0:T(8,128)(2,1)S(1)} %fusion.3.refs_0_), channel_id=1, source_target_pairs={{0,1},{1,0},{2,3},{3,2},{4,5},{5,4},{6,7},{7,6},{8,9},{9,8},{10,11... | collective-permute-start | bytes 1179656 | tf_op jit(solution)/shard_map/ppermute | solution.py:34
  16.1 72.7 %collective-permute-start.54 = (bf16[5,12,128,128]{3,2,1,0:T(8,128)(2,1)}, bf16[5,12,128,128]{3,2,1,0:T(8,128)(2,1)}, u32[]{:S(2)}, u32[]{:S(2)}) collective-permute-start(bf16[5,12,128,128]{3,2,1,0:T(8,128)(2,1)} %slice_bitcast_fusion.6), channel_id=1, source_target_pairs={{0,8},{8,16},{16,24},{1,9},{9,17},{17,25},{2,10},{10,18},{18,26},{... | collective-permute-start | bytes 5898248 | tf_op jit(solution)/shard_map/ppermute | solution.py:39
  19.5 8.8 %copy-start.3 = (bf16[1536,128]{1,0:T(8,128)(2,1)}, bf16[1536,128]{1,0:T(8,128)(2,1)S(1)}, u32[]{:S(2)}) copy-start(bf16[1536,128]{1,0:T(8,128)(2,1)S(1)} %collective-permute-done.34.refs_2_) | copy-start | bytes 1179652
  19.5 5.9 %collective-permute-start.38 = (bf16[768,128]{1,0:T(8,128)(2,1)S(1)}, bf16[768,128]{1,0:T(8,128)(2,1)S(1)}, u32[]{:S(2)}, u32[]{:S(2)}) collective-permute-start(bf16[768,128]{1,0:T(8,128)(2,1)S(1)} %slice.126), channel_id=1, source_target_pairs={{0,4},{1,5},{2,6},{3,7},{4,0},{5,1},{6,2},{7,3},{8,12},{9,13},{10,... | collective-permute-start | bytes 589832 | tf_op jit(solution)/shard_map/ppermute | solution.py:34
  21.1 7.2 %copy-start.4 = (bf16[1536,128]{1,0:T(8,128)(2,1)}, bf16[1536,128]{1,0:T(8,128)(2,1)S(1)}, u32[]{:S(2)}) copy-start(bf16[1536,128]{1,0:T(8,128)(2,1)S(1)} %collective-permute-done.36.refs_4_) | copy-start | bytes 1179652
  21.1 5.7 %collective-permute-start.39 = (bf16[768,128]{1,0:T(8,128)(2,1)S(1)}, bf16[768,128]{1,0:T(8,128)(2,1)S(1)}, u32[]{:S(2)}, u32[]{:S(2)}) collective-permute-start(bf16[768,128]{1,0:T(8,128)(2,1)S(1)} %slice.127), channel_id=1, source_target_pairs={{0,2},{1,3},{2,0},{3,1},{4,6},{5,7},{6,4},{7,5},{8,10},{9,11},{10,... | collective-permute-start | bytes 589832 | tf_op jit(solution)/shard_map/ppermute | solution.py:34
  22.7 5.6 %collective-permute-start.35 = (bf16[1536,128]{1,0:T(8,128)(2,1)S(1)}, bf16[1536,128]{1,0:T(8,128)(2,1)S(1)}, u32[]{:S(2)}, u32[]{:S(2)}) collective-permute-start(bf16[1536,128]{1,0:T(8,128)(2,1)S(1)} %collective-permute-done.34.refs_2_), channel_id=1, source_target_pairs={{0,1},{1,0},{2,3},{3,2},{4,5},{5,4},{6,7},{7,6},{8,9},{9,8},{10,11... | collective-permute-start | bytes 1179656 | tf_op jit(solution)/shard_map/ppermute | solution.py:34
  22.7 5.7 %copy-start.5 = (bf16[1536,128]{1,0:T(8,128)(2,1)}, bf16[1536,128]{1,0:T(8,128)(2,1)S(1)}, u32[]{:S(2)}) copy-start(bf16[1536,128]{1,0:T(8,128)(2,1)S(1)} %collective-permute-done.33.refs_1_) | copy-start | bytes 1179652
  22.7 5.6 %collective-permute-start.37 = (bf16[1536,128]{1,0:T(8,128)(2,1)S(1)}, bf16[1536,128]{1,0:T(8,128)(2,1)S(1)}, u32[]{:S(2)}, u32[]{:S(2)}) collective-permute-start(bf16[1536,128]{1,0:T(8,128)(2,1)S(1)} %collective-permute-done.36.refs_4_), channel_id=1, source_target_pairs={{0,1},{1,0},{2,3},{3,2},{4,5},{5,4},{6,7},{7,6},{8,9},{9,8},{10,11... | collective-permute-start | bytes 1179656 | tf_op jit(solution)/shard_map/ppermute | solution.py:34
  25.4 2.9 %copy-start.8 = (bf16[768,128]{1,0:T(8,128)(2,1)}, bf16[768,128]{1,0:T(8,128)(2,1)S(1)}, u32[]{:S(2)}) copy-start(bf16[768,128]{1,0:T(8,128)(2,1)S(1)} %collective-permute-done.38.refs_6_) | copy-start | bytes 589828
  25.4 1.6 %collective-permute-start.40 = (bf16[768,128]{1,0:T(8,128)(2,1)S(1)}, bf16[768,128]{1,0:T(8,128)(2,1)S(1)}, u32[]{:S(2)}, u32[]{:S(2)}) collective-permute-start(bf16[768,128]{1,0:T(8,128)(2,1)S(1)} %collective-permute-done.38.refs_6_), channel_id=1, source_target_pairs={{0,1},{1,0},{2,3},{3,2},{4,5},{5,4},{6,7},{7,6},{8,9},{9,8},{10,11... | collective-permute-start | bytes 589832 | tf_op jit(solution)/shard_map/ppermute | solution.py:34
  26.8 1.5 copy-start.9
  26.8 1.4 collective-permute-start.41
  27.0 1.3 copy-start.10
  28.3 0.8 copy-start.6
  28.3 0.9 copy-start.7
  41.1 47.6 %collective-permute-start.55 = (bf16[3,12,128,128]{3,2,1,0:T(8,128)(2,1)}, bf16[3,12,128,128]{3,2,1,0:T(8,128)(2,1)}, u32[]{:S(2)}, u32[]{:S(2)}) collective-permute-start(bf16[3,12,128,128]{3,2,1,0:T(8,128)(2,1)} %get-tuple-element.192), channel_id=1, source_target_pairs={{0,8},{8,16},{16,24},{1,9},{9,17},{17,25},{2,10},{10,18},{18,26},{... | collective-permute-start | bytes 3538952 | tf_op jit(solution)/shard_map/ppermute | solution.py:39
  43.4 11.0 %collective-permute-start.48 = (bf16[1552,128]{1,0:T(8,128)(2,1)S(1)}, bf16[1552,128]{1,0:T(8,128)(2,1)S(1)}, u32[]{:S(2)}, u32[]{:S(2)}) collective-permute-start(bf16[1552,128]{1,0:T(8,128)(2,1)S(1)} %get-tuple-element.184.refs_10_), channel_id=1, source_target_pairs={{0,4},{1,5},{2,6},{3,7},{4,0},{5,1},{6,2},{7,3},{8,12},{9,13},{10,... | collective-permute-start | bytes 1191944 | tf_op jit(solution)/shard_map/ppermute | solution.py:34
  44.7 11.3 %collective-permute-start.46 = (bf16[1552,128]{1,0:T(8,128)(2,1)S(1)}, bf16[1552,128]{1,0:T(8,128)(2,1)S(1)}, u32[]{:S(2)}, u32[]{:S(2)}) collective-permute-start(bf16[1552,128]{1,0:T(8,128)(2,1)S(1)} %get-tuple-element.184.refs_10_), channel_id=1, source_target_pairs={{0,2},{1,3},{2,0},{3,1},{4,6},{5,7},{6,4},{7,5},{8,10},{9,11},{10,... | collective-permute-start | bytes 1191944 | tf_op jit(solution)/shard_map/ppermute | solution.py:34
  45.5 11.1 %collective-permute-start.45 = (bf16[1552,128]{1,0:T(8,128)(2,1)S(1)}, bf16[1552,128]{1,0:T(8,128)(2,1)S(1)}, u32[]{:S(2)}, u32[]{:S(2)}) collective-permute-start(bf16[1552,128]{1,0:T(8,128)(2,1)S(1)} %get-tuple-element.184.refs_10_), channel_id=1, source_target_pairs={{0,1},{1,0},{2,3},{3,2},{4,5},{5,4},{6,7},{7,6},{8,9},{9,8},{10,11... | collective-permute-start | bytes 1191944 | tf_op jit(solution)/shard_map/ppermute | solution.py:34
  54.5 7.3 %collective-permute-start.51 = (bf16[784,128]{1,0:T(8,128)(2,1)S(1)}, bf16[784,128]{1,0:T(8,128)(2,1)S(1)}, u32[]{:S(2)}, u32[]{:S(2)}) collective-permute-start(bf16[784,128]{1,0:T(8,128)(2,1)S(1)} %slice.129), channel_id=1, source_target_pairs={{0,2},{1,3},{2,0},{3,1},{4,6},{5,7},{6,4},{7,5},{8,10},{9,11},{10,... | collective-permute-start | bytes 602120 | tf_op jit(solution)/shard_map/ppermute | solution.py:34
  56.1 5.7 %collective-permute-start.50 = (bf16[768,128]{1,0:T(8,128)(2,1)S(1)}, bf16[768,128]{1,0:T(8,128)(2,1)S(1)}, u32[]{:S(2)}, u32[]{:S(2)}) collective-permute-start(bf16[768,128]{1,0:T(8,128)(2,1)S(1)} %slice.128), channel_id=1, source_target_pairs={{0,4},{1,5},{2,6},{3,7},{4,0},{5,1},{6,2},{7,3},{8,12},{9,13},{10,... | collective-permute-start | bytes 589832 | tf_op jit(solution)/shard_map/ppermute | solution.py:34
  56.6 7.3 %collective-permute-start.47 = (bf16[1552,128]{1,0:T(8,128)(2,1)S(1)}, bf16[1552,128]{1,0:T(8,128)(2,1)S(1)}, u32[]{:S(2)}, u32[]{:S(2)}) collective-permute-start(bf16[1552,128]{1,0:T(8,128)(2,1)S(1)} %collective-permute-done.46.refs_12_), channel_id=1, source_target_pairs={{0,1},{1,0},{2,3},{3,2},{4,5},{5,4},{6,7},{7,6},{8,9},{9,8},{10,11... | collective-permute-start | bytes 1191944 | tf_op jit(solution)/shard_map/ppermute | solution.py:34
  61.8 2.2 %collective-permute-start.49 = (bf16[1552,128]{1,0:T(8,128)(2,1)S(1)}, bf16[1552,128]{1,0:T(8,128)(2,1)S(1)}, u32[]{:S(2)}, u32[]{:S(2)}) collective-permute-start(bf16[1552,128]{1,0:T(8,128)(2,1)S(1)} %collective-permute-done.48.refs_14_), channel_id=1, source_target_pairs={{0,1},{1,0},{2,3},{3,2},{4,5},{5,4},{6,7},{7,6},{8,9},{9,8},{10,11... | collective-permute-start | bytes 1191944 | tf_op jit(solution)/shard_map/ppermute | solution.py:34
  61.8 2.0 %collective-permute-start.52 = (bf16[768,128]{1,0:T(8,128)(2,1)S(1)}, bf16[768,128]{1,0:T(8,128)(2,1)S(1)}, u32[]{:S(2)}, u32[]{:S(2)}) collective-permute-start(bf16[768,128]{1,0:T(8,128)(2,1)S(1)} %collective-permute-done.50.refs_16_), channel_id=1, source_target_pairs={{0,1},{1,0},{2,3},{3,2},{4,5},{5,4},{6,7},{7,6},{8,9},{9,8},{10,11... | collective-permute-start | bytes 589832 | tf_op jit(solution)/shard_map/ppermute | solution.py:34
  63.8 1.4 collective-permute-start.53
  63.9 24.9 %copy-start.1 = (f32[12,128,128]{2,1,0:T(8,128)S(1)}, f32[12,128,128]{2,1,0:T(8,128)}, u32[]{:S(2)}) copy-start(f32[12,128,128]{2,1,0:T(8,128)} %get-tuple-element.189) | copy-start | bytes 2359300
  63.9 24.9 %copy-start.14 = (s32[1,12]{1,0:T(1,128)S(1)}, s32[1,12]{1,0:T(1,128)}, u32[]{:S(2)}) copy-start(s32[1,12]{1,0:T(1,128)} %param.14) | copy-start | bytes 148
  89.6 12.6 %collective-permute-start = (bf16[1536,128]{1,0:T(8,128)(2,1)S(1)}, bf16[1536,128]{1,0:T(8,128)(2,1)S(1)}, u32[]{:S(2)}, u32[]{:S(2)}) collective-permute-start(bf16[1536,128]{1,0:T(8,128)(2,1)S(1)} %get-tuple-element.118), channel_id=1, source_target_pairs={{0,8},{8,16},{16,24},{1,9},{9,17},{17,25},{2,10},{10,18},{18,26},{... | collective-permute-start | bytes 1179656 | tf_op jit(solution)/shard_map/cond/branch_0_fun/ppermute | solution.py:39
  102.2 47.8 %collective-permute-start.2 = (bf16[8112,128]{1,0:T(8,128)(2,1)S(1)}, bf16[8112,128]{1,0:T(8,128)(2,1)S(1)}, u32[]{:S(2)}, u32[]{:S(2)}) collective-permute-start(bf16[8112,128]{1,0:T(8,128)(2,1)S(1)} %pack_update.3), channel_id=1, source_target_pairs={{0,8},{8,16},{16,24},{1,9},{9,17},{17,25},{2,10},{10,18},{18,26},{... | collective-permute-start | bytes 6230024 | tf_op jit(solution)/shard_map/cond/branch_0_fun/ppermute | solution.py:39
  104.6 9.8 %collective-permute-start.1 = (bf16[1536,128]{1,0:T(8,128)(2,1)S(1)}, bf16[1536,128]{1,0:T(8,128)(2,1)S(1)}, u32[]{:S(2)}, u32[]{:S(2)}) collective-permute-start(bf16[1536,128]{1,0:T(8,128)(2,1)S(1)} %collective-permute-done.refs_0_), channel_id=1, source_target_pairs={{0,2},{1,3},{2,0},{3,1},{4,6},{5,7},{6,4},{7,5},{8,10},{9,11},{10,... | collective-permute-start | bytes 1179656 | tf_op jit(solution)/shard_map/cond/branch_0_fun/ppermute | solution.py:34
  105.5 9.8 %collective-permute-start.5 = (bf16[1536,128]{1,0:T(8,128)(2,1)S(1)}, bf16[1536,128]{1,0:T(8,128)(2,1)S(1)}, u32[]{:S(2)}, u32[]{:S(2)}) collective-permute-start(bf16[1536,128]{1,0:T(8,128)(2,1)S(1)} %collective-permute-done.refs_0_), channel_id=1, source_target_pairs={{0,4},{1,5},{2,6},{3,7},{4,0},{5,1},{6,2},{7,3},{8,12},{9,13},{10,... | collective-permute-start | bytes 1179656 | tf_op jit(solution)/shard_map/cond/branch_0_fun/ppermute | solution.py:34
  106.1 12.1 %collective-permute-start.3 = (bf16[1536,128]{1,0:T(8,128)(2,1)S(1)}, bf16[1536,128]{1,0:T(8,128)(2,1)S(1)}, u32[]{:S(2)}, u32[]{:S(2)}) collective-permute-start(bf16[1536,128]{1,0:T(8,128)(2,1)S(1)} %collective-permute-done.refs_0_), channel_id=1, source_target_pairs={{0,1},{1,0},{2,3},{3,2},{4,5},{5,4},{6,7},{7,6},{8,9},{9,8},{10,11... | collective-permute-start | bytes 1179656 | tf_op jit(solution)/shard_map/cond/branch_0_fun/ppermute | solution.py:34
  115.4 5.7 %collective-permute-start.8 = (bf16[768,128]{1,0:T(8,128)(2,1)S(1)}, bf16[768,128]{1,0:T(8,128)(2,1)S(1)}, u32[]{:S(2)}, u32[]{:S(2)}) collective-permute-start(bf16[768,128]{1,0:T(8,128)(2,1)S(1)} %slice.121), channel_id=1, source_target_pairs={{0,2},{1,3},{2,0},{3,1},{4,6},{5,7},{6,4},{7,5},{8,10},{9,11},{10,... | collective-permute-start | bytes 589832 | tf_op jit(solution)/shard_map/cond/branch_0_fun/ppermute | solution.py:34
  116.2 5.7 %collective-permute-start.7 = (bf16[768,128]{1,0:T(8,128)(2,1)S(1)}, bf16[768,128]{1,0:T(8,128)(2,1)S(1)}, u32[]{:S(2)}, u32[]{:S(2)}) collective-permute-start(bf16[768,128]{1,0:T(8,128)(2,1)S(1)} %slice.120), channel_id=1, source_target_pairs={{0,4},{1,5},{2,6},{3,7},{4,0},{5,1},{6,2},{7,3},{8,12},{9,13},{10,... | collective-permute-start | bytes 589832 | tf_op jit(solution)/shard_map/cond/branch_0_fun/ppermute | solution.py:34
  117.6 5.8 %collective-permute-start.4 = (bf16[1536,128]{1,0:T(8,128)(2,1)S(1)}, bf16[1536,128]{1,0:T(8,128)(2,1)S(1)}, u32[]{:S(2)}, u32[]{:S(2)}) collective-permute-start(bf16[1536,128]{1,0:T(8,128)(2,1)S(1)} %collective-permute-done.1.refs_2_), channel_id=1, source_target_pairs={{0,1},{1,0},{2,3},{3,2},{4,5},{5,4},{6,7},{7,6},{8,9},{9,8},{10,11... | collective-permute-start | bytes 1179656 | tf_op jit(solution)/shard_map/cond/branch_0_fun/ppermute | solution.py:34
  118.1 5.3 %collective-permute-start.6 = (bf16[1536,128]{1,0:T(8,128)(2,1)S(1)}, bf16[1536,128]{1,0:T(8,128)(2,1)S(1)}, u32[]{:S(2)}, u32[]{:S(2)}) collective-permute-start(bf16[1536,128]{1,0:T(8,128)(2,1)S(1)} %collective-permute-done.5.refs_4_), channel_id=1, source_target_pairs={{0,1},{1,0},{2,3},{3,2},{4,5},{5,4},{6,7},{7,6},{8,9},{9,8},{10,11... | collective-permute-start | bytes 1179656 | tf_op jit(solution)/shard_map/cond/branch_0_fun/ppermute | solution.py:34
  121.1 2.3 %collective-permute-start.10 = (bf16[768,128]{1,0:T(8,128)(2,1)S(1)}, bf16[768,128]{1,0:T(8,128)(2,1)S(1)}, u32[]{:S(2)}, u32[]{:S(2)}) collective-permute-start(bf16[768,128]{1,0:T(8,128)(2,1)S(1)} %collective-permute-done.8.refs_7_), channel_id=1, source_target_pairs={{0,1},{1,0},{2,3},{3,2},{4,5},{5,4},{6,7},{7,6},{8,9},{9,8},{10,11... | collective-permute-start | bytes 589832 | tf_op jit(solution)/shard_map/cond/branch_0_fun/ppermute | solution.py:34
  122.0 1.5 collective-permute-start.9
  154.6 0.9 copy-start.13
  (2 other events, 1.4 us)

commit v2 on v1

--- a/solution.py
+++ b/solution.py
@@ -10,7 +10,7 @@
 GROUPS = 5
 EXTRA = 16
 SLACK = 128
-HAM_STEP = 4
+HAM_STEP = 6
 PACK_STEP = 2
 UNPACK_STEP = 2
 EARLY_STEP = 1
@@ -568,10 +568,12 @@
     both = jnp.stack([jnp.minimum(dims[:, 1], ranks), offsets]).astype(F32)
     zero = jnp.zeros((), jnp.int32)
     own_lanes = lax.dynamic_update_slice(jnp.zeros((8, 128), F32), both, (zero, (count * sec).astype(jnp.int32)))
+    vpieces = gathered(vzero.reshape((body, width)))
+    own_lanes, one = lax.optimization_barrier((own_lanes, vpieces[1][0]))
+    vpieces[1] = (one, *vpieces[1][1:])
     table = own_lanes
     for shift in range(1, secs):
         table = table + lax.ppermute(own_lanes, "sec", [(i, (i + shift) % secs) for i in range(secs)])
-    vpieces = gathered(vzero.reshape((body, width)))
     sent_one, table = lax.optimization_barrier((lenv[: len(at_once)], table))
     sent_one = onward(sent_one)
     places = tuple((place, first) for _, place, first in vpieces)

time: 158 us -> 160 us (1.013); the launches traced: 155 us -> 161 us
  waiting for transfers between devices: 53.6 us -> 58.5 us
    ppermute x4, waiting for transfers between devices: 19 us -> 24.6 us  [onward(): return lax.ppermute(value, 'sec', [(i, i + 1) for i in range(length - 1)])]
    ppermute x4, starting transfers between devices: 8.78 us -> 11.4 us  [onward(): return lax.ppermute(value, 'sec', [(i, i + 1) for i in range(length - 1)])]
    ppermute x27, starting transfers between devices: 15.7 us -> 14 us  [exchange(): return lax.ppermute(value, 'blk', [(i, i ^ bit) for i in range(length)])]
  transfers between devices with their start and end apart: 34 -> 34, of which waited for: 15 -> 15; matrix products, arithmetic and copies ran while one was open for 6% -> 6% of each run, Pallas kernels for 28% -> 27%
where the time goes in v2:
time: 160 us; the launch traced here: 161 us
  waiting for transfers between devices  58.5 us (37%)
  Pallas kernels  49.1 us (31%)
  starting transfers between devices  30.1 us (19%)
  blocking collectives  8.46 us (5%)
  local copies, waits for them, and re-layouts  7.3 us (5%)
  other arithmetic  5.71 us (4%)
    ppermute x27, waiting for transfers between devices, exchange(): return lax.ppermute(value, 'blk', [(i, i ^ bit) for i in range(length)])  33.8 us
    ppermute x4, waiting for transfers between devices, onward(): return lax.ppermute(value, 'sec', [(i, i + 1) for i in range(length - 1)])  24.6 us
    ppermute x27, starting transfers between devices, exchange(): return lax.ppermute(value, 'blk', [(i, i ^ bit) for i in range(length)])  14 us
    pallas_call x1, Pallas kernels, shards(): call(functools.partial(second_kernel, places, count, cells, secs, late, u...  12.6 us
    pallas_call x1, Pallas kernels, shards(): call(functools.partial(first_kernel, places, count, then), 'ham_first', [...  12 us
    ppermute x4, starting transfers between devices, onward(): return lax.ppermute(value, 'sec', [(i, i + 1) for i in range(length - 1)])  11.4 us
    pallas_call x1, Pallas kernels, branch(): call(functools.partial(early_kernel, places, count, early), 'early_update...  11.2 us
    all_gather x1, blocking collectives, shards(): parts = lax.all_gather(sums, 'blk', axis=0)  8.46 us
  transfers between devices with their start and end apart: 34, of which 15 were waited for; matrix products, arithmetic and copies ran while one was open for 6% of the time, Pallas kernels for 27%

profile of v2, /device:TPU:8, one launch (start us, length us, event | category | flops | bytes accessed | tf_op | source)
XLA Modules:
  0.0 161.0 jit_solution(5835635838297775895)
XLA Ops:
  0.6 0.8 slice_bitcast_fusion.8
  1.5 1.3 fusion.3.refs_0_
  2.9 1.6 collective-permute-start.34
  4.5 1.5 collective-permute-start.36
  6.0 0.7 bitcast_minimum_fusion
  6.7 0.7 add_convert_fusion.3
  7.9 1.6 %collective-permute-start.42 = (f32[8,128]{1,0:T(8,128)S(1)}, f32[8,128]{1,0:T(8,128)S(1)}, u32[]{:S(2)}, u32[]{:S(2)}) collective-permute-start(f32[8,128]{1,0:T(8,128)S(1)} %dynamic_update_slice.3), channel_id=1, source_target_pairs={{0,8},{8,16},{16,24},{24,0},{1,9},{9,17},{17,25},{25,1},{2,10},{10... | collective-permute-start | bytes 12296 | tf_op jit(solution)/shard_map/ppermute | solution.py:576
  9.5 1.1 collective-permute-start.43
  10.6 1.9 %collective-permute-start.44 = (f32[8,128]{1,0:T(8,128)S(1)}, f32[8,128]{1,0:T(8,128)S(1)}, u32[]{:S(2)}, u32[]{:S(2)}) collective-permute-start(f32[8,128]{1,0:T(8,128)S(1)} %dynamic_update_slice.3), channel_id=1, source_target_pairs={{0,24},{8,0},{16,8},{24,16},{1,25},{9,1},{17,9},{25,17},{2,26},{10... | collective-permute-start | bytes 12296 | tf_op jit(solution)/shard_map/ppermute | solution.py:576
  12.6 3.0 %slice_bitcast_fusion.6 = bf16[5,12,128,128]{3,2,1,0:T(8,128)(2,1)} fusion(bf16[1,20,12,128,128]{4,3,2,1,0:T(8,128)(2,1)} %param.10), kind=kLoop, calls=%fused_computation.15 | loop fusion | bytes 3932160 | tf_op jit(solution)/shard_map/slice | solution.py:577
  15.6 2.0 %collective-permute-start.54 = (bf16[5,12,128,128]{3,2,1,0:T(8,128)(2,1)}, bf16[5,12,128,128]{3,2,1,0:T(8,128)(2,1)}, u32[]{:S(2)}, u32[]{:S(2)}) collective-permute-start(bf16[5,12,128,128]{3,2,1,0:T(8,128)(2,1)} %slice_bitcast_fusion.6), channel_id=1, source_target_pairs={{0,8},{8,16},{16,24},{1,9},{9,17},{17,25},{2,10},{10,18},{18,26},{... | collective-permute-start | bytes 5898248 | tf_op jit(solution)/shard_map/ppermute | solution.py:39
  17.7 0.6 collective-permute-start.38
  18.3 0.6 collective-permute-start.39
  19.4 4.2 %collective-permute-done.38.refs_6_ = bf16[768,128]{1,0:T(8,128)(2,1)S(1)} collective-permute-done((bf16[768,128]{1,0:T(8,128)(2,1)S(1)}, bf16[768,128]{1,0:T(8,128)(2,1)S(1)}, u32[]{:S(2)}, u32[]{:S(2)}) %collective-permute-start.38) | collective-permute-done | bytes 196640 | tf_op jit(solution)/shard_map/ppermute | solution.py:34
  24.3 0.8 collective-permute-done.40.refs_8_
  26.4 12.0 %ham_first.1 = (f32[12,128,128]{2,1,0:T(8,128)}, bf16[1552,128]{1,0:T(8,128)(2,1)S(1)}, bf16[3,12,128,128]{3,2,1,0:T(8,128)(2,1)}) custom-call(s32[12]{0:T(128)S(1)} %bitcast.63, s32[2]{0:T(128)S(1)} %pad_add_fusion.device, s32[12,2]{1,0:T(8,128)S(1)} %copy.14.dims, f32[8,128]{1,0:T(8,128)S(1)} %add_add_fusion.table, bf16[1536,128]{1,0:T(8,128)(2,1)} %copy-done.2, ...), custom_call_target="tpu_custom_call" | custom-call | flops 1 | bytes 1 | tf_op jit(solution)/shard_map/ham_first/pallas_call | solution.py:610
  38.5 4.6 %collective-permute-start.55 = (bf16[3,12,128,128]{3,2,1,0:T(8,128)(2,1)}, bf16[3,12,128,128]{3,2,1,0:T(8,128)(2,1)}, u32[]{:S(2)}, u32[]{:S(2)}) collective-permute-start(bf16[3,12,128,128]{3,2,1,0:T(8,128)(2,1)} %get-tuple-element.196), channel_id=1, source_target_pairs={{0,8},{8,16},{16,24},{1,9},{9,17},{17,25},{2,10},{10,18},{18,26},{... | collective-permute-start | bytes 3538952 | tf_op jit(solution)/shard_map/ppermute | solution.py:39
  43.1 1.6 collective-permute-start.48
  44.7 0.5 collective-permute-start.46
  45.2 8.9 %collective-permute-done.48.refs_14_ = bf16[1552,128]{1,0:T(8,128)(2,1)S(1)} collective-permute-done((bf16[1552,128]{1,0:T(8,128)(2,1)S(1)}, bf16[1552,128]{1,0:T(8,128)(2,1)S(1)}, u32[]{:S(2)}, u32[]{:S(2)}) %collective-permute-start.48) | collective-permute-done | bytes 397344 | tf_op jit(solution)/shard_map/ppermute | solution.py:34
  54.1 0.6 collective-permute-start.51
  54.7 0.6 collective-permute-done.46.refs_12_
  55.4 1.0 collective-permute-start.50
  56.3 4.8 %collective-permute-done.50.refs_16_ = bf16[768,128]{1,0:T(8,128)(2,1)S(1)} collective-permute-done((bf16[768,128]{1,0:T(8,128)(2,1)S(1)}, bf16[768,128]{1,0:T(8,128)(2,1)S(1)}, u32[]{:S(2)}, u32[]{:S(2)}) %collective-permute-start.50) | collective-permute-done | bytes 196640 | tf_op jit(solution)/shard_map/ppermute | solution.py:34
  61.6 1.5 collective-permute-done.52.refs_18_
  63.3 1.3 collective-permute-done.53.refs_19_
  64.6 12.6 %ham_second.1 = (f32[12,128,128]{2,1,0:T(8,128)S(1)}, f32[8,128]{1,0:T(8,128)S(1)}, s32[2,8,128]{2,1,0:T(8,128)S(1)}, bf16[5,12,128,128]{3,2,1,0:T(8,128)(2,1)S(1)}, bf16[5,12,128,128]{3,2,1,0:T(8,128)(2,1)S(1)}) custom-call(s32[12]{0:T(128)S(1)} %bitcast.64, s32[2]{0:T(128)S(1)} %pad_add_fusion.device, s32[12,2]{1,0:T(8,128)S(1)} %copy.14.dims, ...), custom_call_target="tpu_custom_call" | custom-call | flops 1 | bytes 1 | tf_op jit(solution)/shard_map/ham_second/pallas_call | solution.py:620
  78.3 8.5 %all-gather = f32[64,128]{1,0:T(8,128)S(1)} all-gather(f32[8,128]{1,0:T(8,128)S(1)} %get-tuple-element.189), channel_id=2, replica_groups=mesh['sec'=4,'blk'=8] {'blk'}, dimensions={0}, use_global_device_ids=true | all-gather | bytes 36864 | tf_op jit(solution)/shard_map/all_gather | solution.py:633
  86.9 73.2 %conditional.4 = (bf16[1,12,128,128]{3,2,1,0:T(8,128)(2,1)S(1)}, f32[1]{0:T(128)}, bf16[1,20,12,128,128]{4,3,2,1,0:T(8,128)(2,1)}, bf16[1,12,128,128]{3,2,1,0:T(8,128)(2,1)S(1)}) conditional(s32[]{:T(128)} %bitcast.43, (s32[2,8,128]{2,1,0:T(8,128)S(1)}, s32[1,12]{1,0:T(1,128)S(1)}, f32[8,8,128]{2,1,0:T(8,128)S(1)}, ...), branch_computations={%region_0.1_spmd, %region_1.2_spmd, %region_2.3_spmd} | conditional | flops 1966084 | bytes 56508928
  87.1 0.8 ritz.4
  87.9 2.3 %collective-permute-start.11 = (bf16[1536,128]{1,0:T(8,128)(2,1)S(1)}, bf16[1536,128]{1,0:T(8,128)(2,1)S(1)}, u32[]{:S(2)}, u32[]{:S(2)}) collective-permute-start(bf16[1536,128]{1,0:T(8,128)(2,1)S(1)} %get-tuple-element.136), channel_id=1, source_target_pairs={{0,8},{8,16},{16,24},{1,9},{9,17},{17,25},{2,10},{10,18},{18,26},{... | collective-permute-start | bytes 1179656 | tf_op jit(solution)/shard_map/cond/branch_1_fun/ppermute | solution.py:39
  90.3 8.2 %pack_update.4 = bf16[9280,128]{1,0:T(8,128)(2,1)S(1)} custom-call(s32[8,128]{1,0:T(8,128)S(1)} %get-tuple-element.213.table, f32[8,128]{1,0:T(8,128)S(1)} %get-tuple-element.138.coefs, bf16[5,12,128,128]{3,2,1,0:T(8,128)(2,1)S(1)} %get-tuple-element.132.vsrc, bf16[5,12,128,128]{3,2,1,0:T(8,128)(2,1)S(1)} %get-tuple-element.133.wsrc, ...), custom_call_target="tpu_custom_call" | custom-call | flops 1 | bytes 20971520 | tf_op jit(solution)/shard_map/cond/branch_1_fun/pack_update/pallas_call | solution.py:651
  98.5 2.6 %collective-permute-done.11.refs_0_ = bf16[1536,128]{1,0:T(8,128)(2,1)S(1)} collective-permute-done((bf16[1536,128]{1,0:T(8,128)(2,1)S(1)}, bf16[1536,128]{1,0:T(8,128)(2,1)S(1)}, u32[]{:S(2)}, u32[]{:S(2)}) %collective-permute-start.11) | collective-permute-done | bytes 393248 | tf_op jit(solution)/shard_map/cond/branch_1_fun/ppermute | solution.py:39
  101.0 2.4 %collective-permute-start.13 = (bf16[9280,128]{1,0:T(8,128)(2,1)S(1)}, bf16[9280,128]{1,0:T(8,128)(2,1)S(1)}, u32[]{:S(2)}, u32[]{:S(2)}) collective-permute-start(bf16[9280,128]{1,0:T(8,128)(2,1)S(1)} %pack_update.4), channel_id=1, source_target_pairs={{0,8},{8,16},{16,24},{1,9},{9,17},{17,25},{2,10},{10,18},{18,26},{... | collective-permute-start | bytes 7127048 | tf_op jit(solution)/shard_map/cond/branch_1_fun/ppermute | solution.py:39
  103.5 1.6 collective-permute-start.12
  105.1 0.5 collective-permute-start.16
  105.6 8.2 %collective-permute-done.12.refs_2_ = bf16[1536,128]{1,0:T(8,128)(2,1)S(1)} collective-permute-done((bf16[1536,128]{1,0:T(8,128)(2,1)S(1)}, bf16[1536,128]{1,0:T(8,128)(2,1)S(1)}, u32[]{:S(2)}, u32[]{:S(2)}) %collective-permute-start.12) | collective-permute-done | bytes 393248 | tf_op jit(solution)/shard_map/cond/branch_1_fun/ppermute | solution.py:34
  113.8 1.6 collective-permute-start.18
  115.4 0.6 collective-permute-start.19
  116.0 0.5 fusion.6
  117.0 1.4 fusion.1
  118.5 1.1 collective-permute-done.18.refs_6_
  119.6 1.6 collective-permute-done.19.refs_7_
  121.2 1.4 multiply_add_fusion.1
  122.7 11.2 %early_update.4.so_far = bf16[4,5,12,128,128]{4,3,2,1,0:T(8,128)(2,1)} custom-call(s32[8,128]{1,0:T(8,128)S(1)} %get-tuple-element.212.table, s32[2]{0:T(128)S(1)} %get-tuple-element.143.device, s32[1]{0:T(128)} %bitcast.18.first_sec, bf16[1536,128]{1,0:T(8,128)(2,1)S(1)} %collective-permute-done.11.refs_0_, ...), custom_call_target="tpu_custom_call" | custom-call | flops 1 | bytes 1 | tf_op jit(solution)/shard_map/cond/branch_1_fun/early_update/pallas_call | solution.py:672
  133.9 21.9 %collective-permute-done.13.packed = bf16[9280,128]{1,0:T(8,128)(2,1)S(1)} collective-permute-done((bf16[9280,128]{1,0:T(8,128)(2,1)S(1)}, bf16[9280,128]{1,0:T(8,128)(2,1)S(1)}, u32[]{:S(2)}, u32[]{:S(2)}) %collective-permute-start.13) | collective-permute-done | bytes 2375712 | tf_op jit(solution)/shard_map/cond/branch_1_fun/ppermute | solution.py:39
  155.8 4.3 %unpack_update.4 = bf16[4,5,12,128,128]{4,3,2,1,0:T(8,128)(2,1)} custom-call(s32[8,128]{1,0:T(8,128)S(1)} %get-tuple-element.212.table, s32[1]{0:T(128)} %bitcast.18.first_sec, bf16[9280,128]{1,0:T(8,128)(2,1)S(1)} %collective-permute-done.13.packed, bf16[4,5,12,128,128]{4,3,2,1,0:T(8,128)(2,1)} %bitcast.72, ...), custom_call_target="tpu_custom_call", output_to_operand_aliasing={{}: (4, {})} | custom-call | flops 1 | bytes 1 | tf_op jit(solution)/shard_map/cond/branch_1_fun/unpack_update/pallas_call | solution.py:687
  160.1 0.7 copy-done.12
  (83 shorter events, 5.3 us)
Async XLA Ops:
  2.8 14.9 %copy-start.2 = (bf16[1536,128]{1,0:T(8,128)(2,1)}, bf16[1536,128]{1,0:T(8,128)(2,1)S(1)}, u32[]{:S(2)}) copy-start(bf16[1536,128]{1,0:T(8,128)(2,1)S(1)} %fusion.3.refs_0_) | copy-start | bytes 1179652
  2.8 5.0 %collective-permute-start.33 = (bf16[1536,128]{1,0:T(8,128)(2,1)S(1)}, bf16[1536,128]{1,0:T(8,128)(2,1)S(1)}, u32[]{:S(2)}, u32[]{:S(2)}) collective-permute-start(bf16[1536,128]{1,0:T(8,128)(2,1)S(1)} %fusion.3.refs_0_), channel_id=1, source_target_pairs={{0,1},{1,0},{2,3},{3,2},{4,5},{5,4},{6,7},{7,6},{8,9},{9,8},{10,11... | collective-permute-start | bytes 1179656 | tf_op jit(solution)/shard_map/ppermute | solution.py:34
  2.9 14.7 %collective-permute-start.34 = (bf16[1536,128]{1,0:T(8,128)(2,1)S(1)}, bf16[1536,128]{1,0:T(8,128)(2,1)S(1)}, u32[]{:S(2)}, u32[]{:S(2)}) collective-permute-start(bf16[1536,128]{1,0:T(8,128)(2,1)S(1)} %fusion.3.refs_0_), channel_id=1, source_target_pairs={{0,2},{1,3},{2,0},{3,1},{4,6},{5,7},{6,4},{7,5},{8,10},{9,11},{10,... | collective-permute-start | bytes 1179656 | tf_op jit(solution)/shard_map/ppermute | solution.py:34
  4.5 13.8 %collective-permute-start.36 = (bf16[1536,128]{1,0:T(8,128)(2,1)S(1)}, bf16[1536,128]{1,0:T(8,128)(2,1)S(1)}, u32[]{:S(2)}, u32[]{:S(2)}) collective-permute-start(bf16[1536,128]{1,0:T(8,128)(2,1)S(1)} %fusion.3.refs_0_), channel_id=1, source_target_pairs={{0,4},{1,5},{2,6},{3,7},{4,0},{5,1},{6,2},{7,3},{8,12},{9,13},{10,... | collective-permute-start | bytes 1179656 | tf_op jit(solution)/shard_map/ppermute | solution.py:34
  7.8 16.3 %copy-start.15 = (s32[1,12,2]{1,2,0:T(2,128)S(1)}, s32[1,12,2]{1,2,0:T(2,128)}, u32[]{:S(2)}) copy-start(s32[1,12,2]{1,2,0:T(2,128)} %param.13) | copy-start | bytes 292
  7.9 18.5 %copy-start = (s32[1,12]{1,0:T(1,128)S(1)}, s32[1,12]{1,0:T(1,128)}, u32[]{:S(2)}) copy-start(s32[1,12]{1,0:T(1,128)} %param.12) | copy-start | bytes 148
  7.9 9.8 %copy-start.5 = (bf16[1536,128]{1,0:T(8,128)(2,1)}, bf16[1536,128]{1,0:T(8,128)(2,1)S(1)}, u32[]{:S(2)}) copy-start(bf16[1536,128]{1,0:T(8,128)(2,1)S(1)} %collective-permute-done.33.refs_1_) | copy-start | bytes 1179652
  7.9 7.7 %collective-permute-start.42 = (f32[8,128]{1,0:T(8,128)S(1)}, f32[8,128]{1,0:T(8,128)S(1)}, u32[]{:S(2)}, u32[]{:S(2)}) collective-permute-start(f32[8,128]{1,0:T(8,128)S(1)} %dynamic_update_slice.3), channel_id=1, source_target_pairs={{0,8},{8,16},{16,24},{24,0},{1,9},{9,17},{17,25},{25,1},{2,10},{10... | collective-permute-start | bytes 12296 | tf_op jit(solution)/shard_map/ppermute | solution.py:576
  9.5 6.1 %collective-permute-start.43 = (f32[8,128]{1,0:T(8,128)S(1)}, f32[8,128]{1,0:T(8,128)S(1)}, u32[]{:S(2)}, u32[]{:S(2)}) collective-permute-start(f32[8,128]{1,0:T(8,128)S(1)} %dynamic_update_slice.3), channel_id=1, source_target_pairs={{0,16},{8,24},{16,0},{24,8},{1,17},{9,25},{17,1},{25,9},{2,18},{10... | collective-permute-start | bytes 12296 | tf_op jit(solution)/shard_map/ppermute | solution.py:576
  10.6 5.0 %collective-permute-start.44 = (f32[8,128]{1,0:T(8,128)S(1)}, f32[8,128]{1,0:T(8,128)S(1)}, u32[]{:S(2)}, u32[]{:S(2)}) collective-permute-start(f32[8,128]{1,0:T(8,128)S(1)} %dynamic_update_slice.3), channel_id=1, source_target_pairs={{0,24},{8,0},{16,8},{24,16},{1,25},{9,1},{17,9},{25,17},{2,26},{10... | collective-permute-start | bytes 12296 | tf_op jit(solution)/shard_map/ppermute | solution.py:576
  15.6 71.3 %collective-permute-start.54 = (bf16[5,12,128,128]{3,2,1,0:T(8,128)(2,1)}, bf16[5,12,128,128]{3,2,1,0:T(8,128)(2,1)}, u32[]{:S(2)}, u32[]{:S(2)}) collective-permute-start(bf16[5,12,128,128]{3,2,1,0:T(8,128)(2,1)} %slice_bitcast_fusion.6), channel_id=1, source_target_pairs={{0,8},{8,16},{16,24},{1,9},{9,17},{17,25},{2,10},{10,18},{18,26},{... | collective-permute-start | bytes 5898248 | tf_op jit(solution)/shard_map/ppermute | solution.py:39
  17.6 7.9 %copy-start.3 = (bf16[1536,128]{1,0:T(8,128)(2,1)}, bf16[1536,128]{1,0:T(8,128)(2,1)S(1)}, u32[]{:S(2)}) copy-start(bf16[1536,128]{1,0:T(8,128)(2,1)S(1)} %collective-permute-done.34.refs_2_) | copy-start | bytes 1179652
  17.7 5.9 %collective-permute-start.38 = (bf16[768,128]{1,0:T(8,128)(2,1)S(1)}, bf16[768,128]{1,0:T(8,128)(2,1)S(1)}, u32[]{:S(2)}, u32[]{:S(2)}) collective-permute-start(bf16[768,128]{1,0:T(8,128)(2,1)S(1)} %slice.126), channel_id=1, source_target_pairs={{0,4},{1,5},{2,6},{3,7},{4,0},{5,1},{6,2},{7,3},{8,12},{9,13},{10,... | collective-permute-start | bytes 589832 | tf_op jit(solution)/shard_map/ppermute | solution.py:34
  18.3 7.2 %copy-start.4 = (bf16[1536,128]{1,0:T(8,128)(2,1)}, bf16[1536,128]{1,0:T(8,128)(2,1)S(1)}, u32[]{:S(2)}) copy-start(bf16[1536,128]{1,0:T(8,128)(2,1)S(1)} %collective-permute-done.36.refs_4_) | copy-start | bytes 1179652
  18.3 5.7 %collective-permute-start.39 = (bf16[768,128]{1,0:T(8,128)(2,1)S(1)}, bf16[768,128]{1,0:T(8,128)(2,1)S(1)}, u32[]{:S(2)}, u32[]{:S(2)}) collective-permute-start(bf16[768,128]{1,0:T(8,128)(2,1)S(1)} %slice.127), channel_id=1, source_target_pairs={{0,2},{1,3},{2,0},{3,1},{4,6},{5,7},{6,4},{7,5},{8,10},{9,11},{10,... | collective-permute-start | bytes 589832 | tf_op jit(solution)/shard_map/ppermute | solution.py:34
  18.9 6.6 %collective-permute-start.35 = (bf16[1536,128]{1,0:T(8,128)(2,1)S(1)}, bf16[1536,128]{1,0:T(8,128)(2,1)S(1)}, u32[]{:S(2)}, u32[]{:S(2)}) collective-permute-start(bf16[1536,128]{1,0:T(8,128)(2,1)S(1)} %collective-permute-done.34.refs_2_), channel_id=1, source_target_pairs={{0,1},{1,0},{2,3},{3,2},{4,5},{5,4},{6,7},{7,6},{8,9},{9,8},{10,11... | collective-permute-start | bytes 1179656 | tf_op jit(solution)/shard_map/ppermute | solution.py:34
  18.9 6.6 %collective-permute-start.37 = (bf16[1536,128]{1,0:T(8,128)(2,1)S(1)}, bf16[1536,128]{1,0:T(8,128)(2,1)S(1)}, u32[]{:S(2)}, u32[]{:S(2)}) collective-permute-start(bf16[1536,128]{1,0:T(8,128)(2,1)S(1)} %collective-permute-done.36.refs_4_), channel_id=1, source_target_pairs={{0,1},{1,0},{2,3},{3,2},{4,5},{5,4},{6,7},{7,6},{8,9},{9,8},{10,11... | collective-permute-start | bytes 1179656 | tf_op jit(solution)/shard_map/ppermute | solution.py:34
  23.6 1.9 %copy-start.8 = (bf16[768,128]{1,0:T(8,128)(2,1)}, bf16[768,128]{1,0:T(8,128)(2,1)S(1)}, u32[]{:S(2)}) copy-start(bf16[768,128]{1,0:T(8,128)(2,1)S(1)} %collective-permute-done.38.refs_6_) | copy-start | bytes 589828
  23.6 1.4 collective-permute-start.40
  24.0 1.5 copy-start.9
  24.0 1.4 collective-permute-start.41
  25.5 0.8 copy-start.6
  25.5 0.9 copy-start.7
  38.5 48.4 %collective-permute-start.55 = (bf16[3,12,128,128]{3,2,1,0:T(8,128)(2,1)}, bf16[3,12,128,128]{3,2,1,0:T(8,128)(2,1)}, u32[]{:S(2)}, u32[]{:S(2)}) collective-permute-start(bf16[3,12,128,128]{3,2,1,0:T(8,128)(2,1)} %get-tuple-element.196), channel_id=1, source_target_pairs={{0,8},{8,16},{16,24},{1,9},{9,17},{17,25},{2,10},{10,18},{18,26},{... | collective-permute-start | bytes 3538952 | tf_op jit(solution)/shard_map/ppermute | solution.py:39
  43.1 11.0 %collective-permute-start.48 = (bf16[1552,128]{1,0:T(8,128)(2,1)S(1)}, bf16[1552,128]{1,0:T(8,128)(2,1)S(1)}, u32[]{:S(2)}, u32[]{:S(2)}) collective-permute-start(bf16[1552,128]{1,0:T(8,128)(2,1)S(1)} %get-tuple-element.188.refs_10_), channel_id=1, source_target_pairs={{0,4},{1,5},{2,6},{3,7},{4,0},{5,1},{6,2},{7,3},{8,12},{9,13},{10,... | collective-permute-start | bytes 1191944 | tf_op jit(solution)/shard_map/ppermute | solution.py:34
  44.7 10.7 %collective-permute-start.46 = (bf16[1552,128]{1,0:T(8,128)(2,1)S(1)}, bf16[1552,128]{1,0:T(8,128)(2,1)S(1)}, u32[]{:S(2)}, u32[]{:S(2)}) collective-permute-start(bf16[1552,128]{1,0:T(8,128)(2,1)S(1)} %get-tuple-element.188.refs_10_), channel_id=1, source_target_pairs={{0,2},{1,3},{2,0},{3,1},{4,6},{5,7},{6,4},{7,5},{8,10},{9,11},{10,... | collective-permute-start | bytes 1191944 | tf_op jit(solution)/shard_map/ppermute | solution.py:34
  45.2 11.1 %collective-permute-start.45 = (bf16[1552,128]{1,0:T(8,128)(2,1)S(1)}, bf16[1552,128]{1,0:T(8,128)(2,1)S(1)}, u32[]{:S(2)}, u32[]{:S(2)}) collective-permute-start(bf16[1552,128]{1,0:T(8,128)(2,1)S(1)} %get-tuple-element.188.refs_10_), channel_id=1, source_target_pairs={{0,1},{1,0},{2,3},{3,2},{4,5},{5,4},{6,7},{7,6},{8,9},{9,8},{10,11... | collective-permute-start | bytes 1191944 | tf_op jit(solution)/shard_map/ppermute | solution.py:34
  54.1 7.0 %collective-permute-start.51 = (bf16[784,128]{1,0:T(8,128)(2,1)S(1)}, bf16[784,128]{1,0:T(8,128)(2,1)S(1)}, u32[]{:S(2)}, u32[]{:S(2)}) collective-permute-start(bf16[784,128]{1,0:T(8,128)(2,1)S(1)} %slice.129), channel_id=1, source_target_pairs={{0,2},{1,3},{2,0},{3,1},{4,6},{5,7},{6,4},{7,5},{8,10},{9,11},{10,... | collective-permute-start | bytes 602120 | tf_op jit(solution)/shard_map/ppermute | solution.py:34
  55.4 5.7 %collective-permute-start.50 = (bf16[768,128]{1,0:T(8,128)(2,1)S(1)}, bf16[768,128]{1,0:T(8,128)(2,1)S(1)}, u32[]{:S(2)}, u32[]{:S(2)}) collective-permute-start(bf16[768,128]{1,0:T(8,128)(2,1)S(1)} %slice.128), channel_id=1, source_target_pairs={{0,4},{1,5},{2,6},{3,7},{4,0},{5,1},{6,2},{7,3},{8,12},{9,13},{10,... | collective-permute-start | bytes 589832 | tf_op jit(solution)/shard_map/ppermute | solution.py:34
  56.3 6.9 %collective-permute-start.47 = (bf16[1552,128]{1,0:T(8,128)(2,1)S(1)}, bf16[1552,128]{1,0:T(8,128)(2,1)S(1)}, u32[]{:S(2)}, u32[]{:S(2)}) collective-permute-start(bf16[1552,128]{1,0:T(8,128)(2,1)S(1)} %collective-permute-done.46.refs_12_), channel_id=1, source_target_pairs={{0,1},{1,0},{2,3},{3,2},{4,5},{5,4},{6,7},{7,6},{8,9},{9,8},{10,11... | collective-permute-start | bytes 1191944 | tf_op jit(solution)/shard_map/ppermute | solution.py:34
  61.1 2.2 %collective-permute-start.49 = (bf16[1552,128]{1,0:T(8,128)(2,1)S(1)}, bf16[1552,128]{1,0:T(8,128)(2,1)S(1)}, u32[]{:S(2)}, u32[]{:S(2)}) collective-permute-start(bf16[1552,128]{1,0:T(8,128)(2,1)S(1)} %collective-permute-done.48.refs_14_), channel_id=1, source_target_pairs={{0,1},{1,0},{2,3},{3,2},{4,5},{5,4},{6,7},{7,6},{8,9},{9,8},{10,11... | collective-permute-start | bytes 1191944 | tf_op jit(solution)/shard_map/ppermute | solution.py:34
  61.1 2.0 %collective-permute-start.52 = (bf16[768,128]{1,0:T(8,128)(2,1)S(1)}, bf16[768,128]{1,0:T(8,128)(2,1)S(1)}, u32[]{:S(2)}, u32[]{:S(2)}) collective-permute-start(bf16[768,128]{1,0:T(8,128)(2,1)S(1)} %collective-permute-done.50.refs_16_), channel_id=1, source_target_pairs={{0,1},{1,0},{2,3},{3,2},{4,5},{5,4},{6,7},{7,6},{8,9},{9,8},{10,11... | collective-permute-start | bytes 589832 | tf_op jit(solution)/shard_map/ppermute | solution.py:34
  63.1 1.4 collective-permute-start.53
  63.2 23.7 %copy-start.1 = (f32[12,128,128]{2,1,0:T(8,128)S(1)}, f32[12,128,128]{2,1,0:T(8,128)}, u32[]{:S(2)}) copy-start(f32[12,128,128]{2,1,0:T(8,128)} %get-tuple-element.193) | copy-start | bytes 2359300
  63.2 23.7 %copy-start.14 = (s32[1,12]{1,0:T(1,128)S(1)}, s32[1,12]{1,0:T(1,128)}, u32[]{:S(2)}) copy-start(s32[1,12]{1,0:T(1,128)} %param.14) | copy-start | bytes 148
  87.9 13.1 %collective-permute-start.11 = (bf16[1536,128]{1,0:T(8,128)(2,1)S(1)}, bf16[1536,128]{1,0:T(8,128)(2,1)S(1)}, u32[]{:S(2)}, u32[]{:S(2)}) collective-permute-start(bf16[1536,128]{1,0:T(8,128)(2,1)S(1)} %get-tuple-element.136), channel_id=1, source_target_pairs={{0,8},{8,16},{16,24},{1,9},{9,17},{17,25},{2,10},{10,18},{18,26},{... | collective-permute-start | bytes 1179656 | tf_op jit(solution)/shard_map/cond/branch_1_fun/ppermute | solution.py:39
  101.0 54.8 %collective-permute-start.13 = (bf16[9280,128]{1,0:T(8,128)(2,1)S(1)}, bf16[9280,128]{1,0:T(8,128)(2,1)S(1)}, u32[]{:S(2)}, u32[]{:S(2)}) collective-permute-start(bf16[9280,128]{1,0:T(8,128)(2,1)S(1)} %pack_update.4), channel_id=1, source_target_pairs={{0,8},{8,16},{16,24},{1,9},{9,17},{17,25},{2,10},{10,18},{18,26},{... | collective-permute-start | bytes 7127048 | tf_op jit(solution)/shard_map/cond/branch_1_fun/ppermute | solution.py:39
  103.5 10.3 %collective-permute-start.12 = (bf16[1536,128]{1,0:T(8,128)(2,1)S(1)}, bf16[1536,128]{1,0:T(8,128)(2,1)S(1)}, u32[]{:S(2)}, u32[]{:S(2)}) collective-permute-start(bf16[1536,128]{1,0:T(8,128)(2,1)S(1)} %collective-permute-done.11.refs_0_), channel_id=1, source_target_pairs={{0,2},{1,3},{2,0},{3,1},{4,6},{5,7},{6,4},{7,5},{8,10},{9,11},{10,... | collective-permute-start | bytes 1179656 | tf_op jit(solution)/shard_map/cond/branch_1_fun/ppermute | solution.py:34
  105.1 10.3 %collective-permute-start.16 = (bf16[1536,128]{1,0:T(8,128)(2,1)S(1)}, bf16[1536,128]{1,0:T(8,128)(2,1)S(1)}, u32[]{:S(2)}, u32[]{:S(2)}) collective-permute-start(bf16[1536,128]{1,0:T(8,128)(2,1)S(1)} %collective-permute-done.11.refs_0_), channel_id=1, source_target_pairs={{0,4},{1,5},{2,6},{3,7},{4,0},{5,1},{6,2},{7,3},{8,12},{9,13},{10,... | collective-permute-start | bytes 1179656 | tf_op jit(solution)/shard_map/cond/branch_1_fun/ppermute | solution.py:34
  105.6 11.0 %collective-permute-start.14 = (bf16[1536,128]{1,0:T(8,128)(2,1)S(1)}, bf16[1536,128]{1,0:T(8,128)(2,1)S(1)}, u32[]{:S(2)}, u32[]{:S(2)}) collective-permute-start(bf16[1536,128]{1,0:T(8,128)(2,1)S(1)} %collective-permute-done.11.refs_0_), channel_id=1, source_target_pairs={{0,1},{1,0},{2,3},{3,2},{4,5},{5,4},{6,7},{7,6},{8,9},{9,8},{10,11... | collective-permute-start | bytes 1179656 | tf_op jit(solution)/shard_map/cond/branch_1_fun/ppermute | solution.py:34
  113.8 5.7 %collective-permute-start.18 = (bf16[768,128]{1,0:T(8,128)(2,1)S(1)}, bf16[768,128]{1,0:T(8,128)(2,1)S(1)}, u32[]{:S(2)}, u32[]{:S(2)}) collective-permute-start(bf16[768,128]{1,0:T(8,128)(2,1)S(1)} %slice.122), channel_id=1, source_target_pairs={{0,4},{1,5},{2,6},{3,7},{4,0},{5,1},{6,2},{7,3},{8,12},{9,13},{10,... | collective-permute-start | bytes 589832 | tf_op jit(solution)/shard_map/cond/branch_1_fun/ppermute | solution.py:34
  115.4 5.7 %collective-permute-start.19 = (bf16[768,128]{1,0:T(8,128)(2,1)S(1)}, bf16[768,128]{1,0:T(8,128)(2,1)S(1)}, u32[]{:S(2)}, u32[]{:S(2)}) collective-permute-start(bf16[768,128]{1,0:T(8,128)(2,1)S(1)} %slice.123), channel_id=1, source_target_pairs={{0,2},{1,3},{2,0},{3,1},{4,6},{5,7},{6,4},{7,5},{8,10},{9,11},{10,... | collective-permute-start | bytes 589832 | tf_op jit(solution)/shard_map/cond/branch_1_fun/ppermute | solution.py:34
  116.0 6.6 %collective-permute-start.15 = (bf16[1536,128]{1,0:T(8,128)(2,1)S(1)}, bf16[1536,128]{1,0:T(8,128)(2,1)S(1)}, u32[]{:S(2)}, u32[]{:S(2)}) collective-permute-start(bf16[1536,128]{1,0:T(8,128)(2,1)S(1)} %collective-permute-done.12.refs_2_), channel_id=1, source_target_pairs={{0,1},{1,0},{2,3},{3,2},{4,5},{5,4},{6,7},{7,6},{8,9},{9,8},{10,11... | collective-permute-start | bytes 1179656 | tf_op jit(solution)/shard_map/cond/branch_1_fun/ppermute | solution.py:34
  116.5 6.1 %collective-permute-start.17 = (bf16[1536,128]{1,0:T(8,128)(2,1)S(1)}, bf16[1536,128]{1,0:T(8,128)(2,1)S(1)}, u32[]{:S(2)}, u32[]{:S(2)}) collective-permute-start(bf16[1536,128]{1,0:T(8,128)(2,1)S(1)} %collective-permute-done.16.refs_4_), channel_id=1, source_target_pairs={{0,1},{1,0},{2,3},{3,2},{4,5},{5,4},{6,7},{7,6},{8,9},{9,8},{10,11... | collective-permute-start | bytes 1179656 | tf_op jit(solution)/shard_map/cond/branch_1_fun/ppermute | solution.py:34
  119.6 3.0 %collective-permute-start.20 = (bf16[768,128]{1,0:T(8,128)(2,1)S(1)}, bf16[768,128]{1,0:T(8,128)(2,1)S(1)}, u32[]{:S(2)}, u32[]{:S(2)}) collective-permute-start(bf16[768,128]{1,0:T(8,128)(2,1)S(1)} %collective-permute-done.18.refs_6_), channel_id=1, source_target_pairs={{0,1},{1,0},{2,3},{3,2},{4,5},{5,4},{6,7},{7,6},{8,9},{9,8},{10,11... | collective-permute-start | bytes 589832 | tf_op jit(solution)/shard_map/cond/branch_1_fun/ppermute | solution.py:34
  121.2 1.5 collective-permute-start.21
  160.1 0.7 copy-start.12
  160.1 0.9 copy-start.13
  (2 other events, 1.4 us)

commit v3 on v2

--- a/solution.py
+++ b/solution.py
@@ -204,7 +204,9 @@
         alpha = jnp.where(norm > 1e-30, num / jnp.maximum(norm, 1e-30), 0.0).astype(BF16).astype(F32)
         payload[pl.ds(pl.multiple_of(t * width, width), width), :] = (h - alpha * v).astype(BF16)
         now = jnp.where(row == t, alpha, ext[...])
-        ext[...] = now + jnp.where(row == count, norm, 0.0) + jnp.where(row == count + 1, num, 0.0)
+        now = now + jnp.where(row == count, norm, 0.0) + jnp.where(row == count + 1, num, 0.0)
+        top = jnp.max(jnp.max(jnp.abs(h), axis=0, keepdims=True), axis=1, keepdims=True)
+        ext[...] = jnp.where(row == count + 2, jnp.maximum(now, top), now)
 
     def before(i):
         arrival(envs, count)(i)
@@ -221,6 +223,7 @@
     mid = rest.astype(BF16).astype(F32)
     low = rest - mid
     split = jnp.where(lane == 0, high, jnp.where(lane == 1, mid, jnp.where(lane == 2, low, 0.0)))
+    split = jnp.where((row == count) & (lane == 3), now[count + 2 : count + 3], split)
     extra = jnp.where(row < count, now, split)
     extra = jnp.where(row == count + 2, table[0:1, :], jnp.where(row == count + 3, table[1:2, :], extra))
     payload[pl.ds(count * width, EXTRA), :] = extra.astype(BF16)
@@ -292,22 +295,28 @@
     copies = start_pieces(places, rpieces, rheld, hsem) + start_pieces(places, vpieces, vheld, vsem)
     bring_in(envs, count, copies)
     both = jnp.zeros((EXTRA, 128), F32)
-    caps = []
+    caps, tops = [], []
     for place in range(nblk):
         part = rheld[place, pl.ds(count * width, EXTRA), :].astype(F32)
         ext[pl.ds(place * EXTRA, EXTRA), :] = part
         caps.append(part[count + 2 : count + 3])
+        tops.append(part[count : count + 1])
         both = both + part
     turns = part[count + 3 : count + 4].astype(jnp.int32)
     most, (table, table_before) = layout_of(
         jnp.concatenate(caps, 0), turns, device[0], device[1], count, secs, late
     )
     tables[0], tables[1] = table, table_before
-    both = jnp.sum(both, axis=1, keepdims=True)
+    lane = lax.broadcasted_iota(jnp.int32, (1, 128), 1)
+    top = jnp.where(lane == 3, functools.reduce(jnp.maximum, tops), 0.0)
+    top = jnp.max(top, axis=1, keepdims=True)
+    top = jnp.where(top > 0.0, top, 1.0)
+    both = jnp.sum(jnp.where(lane < 3, both, 0.0), axis=1, keepdims=True)
     norm, num = both[count : count + 1], both[count + 1 : count + 2]
     firsts = jnp.where(srow == 2, num / norm, jnp.where(srow == 3, jnp.sqrt(cells / norm), 0.0))
+    firsts = jnp.where(srow == 5, jnp.sqrt(cells / norm) * top, firsts)
     sums[...] = jnp.where(srow == 4, most, firsts)
-    a_zero, scale = sums[2:3, :], sums[3:4, :]
+    a_zero, scale = sums[2:3, :], 1.0 / top
 
     def slot(t):
         x = []
@@ -340,13 +349,16 @@
         both = both + parts[i]
     squares, num = both[0:1, :] / cells, both[1:2, :] / cells
     a_zero, scale = parts[0, 2:3, :], parts[0, 3:4, :]
-    beta = jnp.sqrt(squares + 1e-06)
-    a_one = num / (beta * beta)
+    unit = parts[0, 5:6, :]
+    size = unit * jnp.sqrt(squares)
+    beta = jnp.sqrt(size * size + 1e-06)
+    in_units = beta / unit
+    a_one = num / (in_units * in_units)
     half_gap = (a_zero - a_one) / 2.0
     ritz = (a_zero + a_one) / 2.0 - jnp.sqrt(half_gap * half_gap + beta * beta)
     gap_val = ritz - a_zero
     length = jnp.sqrt(beta * beta + gap_val * gap_val)
-    from_v, from_w = beta / length * scale, gap_val / length / beta
+    from_v, from_w = beta / length * scale, gap_val / length / in_units
     row = lax.broadcasted_iota(jnp.int32, coefs.shape, 0)
     coefs[...] = jnp.where(row == 0, from_v, jnp.where(row == 1, from_w, ritz))
     lane = lax.broadcasted_iota(jnp.int32, (width, width), 1)

time: 160 us -> 157 us (0.981); the launches traced: 161 us -> 155 us
  waiting for transfers between devices: 58.5 us -> 52.1 us
    ppermute x4, waiting for transfers between devices: 24.6 us -> 18 us  [onward(): return lax.ppermute(value, 'sec', [(i, i + 1) for i in range(length - 1)])]
  transfers between devices with their start and end apart: 34 -> 34, of which waited for: 15 -> 15; matrix products, arithmetic and copies ran while one was open for 6% -> 6% of each run, Pallas kernels for 27% -> 29%
where the time goes in v3:
time: 157 us; the launch traced here: 155 us
  waiting for transfers between devices  52.1 us (33%)
  Pallas kernels  49.2 us (31%)
  starting transfers between devices  30.2 us (19%)
  blocking collectives  8.46 us (5%)
  local copies, waits for them, and re-layouts  7.3 us (5%)
  other arithmetic  5.71 us (4%)
    ppermute x27, waiting for transfers between devices, exchange(): return lax.ppermute(value, 'blk', [(i, i ^ bit) for i in range(length)])  34.1 us
    ppermute x4, waiting for transfers between devices, onward(): return lax.ppermute(value, 'sec', [(i, i + 1) for i in range(length - 1)])  18 us
    ppermute x27, starting transfers between devices, exchange(): return lax.ppermute(value, 'blk', [(i, i ^ bit) for i in range(length)])  14 us
    pallas_call x1, Pallas kernels, shards(): call(functools.partial(second_kernel, places, count, cells, secs, late, u...  12.6 us
    pallas_call x1, Pallas kernels, shards(): call(functools.partial(first_kernel, places, count, then), 'ham_first', [...  12.2 us
    ppermute x4, starting transfers between devices, onward(): return lax.ppermute(value, 'sec', [(i, i + 1) for i in range(length - 1)])  11.5 us
    pallas_call x1, Pallas kernels, branch(): call(functools.partial(early_kernel, places, count, early), 'early_update...  11.2 us
    all_gather x1, blocking collectives, shards(): parts = lax.all_gather(sums, 'blk', axis=0)  8.46 us
  transfers between devices with their start and end apart: 34, of which 15 were waited for; matrix products, arithmetic and copies ran while one was open for 6% of the time, Pallas kernels for 29%

profile of v3, /device:TPU:8, one launch (start us, length us, event | category | flops | bytes accessed | tf_op | source)
XLA Modules:
  0.0 154.8 jit_solution(3883188606094692218)
XLA Ops:
  0.6 0.8 slice_bitcast_fusion.8
  1.5 1.3 fusion.3.refs_0_
  2.9 1.6 %collective-permute-start.34 = (bf16[1536,128]{1,0:T(8,128)(2,1)S(1)}, bf16[1536,128]{1,0:T(8,128)(2,1)S(1)}, u32[]{:S(2)}, u32[]{:S(2)}) collective-permute-start(bf16[1536,128]{1,0:T(8,128)(2,1)S(1)} %fusion.3.refs_0_), channel_id=1, source_target_pairs={{0,2},{1,3},{2,0},{3,1},{4,6},{5,7},{6,4},{7,5},{8,10},{9,11},{10,... | collective-permute-start | bytes 1179656 | tf_op jit(solution)/shard_map/ppermute | solution.py:34
  4.5 1.5 collective-permute-start.36
  6.0 0.7 bitcast_minimum_fusion
  6.7 0.7 add_convert_fusion.3
  7.9 1.6 %collective-permute-start.42 = (f32[8,128]{1,0:T(8,128)S(1)}, f32[8,128]{1,0:T(8,128)S(1)}, u32[]{:S(2)}, u32[]{:S(2)}) collective-permute-start(f32[8,128]{1,0:T(8,128)S(1)} %dynamic_update_slice.3), channel_id=1, source_target_pairs={{0,8},{8,16},{16,24},{24,0},{1,9},{9,17},{17,25},{25,1},{2,10},{10... | collective-permute-start | bytes 12296 | tf_op jit(solution)/shard_map/ppermute | solution.py:588
  9.5 1.1 collective-permute-start.43
  10.6 1.9 %collective-permute-start.44 = (f32[8,128]{1,0:T(8,128)S(1)}, f32[8,128]{1,0:T(8,128)S(1)}, u32[]{:S(2)}, u32[]{:S(2)}) collective-permute-start(f32[8,128]{1,0:T(8,128)S(1)} %dynamic_update_slice.3), channel_id=1, source_target_pairs={{0,24},{8,0},{16,8},{24,16},{1,25},{9,1},{17,9},{25,17},{2,26},{10... | collective-permute-start | bytes 12296 | tf_op jit(solution)/shard_map/ppermute | solution.py:588
  12.6 3.0 %slice_bitcast_fusion.6 = bf16[5,12,128,128]{3,2,1,0:T(8,128)(2,1)} fusion(bf16[1,20,12,128,128]{4,3,2,1,0:T(8,128)(2,1)} %param.10), kind=kLoop, calls=%fused_computation.15 | loop fusion | bytes 3932160 | tf_op jit(solution)/shard_map/slice | solution.py:589
  15.6 2.0 %collective-permute-start.54 = (bf16[5,12,128,128]{3,2,1,0:T(8,128)(2,1)}, bf16[5,12,128,128]{3,2,1,0:T(8,128)(2,1)}, u32[]{:S(2)}, u32[]{:S(2)}) collective-permute-start(bf16[5,12,128,128]{3,2,1,0:T(8,128)(2,1)} %slice_bitcast_fusion.6), channel_id=1, source_target_pairs={{0,8},{8,16},{16,24},{1,9},{9,17},{17,25},{2,10},{10,18},{18,26},{... | collective-permute-start | bytes 5898248 | tf_op jit(solution)/shard_map/ppermute | solution.py:39
  17.7 0.6 collective-permute-start.38
  18.3 0.6 collective-permute-start.39
  19.4 4.2 %collective-permute-done.38.refs_6_ = bf16[768,128]{1,0:T(8,128)(2,1)S(1)} collective-permute-done((bf16[768,128]{1,0:T(8,128)(2,1)S(1)}, bf16[768,128]{1,0:T(8,128)(2,1)S(1)}, u32[]{:S(2)}, u32[]{:S(2)}) %collective-permute-start.38) | collective-permute-done | bytes 196640 | tf_op jit(solution)/shard_map/ppermute | solution.py:34
  24.3 0.8 collective-permute-done.40.refs_8_
  26.4 12.2 %ham_first.1 = (f32[12,128,128]{2,1,0:T(8,128)}, bf16[1552,128]{1,0:T(8,128)(2,1)S(1)}, bf16[3,12,128,128]{3,2,1,0:T(8,128)(2,1)}) custom-call(s32[12]{0:T(128)S(1)} %bitcast.63, s32[2]{0:T(128)S(1)} %pad_add_fusion.device, s32[12,2]{1,0:T(8,128)S(1)} %copy.14.dims, f32[8,128]{1,0:T(8,128)S(1)} %add_add_fusion.table, bf16[1536,128]{1,0:T(8,128)(2,1)} %copy-done.2, ...), custom_call_target="tpu_custom_call" | custom-call | flops 1 | bytes 1 | tf_op jit(solution)/shard_map/ham_first/pallas_call | solution.py:622
  38.6 4.6 %collective-permute-start.55 = (bf16[3,12,128,128]{3,2,1,0:T(8,128)(2,1)}, bf16[3,12,128,128]{3,2,1,0:T(8,128)(2,1)}, u32[]{:S(2)}, u32[]{:S(2)}) collective-permute-start(bf16[3,12,128,128]{3,2,1,0:T(8,128)(2,1)} %get-tuple-element.196), channel_id=1, source_target_pairs={{0,8},{8,16},{16,24},{1,9},{9,17},{17,25},{2,10},{10,18},{18,26},{... | collective-permute-start | bytes 3538952 | tf_op jit(solution)/shard_map/ppermute | solution.py:39
  43.2 1.6 %collective-permute-start.48 = (bf16[1552,128]{1,0:T(8,128)(2,1)S(1)}, bf16[1552,128]{1,0:T(8,128)(2,1)S(1)}, u32[]{:S(2)}, u32[]{:S(2)}) collective-permute-start(bf16[1552,128]{1,0:T(8,128)(2,1)S(1)} %get-tuple-element.188.refs_10_), channel_id=1, source_target_pairs={{0,4},{1,5},{2,6},{3,7},{4,0},{5,1},{6,2},{7,3},{8,12},{9,13},{10,... | collective-permute-start | bytes 1191944 | tf_op jit(solution)/shard_map/ppermute | solution.py:34
  44.8 0.5 collective-permute-start.46
  45.3 8.9 %collective-permute-done.48.refs_14_ = bf16[1552,128]{1,0:T(8,128)(2,1)S(1)} collective-permute-done((bf16[1552,128]{1,0:T(8,128)(2,1)S(1)}, bf16[1552,128]{1,0:T(8,128)(2,1)S(1)}, u32[]{:S(2)}, u32[]{:S(2)}) %collective-permute-start.48) | collective-permute-done | bytes 397344 | tf_op jit(solution)/shard_map/ppermute | solution.py:34
  54.2 0.6 collective-permute-start.51
  54.9 0.6 collective-permute-done.46.refs_12_
  55.5 1.0 collective-permute-start.50
  56.5 4.8 %collective-permute-done.50.refs_16_ = bf16[768,128]{1,0:T(8,128)(2,1)S(1)} collective-permute-done((bf16[768,128]{1,0:T(8,128)(2,1)S(1)}, bf16[768,128]{1,0:T(8,128)(2,1)S(1)}, u32[]{:S(2)}, u32[]{:S(2)}) %collective-permute-start.50) | collective-permute-done | bytes 196640 | tf_op jit(solution)/shard_map/ppermute | solution.py:34
  61.7 1.5 collective-permute-done.52.refs_18_
  63.4 1.3 collective-permute-done.53.refs_19_
  64.7 12.6 %ham_second.1 = (f32[12,128,128]{2,1,0:T(8,128)S(1)}, f32[8,128]{1,0:T(8,128)S(1)}, s32[2,8,128]{2,1,0:T(8,128)S(1)}, bf16[5,12,128,128]{3,2,1,0:T(8,128)(2,1)S(1)}, bf16[5,12,128,128]{3,2,1,0:T(8,128)(2,1)S(1)}) custom-call(s32[12]{0:T(128)S(1)} %bitcast.64, s32[2]{0:T(128)S(1)} %pad_add_fusion.device, s32[12,2]{1,0:T(8,128)S(1)} %copy.14.dims, ...), custom_call_target="tpu_custom_call" | custom-call | flops 1 | bytes 1 | tf_op jit(solution)/shard_map/ham_second/pallas_call | solution.py:632
  78.4 8.5 %all-gather = f32[64,128]{1,0:T(8,128)S(1)} all-gather(f32[8,128]{1,0:T(8,128)S(1)} %get-tuple-element.189), channel_id=2, replica_groups=mesh['sec'=4,'blk'=8] {'blk'}, dimensions={0}, use_global_device_ids=true | all-gather | bytes 36864 | tf_op jit(solution)/shard_map/all_gather | solution.py:645
  86.9 67.0 %conditional.4 = (bf16[1,12,128,128]{3,2,1,0:T(8,128)(2,1)S(1)}, f32[1]{0:T(128)}, bf16[1,20,12,128,128]{4,3,2,1,0:T(8,128)(2,1)}, bf16[1,12,128,128]{3,2,1,0:T(8,128)(2,1)S(1)}) conditional(s32[]{:T(128)} %bitcast.43, (s32[2,8,128]{2,1,0:T(8,128)S(1)}, s32[1,12]{1,0:T(1,128)S(1)}, f32[8,8,128]{2,1,0:T(8,128)S(1)}, ...), branch_computations={%region_0.1_spmd, %region_1.2_spmd, %region_2.3_spmd} | conditional | flops 1966084 | bytes 56508928
  86.9 0.8 ritz.3
  87.7 2.5 %collective-permute-start = (bf16[1536,128]{1,0:T(8,128)(2,1)S(1)}, bf16[1536,128]{1,0:T(8,128)(2,1)S(1)}, u32[]{:S(2)}, u32[]{:S(2)}) collective-permute-start(bf16[1536,128]{1,0:T(8,128)(2,1)S(1)} %get-tuple-element.118), channel_id=1, source_target_pairs={{0,8},{8,16},{16,24},{1,9},{9,17},{17,25},{2,10},{10,18},{18,26},{... | collective-permute-start | bytes 1179656 | tf_op jit(solution)/shard_map/cond/branch_0_fun/ppermute | solution.py:39
  90.2 8.2 %pack_update.3 = bf16[8112,128]{1,0:T(8,128)(2,1)S(1)} custom-call(s32[8,128]{1,0:T(8,128)S(1)} %get-tuple-element.208.table, f32[8,128]{1,0:T(8,128)S(1)} %get-tuple-element.120.coefs, bf16[5,12,128,128]{3,2,1,0:T(8,128)(2,1)S(1)} %get-tuple-element.114.vsrc, bf16[5,12,128,128]{3,2,1,0:T(8,128)(2,1)S(1)} %get-tuple-element.115.wsrc, ...), custom_call_target="tpu_custom_call" | custom-call | flops 1 | bytes 20971520 | tf_op jit(solution)/shard_map/cond/branch_0_fun/pack_update/pallas_call | solution.py:663
  98.4 2.6 %collective-permute-done.refs_0_ = bf16[1536,128]{1,0:T(8,128)(2,1)S(1)} collective-permute-done((bf16[1536,128]{1,0:T(8,128)(2,1)S(1)}, bf16[1536,128]{1,0:T(8,128)(2,1)S(1)}, u32[]{:S(2)}, u32[]{:S(2)}) %collective-permute-start) | collective-permute-done | bytes 393248 | tf_op jit(solution)/shard_map/cond/branch_0_fun/ppermute | solution.py:39
  101.0 2.4 %collective-permute-start.2 = (bf16[8112,128]{1,0:T(8,128)(2,1)S(1)}, bf16[8112,128]{1,0:T(8,128)(2,1)S(1)}, u32[]{:S(2)}, u32[]{:S(2)}) collective-permute-start(bf16[8112,128]{1,0:T(8,128)(2,1)S(1)} %pack_update.3), channel_id=1, source_target_pairs={{0,8},{8,16},{16,24},{1,9},{9,17},{17,25},{2,10},{10,18},{18,26},{... | collective-permute-start | bytes 6230024 | tf_op jit(solution)/shard_map/cond/branch_0_fun/ppermute | solution.py:39
  103.4 1.5 %collective-permute-start.1 = (bf16[1536,128]{1,0:T(8,128)(2,1)S(1)}, bf16[1536,128]{1,0:T(8,128)(2,1)S(1)}, u32[]{:S(2)}, u32[]{:S(2)}) collective-permute-start(bf16[1536,128]{1,0:T(8,128)(2,1)S(1)} %collective-permute-done.refs_0_), channel_id=1, source_target_pairs={{0,2},{1,3},{2,0},{3,1},{4,6},{5,7},{6,4},{7,5},{8,10},{9,11},{10,... | collective-permute-start | bytes 1179656 | tf_op jit(solution)/shard_map/cond/branch_0_fun/ppermute | solution.py:34
  105.0 0.5 collective-permute-start.5
  105.5 8.2 %collective-permute-done.1.refs_2_ = bf16[1536,128]{1,0:T(8,128)(2,1)S(1)} collective-permute-done((bf16[1536,128]{1,0:T(8,128)(2,1)S(1)}, bf16[1536,128]{1,0:T(8,128)(2,1)S(1)}, u32[]{:S(2)}, u32[]{:S(2)}) %collective-permute-start.1) | collective-permute-done | bytes 393248 | tf_op jit(solution)/shard_map/cond/branch_0_fun/ppermute | solution.py:34
  113.8 1.2 collective-permute-done.5.refs_4_
  115.0 0.6 collective-permute-start.8
  115.6 1.5 collective-permute-start.7
  118.2 1.4 fusion
  119.6 1.1 collective-permute-done.8.refs_7_
  120.7 0.6 collective-permute-done.7.refs_6_
  121.4 1.4 multiply_add_fusion
  122.9 11.2 %early_update.3.so_far = bf16[4,5,12,128,128]{4,3,2,1,0:T(8,128)(2,1)} custom-call(s32[8,128]{1,0:T(8,128)S(1)} %get-tuple-element.207.table, s32[2]{0:T(128)S(1)} %get-tuple-element.125.device, s32[1]{0:T(128)} %bitcast.8.first_sec, bf16[1536,128]{1,0:T(8,128)(2,1)S(1)} %collective-permute-done.refs_0_, ...), custom_call_target="tpu_custom_call" | custom-call | flops 1 | bytes 1 | tf_op jit(solution)/shard_map/cond/branch_0_fun/early_update/pallas_call | solution.py:684
  134.1 15.4 %collective-permute-done.2.packed = bf16[8112,128]{1,0:T(8,128)(2,1)S(1)} collective-permute-done((bf16[8112,128]{1,0:T(8,128)(2,1)S(1)}, bf16[8112,128]{1,0:T(8,128)(2,1)S(1)}, u32[]{:S(2)}, u32[]{:S(2)}) %collective-permute-start.2) | collective-permute-done | bytes 2076704 | tf_op jit(solution)/shard_map/cond/branch_0_fun/ppermute | solution.py:39
  149.5 4.2 %unpack_update.3 = bf16[4,5,12,128,128]{4,3,2,1,0:T(8,128)(2,1)} custom-call(s32[8,128]{1,0:T(8,128)S(1)} %get-tuple-element.207.table, s32[1]{0:T(128)} %bitcast.8.first_sec, bf16[8112,128]{1,0:T(8,128)(2,1)S(1)} %collective-permute-done.2.packed, bf16[4,5,12,128,128]{4,3,2,1,0:T(8,128)(2,1)} %bitcast.69, ...), custom_call_target="tpu_custom_call", output_to_operand_aliasing={{}: (4, {})} | custom-call | flops 1 | bytes 1 | tf_op jit(solution)/shard_map/cond/branch_0_fun/unpack_update/pallas_call | solution.py:699
  154.0 0.7 copy-done.12
  (83 shorter events, 5.7 us)
Async XLA Ops:
  2.8 14.9 %copy-start.2 = (bf16[1536,128]{1,0:T(8,128)(2,1)}, bf16[1536,128]{1,0:T(8,128)(2,1)S(1)}, u32[]{:S(2)}) copy-start(bf16[1536,128]{1,0:T(8,128)(2,1)S(1)} %fusion.3.refs_0_) | copy-start | bytes 1179652
  2.8 5.0 %collective-permute-start.33 = (bf16[1536,128]{1,0:T(8,128)(2,1)S(1)}, bf16[1536,128]{1,0:T(8,128)(2,1)S(1)}, u32[]{:S(2)}, u32[]{:S(2)}) collective-permute-start(bf16[1536,128]{1,0:T(8,128)(2,1)S(1)} %fusion.3.refs_0_), channel_id=1, source_target_pairs={{0,1},{1,0},{2,3},{3,2},{4,5},{5,4},{6,7},{7,6},{8,9},{9,8},{10,11... | collective-permute-start | bytes 1179656 | tf_op jit(solution)/shard_map/ppermute | solution.py:34
  2.9 14.7 %collective-permute-start.34 = (bf16[1536,128]{1,0:T(8,128)(2,1)S(1)}, bf16[1536,128]{1,0:T(8,128)(2,1)S(1)}, u32[]{:S(2)}, u32[]{:S(2)}) collective-permute-start(bf16[1536,128]{1,0:T(8,128)(2,1)S(1)} %fusion.3.refs_0_), channel_id=1, source_target_pairs={{0,2},{1,3},{2,0},{3,1},{4,6},{5,7},{6,4},{7,5},{8,10},{9,11},{10,... | collective-permute-start | bytes 1179656 | tf_op jit(solution)/shard_map/ppermute | solution.py:34
  4.5 13.8 %collective-permute-start.36 = (bf16[1536,128]{1,0:T(8,128)(2,1)S(1)}, bf16[1536,128]{1,0:T(8,128)(2,1)S(1)}, u32[]{:S(2)}, u32[]{:S(2)}) collective-permute-start(bf16[1536,128]{1,0:T(8,128)(2,1)S(1)} %fusion.3.refs_0_), channel_id=1, source_target_pairs={{0,4},{1,5},{2,6},{3,7},{4,0},{5,1},{6,2},{7,3},{8,12},{9,13},{10,... | collective-permute-start | bytes 1179656 | tf_op jit(solution)/shard_map/ppermute | solution.py:34
  7.8 16.3 %copy-start.15 = (s32[1,12,2]{1,2,0:T(2,128)S(1)}, s32[1,12,2]{1,2,0:T(2,128)}, u32[]{:S(2)}) copy-start(s32[1,12,2]{1,2,0:T(2,128)} %param.13) | copy-start | bytes 292
  7.9 18.5 %copy-start = (s32[1,12]{1,0:T(1,128)S(1)}, s32[1,12]{1,0:T(1,128)}, u32[]{:S(2)}) copy-start(s32[1,12]{1,0:T(1,128)} %param.12) | copy-start | bytes 148
  7.9 9.8 %copy-start.5 = (bf16[1536,128]{1,0:T(8,128)(2,1)}, bf16[1536,128]{1,0:T(8,128)(2,1)S(1)}, u32[]{:S(2)}) copy-start(bf16[1536,128]{1,0:T(8,128)(2,1)S(1)} %collective-permute-done.33.refs_1_) | copy-start | bytes 1179652
  7.9 7.7 %collective-permute-start.42 = (f32[8,128]{1,0:T(8,128)S(1)}, f32[8,128]{1,0:T(8,128)S(1)}, u32[]{:S(2)}, u32[]{:S(2)}) collective-permute-start(f32[8,128]{1,0:T(8,128)S(1)} %dynamic_update_slice.3), channel_id=1, source_target_pairs={{0,8},{8,16},{16,24},{24,0},{1,9},{9,17},{17,25},{25,1},{2,10},{10... | collective-permute-start | bytes 12296 | tf_op jit(solution)/shard_map/ppermute | solution.py:588
  9.5 6.1 %collective-permute-start.43 = (f32[8,128]{1,0:T(8,128)S(1)}, f32[8,128]{1,0:T(8,128)S(1)}, u32[]{:S(2)}, u32[]{:S(2)}) collective-permute-start(f32[8,128]{1,0:T(8,128)S(1)} %dynamic_update_slice.3), channel_id=1, source_target_pairs={{0,16},{8,24},{16,0},{24,8},{1,17},{9,25},{17,1},{25,9},{2,18},{10... | collective-permute-start | bytes 12296 | tf_op jit(solution)/shard_map/ppermute | solution.py:588
  10.6 5.0 %collective-permute-start.44 = (f32[8,128]{1,0:T(8,128)S(1)}, f32[8,128]{1,0:T(8,128)S(1)}, u32[]{:S(2)}, u32[]{:S(2)}) collective-permute-start(f32[8,128]{1,0:T(8,128)S(1)} %dynamic_update_slice.3), channel_id=1, source_target_pairs={{0,24},{8,0},{16,8},{24,16},{1,25},{9,1},{17,9},{25,17},{2,26},{10... | collective-permute-start | bytes 12296 | tf_op jit(solution)/shard_map/ppermute | solution.py:588
  15.6 71.3 %collective-permute-start.54 = (bf16[5,12,128,128]{3,2,1,0:T(8,128)(2,1)}, bf16[5,12,128,128]{3,2,1,0:T(8,128)(2,1)}, u32[]{:S(2)}, u32[]{:S(2)}) collective-permute-start(bf16[5,12,128,128]{3,2,1,0:T(8,128)(2,1)} %slice_bitcast_fusion.6), channel_id=1, source_target_pairs={{0,8},{8,16},{16,24},{1,9},{9,17},{17,25},{2,10},{10,18},{18,26},{... | collective-permute-start | bytes 5898248 | tf_op jit(solution)/shard_map/ppermute | solution.py:39
  17.6 7.9 %copy-start.3 = (bf16[1536,128]{1,0:T(8,128)(2,1)}, bf16[1536,128]{1,0:T(8,128)(2,1)S(1)}, u32[]{:S(2)}) copy-start(bf16[1536,128]{1,0:T(8,128)(2,1)S(1)} %collective-permute-done.34.refs_2_) | copy-start | bytes 1179652
  17.7 5.9 %collective-permute-start.38 = (bf16[768,128]{1,0:T(8,128)(2,1)S(1)}, bf16[768,128]{1,0:T(8,128)(2,1)S(1)}, u32[]{:S(2)}, u32[]{:S(2)}) collective-permute-start(bf16[768,128]{1,0:T(8,128)(2,1)S(1)} %slice.126), channel_id=1, source_target_pairs={{0,4},{1,5},{2,6},{3,7},{4,0},{5,1},{6,2},{7,3},{8,12},{9,13},{10,... | collective-permute-start | bytes 589832 | tf_op jit(solution)/shard_map/ppermute | solution.py:34
  18.3 7.2 %copy-start.4 = (bf16[1536,128]{1,0:T(8,128)(2,1)}, bf16[1536,128]{1,0:T(8,128)(2,1)S(1)}, u32[]{:S(2)}) copy-start(bf16[1536,128]{1,0:T(8,128)(2,1)S(1)} %collective-permute-done.36.refs_4_) | copy-start | bytes 1179652
  18.3 5.7 %collective-permute-start.39 = (bf16[768,128]{1,0:T(8,128)(2,1)S(1)}, bf16[768,128]{1,0:T(8,128)(2,1)S(1)}, u32[]{:S(2)}, u32[]{:S(2)}) collective-permute-start(bf16[768,128]{1,0:T(8,128)(2,1)S(1)} %slice.127), channel_id=1, source_target_pairs={{0,2},{1,3},{2,0},{3,1},{4,6},{5,7},{6,4},{7,5},{8,10},{9,11},{10,... | collective-permute-start | bytes 589832 | tf_op jit(solution)/shard_map/ppermute | solution.py:34
  18.9 6.6 %collective-permute-start.35 = (bf16[1536,128]{1,0:T(8,128)(2,1)S(1)}, bf16[1536,128]{1,0:T(8,128)(2,1)S(1)}, u32[]{:S(2)}, u32[]{:S(2)}) collective-permute-start(bf16[1536,128]{1,0:T(8,128)(2,1)S(1)} %collective-permute-done.34.refs_2_), channel_id=1, source_target_pairs={{0,1},{1,0},{2,3},{3,2},{4,5},{5,4},{6,7},{7,6},{8,9},{9,8},{10,11... | collective-permute-start | bytes 1179656 | tf_op jit(solution)/shard_map/ppermute | solution.py:34
  18.9 6.6 %collective-permute-start.37 = (bf16[1536,128]{1,0:T(8,128)(2,1)S(1)}, bf16[1536,128]{1,0:T(8,128)(2,1)S(1)}, u32[]{:S(2)}, u32[]{:S(2)}) collective-permute-start(bf16[1536,128]{1,0:T(8,128)(2,1)S(1)} %collective-permute-done.36.refs_4_), channel_id=1, source_target_pairs={{0,1},{1,0},{2,3},{3,2},{4,5},{5,4},{6,7},{7,6},{8,9},{9,8},{10,11... | collective-permute-start | bytes 1179656 | tf_op jit(solution)/shard_map/ppermute | solution.py:34
  23.6 1.9 %copy-start.8 = (bf16[768,128]{1,0:T(8,128)(2,1)}, bf16[768,128]{1,0:T(8,128)(2,1)S(1)}, u32[]{:S(2)}) copy-start(bf16[768,128]{1,0:T(8,128)(2,1)S(1)} %collective-permute-done.38.refs_6_) | copy-start | bytes 589828
  23.6 1.4 collective-permute-start.40
  24.0 1.5 copy-start.9
  24.0 1.4 collective-permute-start.41
  25.5 0.8 copy-start.6
  25.5 0.9 copy-start.7
  38.6 48.3 %collective-permute-start.55 = (bf16[3,12,128,128]{3,2,1,0:T(8,128)(2,1)}, bf16[3,12,128,128]{3,2,1,0:T(8,128)(2,1)}, u32[]{:S(2)}, u32[]{:S(2)}) collective-permute-start(bf16[3,12,128,128]{3,2,1,0:T(8,128)(2,1)} %get-tuple-element.196), channel_id=1, source_target_pairs={{0,8},{8,16},{16,24},{1,9},{9,17},{17,25},{2,10},{10,18},{18,26},{... | collective-permute-start | bytes 3538952 | tf_op jit(solution)/shard_map/ppermute | solution.py:39
  43.2 11.0 %collective-permute-start.48 = (bf16[1552,128]{1,0:T(8,128)(2,1)S(1)}, bf16[1552,128]{1,0:T(8,128)(2,1)S(1)}, u32[]{:S(2)}, u32[]{:S(2)}) collective-permute-start(bf16[1552,128]{1,0:T(8,128)(2,1)S(1)} %get-tuple-element.188.refs_10_), channel_id=1, source_target_pairs={{0,4},{1,5},{2,6},{3,7},{4,0},{5,1},{6,2},{7,3},{8,12},{9,13},{10,... | collective-permute-start | bytes 1191944 | tf_op jit(solution)/shard_map/ppermute | solution.py:34
  44.8 10.7 %collective-permute-start.46 = (bf16[1552,128]{1,0:T(8,128)(2,1)S(1)}, bf16[1552,128]{1,0:T(8,128)(2,1)S(1)}, u32[]{:S(2)}, u32[]{:S(2)}) collective-permute-start(bf16[1552,128]{1,0:T(8,128)(2,1)S(1)} %get-tuple-element.188.refs_10_), channel_id=1, source_target_pairs={{0,2},{1,3},{2,0},{3,1},{4,6},{5,7},{6,4},{7,5},{8,10},{9,11},{10,... | collective-permute-start | bytes 1191944 | tf_op jit(solution)/shard_map/ppermute | solution.py:34
  45.3 11.1 %collective-permute-start.45 = (bf16[1552,128]{1,0:T(8,128)(2,1)S(1)}, bf16[1552,128]{1,0:T(8,128)(2,1)S(1)}, u32[]{:S(2)}, u32[]{:S(2)}) collective-permute-start(bf16[1552,128]{1,0:T(8,128)(2,1)S(1)} %get-tuple-element.188.refs_10_), channel_id=1, source_target_pairs={{0,1},{1,0},{2,3},{3,2},{4,5},{5,4},{6,7},{7,6},{8,9},{9,8},{10,11... | collective-permute-start | bytes 1191944 | tf_op jit(solution)/shard_map/ppermute | solution.py:34
  54.2 7.0 %collective-permute-start.51 = (bf16[784,128]{1,0:T(8,128)(2,1)S(1)}, bf16[784,128]{1,0:T(8,128)(2,1)S(1)}, u32[]{:S(2)}, u32[]{:S(2)}) collective-permute-start(bf16[784,128]{1,0:T(8,128)(2,1)S(1)} %slice.129), channel_id=1, source_target_pairs={{0,2},{1,3},{2,0},{3,1},{4,6},{5,7},{6,4},{7,5},{8,10},{9,11},{10,... | collective-permute-start | bytes 602120 | tf_op jit(solution)/shard_map/ppermute | solution.py:34
  55.5 5.7 %collective-permute-start.50 = (bf16[768,128]{1,0:T(8,128)(2,1)S(1)}, bf16[768,128]{1,0:T(8,128)(2,1)S(1)}, u32[]{:S(2)}, u32[]{:S(2)}) collective-permute-start(bf16[768,128]{1,0:T(8,128)(2,1)S(1)} %slice.128), channel_id=1, source_target_pairs={{0,4},{1,5},{2,6},{3,7},{4,0},{5,1},{6,2},{7,3},{8,12},{9,13},{10,... | collective-permute-start | bytes 589832 | tf_op jit(solution)/shard_map/ppermute | solution.py:34
  56.5 6.9 %collective-permute-start.47 = (bf16[1552,128]{1,0:T(8,128)(2,1)S(1)}, bf16[1552,128]{1,0:T(8,128)(2,1)S(1)}, u32[]{:S(2)}, u32[]{:S(2)}) collective-permute-start(bf16[1552,128]{1,0:T(8,128)(2,1)S(1)} %collective-permute-done.46.refs_12_), channel_id=1, source_target_pairs={{0,1},{1,0},{2,3},{3,2},{4,5},{5,4},{6,7},{7,6},{8,9},{9,8},{10,11... | collective-permute-start | bytes 1191944 | tf_op jit(solution)/shard_map/ppermute | solution.py:34
  61.2 2.2 %collective-permute-start.49 = (bf16[1552,128]{1,0:T(8,128)(2,1)S(1)}, bf16[1552,128]{1,0:T(8,128)(2,1)S(1)}, u32[]{:S(2)}, u32[]{:S(2)}) collective-permute-start(bf16[1552,128]{1,0:T(8,128)(2,1)S(1)} %collective-permute-done.48.refs_14_), channel_id=1, source_target_pairs={{0,1},{1,0},{2,3},{3,2},{4,5},{5,4},{6,7},{7,6},{8,9},{9,8},{10,11... | collective-permute-start | bytes 1191944 | tf_op jit(solution)/shard_map/ppermute | solution.py:34
  61.2 2.0 %collective-permute-start.52 = (bf16[768,128]{1,0:T(8,128)(2,1)S(1)}, bf16[768,128]{1,0:T(8,128)(2,1)S(1)}, u32[]{:S(2)}, u32[]{:S(2)}) collective-permute-start(bf16[768,128]{1,0:T(8,128)(2,1)S(1)} %collective-permute-done.50.refs_16_), channel_id=1, source_target_pairs={{0,1},{1,0},{2,3},{3,2},{4,5},{5,4},{6,7},{7,6},{8,9},{9,8},{10,11... | collective-permute-start | bytes 589832 | tf_op jit(solution)/shard_map/ppermute | solution.py:34
  63.2 1.4 collective-permute-start.53
  63.4 23.5 %copy-start.1 = (f32[12,128,128]{2,1,0:T(8,128)S(1)}, f32[12,128,128]{2,1,0:T(8,128)}, u32[]{:S(2)}) copy-start(f32[12,128,128]{2,1,0:T(8,128)} %get-tuple-element.193) | copy-start | bytes 2359300
  63.4 23.5 %copy-start.14 = (s32[1,12]{1,0:T(1,128)S(1)}, s32[1,12]{1,0:T(1,128)}, u32[]{:S(2)}) copy-start(s32[1,12]{1,0:T(1,128)} %param.14) | copy-start | bytes 148
  87.7 13.2 %collective-permute-start = (bf16[1536,128]{1,0:T(8,128)(2,1)S(1)}, bf16[1536,128]{1,0:T(8,128)(2,1)S(1)}, u32[]{:S(2)}, u32[]{:S(2)}) collective-permute-start(bf16[1536,128]{1,0:T(8,128)(2,1)S(1)} %get-tuple-element.118), channel_id=1, source_target_pairs={{0,8},{8,16},{16,24},{1,9},{9,17},{17,25},{2,10},{10,18},{18,26},{... | collective-permute-start | bytes 1179656 | tf_op jit(solution)/shard_map/cond/branch_0_fun/ppermute | solution.py:39
  101.0 48.5 %collective-permute-start.2 = (bf16[8112,128]{1,0:T(8,128)(2,1)S(1)}, bf16[8112,128]{1,0:T(8,128)(2,1)S(1)}, u32[]{:S(2)}, u32[]{:S(2)}) collective-permute-start(bf16[8112,128]{1,0:T(8,128)(2,1)S(1)} %pack_update.3), channel_id=1, source_target_pairs={{0,8},{8,16},{16,24},{1,9},{9,17},{17,25},{2,10},{10,18},{18,26},{... | collective-permute-start | bytes 6230024 | tf_op jit(solution)/shard_map/cond/branch_0_fun/ppermute | solution.py:39
  103.4 10.3 %collective-permute-start.1 = (bf16[1536,128]{1,0:T(8,128)(2,1)S(1)}, bf16[1536,128]{1,0:T(8,128)(2,1)S(1)}, u32[]{:S(2)}, u32[]{:S(2)}) collective-permute-start(bf16[1536,128]{1,0:T(8,128)(2,1)S(1)} %collective-permute-done.refs_0_), channel_id=1, source_target_pairs={{0,2},{1,3},{2,0},{3,1},{4,6},{5,7},{6,4},{7,5},{8,10},{9,11},{10,... | collective-permute-start | bytes 1179656 | tf_op jit(solution)/shard_map/cond/branch_0_fun/ppermute | solution.py:34
  105.0 10.0 %collective-permute-start.5 = (bf16[1536,128]{1,0:T(8,128)(2,1)S(1)}, bf16[1536,128]{1,0:T(8,128)(2,1)S(1)}, u32[]{:S(2)}, u32[]{:S(2)}) collective-permute-start(bf16[1536,128]{1,0:T(8,128)(2,1)S(1)} %collective-permute-done.refs_0_), channel_id=1, source_target_pairs={{0,4},{1,5},{2,6},{3,7},{4,0},{5,1},{6,2},{7,3},{8,12},{9,13},{10,... | collective-permute-start | bytes 1179656 | tf_op jit(solution)/shard_map/cond/branch_0_fun/ppermute | solution.py:34
  105.5 12.2 %collective-permute-start.3 = (bf16[1536,128]{1,0:T(8,128)(2,1)S(1)}, bf16[1536,128]{1,0:T(8,128)(2,1)S(1)}, u32[]{:S(2)}, u32[]{:S(2)}) collective-permute-start(bf16[1536,128]{1,0:T(8,128)(2,1)S(1)} %collective-permute-done.refs_0_), channel_id=1, source_target_pairs={{0,1},{1,0},{2,3},{3,2},{4,5},{5,4},{6,7},{7,6},{8,9},{9,8},{10,11... | collective-permute-start | bytes 1179656 | tf_op jit(solution)/shard_map/cond/branch_0_fun/ppermute | solution.py:34
  115.0 5.7 %collective-permute-start.8 = (bf16[768,128]{1,0:T(8,128)(2,1)S(1)}, bf16[768,128]{1,0:T(8,128)(2,1)S(1)}, u32[]{:S(2)}, u32[]{:S(2)}) collective-permute-start(bf16[768,128]{1,0:T(8,128)(2,1)S(1)} %slice.121), channel_id=1, source_target_pairs={{0,2},{1,3},{2,0},{3,1},{4,6},{5,7},{6,4},{7,5},{8,10},{9,11},{10,... | collective-permute-start | bytes 589832 | tf_op jit(solution)/shard_map/cond/branch_0_fun/ppermute | solution.py:34
  115.6 5.7 %collective-permute-start.7 = (bf16[768,128]{1,0:T(8,128)(2,1)S(1)}, bf16[768,128]{1,0:T(8,128)(2,1)S(1)}, u32[]{:S(2)}, u32[]{:S(2)}) collective-permute-start(bf16[768,128]{1,0:T(8,128)(2,1)S(1)} %slice.120), channel_id=1, source_target_pairs={{0,4},{1,5},{2,6},{3,7},{4,0},{5,1},{6,2},{7,3},{8,12},{9,13},{10,... | collective-permute-start | bytes 589832 | tf_op jit(solution)/shard_map/cond/branch_0_fun/ppermute | solution.py:34
  117.2 5.7 %collective-permute-start.4 = (bf16[1536,128]{1,0:T(8,128)(2,1)S(1)}, bf16[1536,128]{1,0:T(8,128)(2,1)S(1)}, u32[]{:S(2)}, u32[]{:S(2)}) collective-permute-start(bf16[1536,128]{1,0:T(8,128)(2,1)S(1)} %collective-permute-done.1.refs_2_), channel_id=1, source_target_pairs={{0,1},{1,0},{2,3},{3,2},{4,5},{5,4},{6,7},{7,6},{8,9},{9,8},{10,11... | collective-permute-start | bytes 1179656 | tf_op jit(solution)/shard_map/cond/branch_0_fun/ppermute | solution.py:34
  117.7 5.2 %collective-permute-start.6 = (bf16[1536,128]{1,0:T(8,128)(2,1)S(1)}, bf16[1536,128]{1,0:T(8,128)(2,1)S(1)}, u32[]{:S(2)}, u32[]{:S(2)}) collective-permute-start(bf16[1536,128]{1,0:T(8,128)(2,1)S(1)} %collective-permute-done.5.refs_4_), channel_id=1, source_target_pairs={{0,1},{1,0},{2,3},{3,2},{4,5},{5,4},{6,7},{7,6},{8,9},{9,8},{10,11... | collective-permute-start | bytes 1179656 | tf_op jit(solution)/shard_map/cond/branch_0_fun/ppermute | solution.py:34
  120.7 2.1 %collective-permute-start.10 = (bf16[768,128]{1,0:T(8,128)(2,1)S(1)}, bf16[768,128]{1,0:T(8,128)(2,1)S(1)}, u32[]{:S(2)}, u32[]{:S(2)}) collective-permute-start(bf16[768,128]{1,0:T(8,128)(2,1)S(1)} %collective-permute-done.8.refs_7_), channel_id=1, source_target_pairs={{0,1},{1,0},{2,3},{3,2},{4,5},{5,4},{6,7},{7,6},{8,9},{9,8},{10,11... | collective-permute-start | bytes 589832 | tf_op jit(solution)/shard_map/cond/branch_0_fun/ppermute | solution.py:34
  121.4 1.5 collective-permute-start.9
  153.9 0.7 copy-start.12
  153.9 0.9 copy-start.13
  (2 other events, 1.4 us)

commit v4 on v3

--- a/solution.py
+++ b/solution.py
@@ -671,9 +671,8 @@
                     pltpu.VMEM((per, n_late + 2, width, width), F32),
                     dma(len(late), count // per),
                 ],
-                moved=20 * 1024 * 1024,
+                moved=400 * 1024 * 1024,
             )(table, coefs, vsrc, wsrc, in_hbm(by_group))
-            packed, passed = lax.optimization_barrier((packed, passed))
             arrived = onward(packed)
             kpieces = gathered(passed)
             rows_two, coefs = lax.optimization_barrier((kpieces[2][0], coefs))

time: 157 us -> 191 us (1.22)
  waiting for transfers between devices: 52.1 us -> 86.7 us
    ppermute x4, waiting for transfers between devices: 18 us -> 51.9 us  [onward(): return lax.ppermute(value, 'sec', [(i, i + 1) for i in range(length - 1)])]
  transfers between devices with their start and end apart: 34 -> 34, of which waited for: 15 -> 14; matrix products, arithmetic and copies ran while one was open for 6% -> 5% of each run, Pallas kernels for 29% -> 19%
where the time goes in v4:
time: 191 us; the launch traced here: 190 us
  waiting for transfers between devices  86.7 us (45%)
  Pallas kernels  49 us (26%)
  starting transfers between devices  30.8 us (16%)
  blocking collectives  8.46 us (4%)
  local copies, waits for them, and re-layouts  7.3 us (4%)
  other arithmetic  5.71 us (3%)
    ppermute x4, waiting for transfers between devices, onward(): return lax.ppermute(value, 'sec', [(i, i + 1) for i in range(length - 1)])  51.9 us
    ppermute x27, waiting for transfers between devices, exchange(): return lax.ppermute(value, 'blk', [(i, i ^ bit) for i in range(length)])  34.8 us
    ppermute x27, starting transfers between devices, exchange(): return lax.ppermute(value, 'blk', [(i, i ^ bit) for i in range(length)])  13.6 us
    pallas_call x1, Pallas kernels, shards(): call(functools.partial(second_kernel, places, count, cells, secs, late, u...  12.6 us
    ppermute x4, starting transfers between devices, onward(): return lax.ppermute(value, 'sec', [(i, i + 1) for i in range(length - 1)])  12.5 us
    pallas_call x1, Pallas kernels, shards(): call(functools.partial(first_kernel, places, count, then), 'ham_first', [...  12.2 us
    pallas_call x1, Pallas kernels, branch(): call(functools.partial(early_kernel, places, count, early), 'early_update...  11.2 us
    all_gather x1, blocking collectives, shards(): parts = lax.all_gather(sums, 'blk', axis=0)  8.46 us
  transfers between devices with their start and end apart: 34, of which 14 were waited for; matrix products, arithmetic and copies ran while one was open for 5% of the time, Pallas kernels for 19%

profile of v4, /device:TPU:8, one launch (start us, length us, event | category | flops | bytes accessed | tf_op | source)
XLA Modules:
  0.0 189.9 jit_solution(13730316646387628055)
XLA Ops:
  0.6 0.8 slice_bitcast_fusion.8
  1.5 1.3 fusion.3.refs_0_
  2.9 1.6 collective-permute-start.34
  4.5 1.5 collective-permute-start.36
  6.0 0.7 bitcast_minimum_fusion
  6.7 0.7 add_convert_fusion.3
  7.9 1.6 collective-permute-start.42
  9.5 1.1 collective-permute-start.43
  10.6 1.9 %collective-permute-start.44 = (f32[8,128]{1,0:T(8,128)S(1)}, f32[8,128]{1,0:T(8,128)S(1)}, u32[]{:S(2)}, u32[]{:S(2)}) collective-permute-start(f32[8,128]{1,0:T(8,128)S(1)} %dynamic_update_slice.3), channel_id=1, source_target_pairs={{0,24},{8,0},{16,8},{24,16},{1,25},{9,1},{17,9},{25,17},{2,26},{10... | collective-permute-start | bytes 12296 | tf_op jit(solution)/shard_map/ppermute | solution.py:588
  12.6 3.0 %slice_bitcast_fusion.6 = bf16[5,12,128,128]{3,2,1,0:T(8,128)(2,1)} fusion(bf16[1,20,12,128,128]{4,3,2,1,0:T(8,128)(2,1)} %param.10), kind=kLoop, calls=%fused_computation.15 | loop fusion | bytes 3932160 | tf_op jit(solution)/shard_map/slice | solution.py:589
  15.6 2.0 %collective-permute-start.54 = (bf16[5,12,128,128]{3,2,1,0:T(8,128)(2,1)}, bf16[5,12,128,128]{3,2,1,0:T(8,128)(2,1)}, u32[]{:S(2)}, u32[]{:S(2)}) collective-permute-start(bf16[5,12,128,128]{3,2,1,0:T(8,128)(2,1)} %slice_bitcast_fusion.6), channel_id=1, source_target_pairs={{0,8},{8,16},{16,24},{1,9},{9,17},{17,25},{2,10},{10,18},{18,26},{... | collective-permute-start | bytes 5898248 | tf_op jit(solution)/shard_map/ppermute | solution.py:39
  17.7 0.6 collective-permute-start.38
  18.3 0.6 collective-permute-start.39
  18.9 0.5 collective-permute-start.37
  19.4 4.2 %collective-permute-done.38.refs_6_ = bf16[768,128]{1,0:T(8,128)(2,1)S(1)} collective-permute-done((bf16[768,128]{1,0:T(8,128)(2,1)S(1)}, bf16[768,128]{1,0:T(8,128)(2,1)S(1)}, u32[]{:S(2)}, u32[]{:S(2)}) %collective-permute-start.38) | collective-permute-done | bytes 196640 | tf_op jit(solution)/shard_map/ppermute | solution.py:34
  24.3 0.8 collective-permute-done.40.refs_8_
  26.4 12.2 %ham_first.1 = (f32[12,128,128]{2,1,0:T(8,128)}, bf16[1552,128]{1,0:T(8,128)(2,1)S(1)}, bf16[3,12,128,128]{3,2,1,0:T(8,128)(2,1)}) custom-call(s32[12]{0:T(128)S(1)} %bitcast.63, s32[2]{0:T(128)S(1)} %pad_add_fusion.device, s32[12,2]{1,0:T(8,128)S(1)} %copy.14.dims, f32[8,128]{1,0:T(8,128)S(1)} %add_add_fusion.table, bf16[1536,128]{1,0:T(8,128)(2,1)} %copy-done.2, ...), custom_call_target="tpu_custom_call" | custom-call | flops 1 | bytes 1 | tf_op jit(solution)/shard_map/ham_first/pallas_call | solution.py:622
  38.6 4.6 %collective-permute-start.55 = (bf16[3,12,128,128]{3,2,1,0:T(8,128)(2,1)}, bf16[3,12,128,128]{3,2,1,0:T(8,128)(2,1)}, u32[]{:S(2)}, u32[]{:S(2)}) collective-permute-start(bf16[3,12,128,128]{3,2,1,0:T(8,128)(2,1)} %get-tuple-element.190), channel_id=1, source_target_pairs={{0,8},{8,16},{16,24},{1,9},{9,17},{17,25},{2,10},{10,18},{18,26},{... | collective-permute-start | bytes 3538952 | tf_op jit(solution)/shard_map/ppermute | solution.py:39
  43.2 1.6 collective-permute-start.48
  44.8 0.5 collective-permute-start.46
  45.3 8.9 %collective-permute-done.48.refs_14_ = bf16[1552,128]{1,0:T(8,128)(2,1)S(1)} collective-permute-done((bf16[1552,128]{1,0:T(8,128)(2,1)S(1)}, bf16[1552,128]{1,0:T(8,128)(2,1)S(1)}, u32[]{:S(2)}, u32[]{:S(2)}) %collective-permute-start.48) | collective-permute-done | bytes 397344 | tf_op jit(solution)/shard_map/ppermute | solution.py:34
  54.3 0.6 collective-permute-start.51
  54.9 0.6 collective-permute-done.46.refs_12_
  55.5 1.0 collective-permute-start.50
  56.5 4.8 %collective-permute-done.50.refs_16_ = bf16[768,128]{1,0:T(8,128)(2,1)S(1)} collective-permute-done((bf16[768,128]{1,0:T(8,128)(2,1)S(1)}, bf16[768,128]{1,0:T(8,128)(2,1)S(1)}, u32[]{:S(2)}, u32[]{:S(2)}) %collective-permute-start.50) | collective-permute-done | bytes 196640 | tf_op jit(solution)/shard_map/ppermute | solution.py:34
  61.2 0.5 collective-permute-start.52
  61.7 1.5 collective-permute-done.52.refs_18_
  63.4 1.3 collective-permute-done.53.refs_19_
  64.7 12.6 %ham_second.1 = (f32[12,128,128]{2,1,0:T(8,128)S(1)}, f32[8,128]{1,0:T(8,128)S(1)}, s32[2,8,128]{2,1,0:T(8,128)S(1)}, bf16[5,12,128,128]{3,2,1,0:T(8,128)(2,1)S(1)}, bf16[5,12,128,128]{3,2,1,0:T(8,128)(2,1)S(1)}) custom-call(s32[12]{0:T(128)S(1)} %bitcast.64, s32[2]{0:T(128)S(1)} %pad_add_fusion.device, s32[12,2]{1,0:T(8,128)S(1)} %copy.14.dims, ...), custom_call_target="tpu_custom_call" | custom-call | flops 1 | bytes 1 | tf_op jit(solution)/shard_map/ham_second/pallas_call | solution.py:632
  77.3 0.5 slice.119
  78.4 8.5 %all-gather = f32[64,128]{1,0:T(8,128)S(1)} all-gather(f32[8,128]{1,0:T(8,128)S(1)} %get-tuple-element.183), channel_id=2, replica_groups=mesh['sec'=4,'blk'=8] {'blk'}, dimensions={0}, use_global_device_ids=true | all-gather | bytes 36864 | tf_op jit(solution)/shard_map/all_gather | solution.py:645
  86.9 102.1 %conditional.4 = (bf16[1,12,128,128]{3,2,1,0:T(8,128)(2,1)S(1)}, f32[1]{0:T(128)}, bf16[1,20,12,128,128]{4,3,2,1,0:T(8,128)(2,1)}, bf16[1,12,128,128]{3,2,1,0:T(8,128)(2,1)S(1)}) conditional(s32[]{:T(128)} %bitcast.43, (s32[1,12]{1,0:T(1,128)S(1)}, f32[8,8,128]{2,1,0:T(8,128)S(1)}, bf16[5,12,128,128]{3,2,1,0:T(8,128)(2,1)S(1)}, ...), branch_computations={%region_0.1_spmd, %region_1.2_spmd, %region_2.3_spmd} | conditional | flops 1966084 | bytes 454967712
  86.9 0.8 ritz.3
  87.8 8.0 %pack_update.3 = bf16[8112,128]{1,0:T(8,128)(2,1)S(1)} custom-call(s32[8,128]{1,0:T(8,128)S(1)} %get-tuple-element.201.table, f32[8,128]{1,0:T(8,128)S(1)} %get-tuple-element.117.coefs, bf16[5,12,128,128]{3,2,1,0:T(8,128)(2,1)S(1)} %get-tuple-element.113.vsrc, bf16[5,12,128,128]{3,2,1,0:T(8,128)(2,1)S(1)} %get-tuple-element.114.wsrc, ...), custom_call_target="tpu_custom_call" | custom-call | flops 1 | bytes 419430400 | tf_op jit(solution)/shard_map/cond/branch_0_fun/pack_update/pallas_call | solution.py:663
  95.8 2.6 %collective-permute-start.2 = (bf16[8112,128]{1,0:T(8,128)(2,1)S(1)}, bf16[8112,128]{1,0:T(8,128)(2,1)S(1)}, u32[]{:S(2)}, u32[]{:S(2)}) collective-permute-start(bf16[8112,128]{1,0:T(8,128)(2,1)S(1)} %pack_update.3), channel_id=1, source_target_pairs={{0,8},{8,16},{16,24},{1,9},{9,17},{17,25},{2,10},{10,18},{18,26},{... | collective-permute-start | bytes 6230024 | tf_op jit(solution)/shard_map/cond/branch_0_fun/ppermute | solution.py:39
  98.4 3.3 %collective-permute-start = (bf16[1536,128]{1,0:T(8,128)(2,1)S(1)}, bf16[1536,128]{1,0:T(8,128)(2,1)S(1)}, u32[]{:S(2)}, u32[]{:S(2)}) collective-permute-start(bf16[1536,128]{1,0:T(8,128)(2,1)S(1)} %get-tuple-element.115), channel_id=1, source_target_pairs={{0,8},{8,16},{16,24},{1,9},{9,17},{17,25},{2,10},{10,18},{18,26},{... | collective-permute-start | bytes 1179656 | tf_op jit(solution)/shard_map/cond/branch_0_fun/ppermute | solution.py:39
  101.7 51.9 %collective-permute-done.refs_0_ = bf16[1536,128]{1,0:T(8,128)(2,1)S(1)} collective-permute-done((bf16[1536,128]{1,0:T(8,128)(2,1)S(1)}, bf16[1536,128]{1,0:T(8,128)(2,1)S(1)}, u32[]{:S(2)}, u32[]{:S(2)}) %collective-permute-start) | collective-permute-done | bytes 393248 | tf_op jit(solution)/shard_map/cond/branch_0_fun/ppermute | solution.py:39
  153.6 1.6 collective-permute-start.1
  155.6 8.6 %collective-permute-done.1.refs_2_ = bf16[1536,128]{1,0:T(8,128)(2,1)S(1)} collective-permute-done((bf16[1536,128]{1,0:T(8,128)(2,1)S(1)}, bf16[1536,128]{1,0:T(8,128)(2,1)S(1)}, u32[]{:S(2)}, u32[]{:S(2)}) %collective-permute-start.1) | collective-permute-done | bytes 393248 | tf_op jit(solution)/shard_map/cond/branch_0_fun/ppermute | solution.py:34
  164.2 1.4 collective-permute-done.5.refs_4_
  166.0 1.4 collective-permute-start.7
  167.4 0.5 fusion.5
  168.4 1.4 fusion
  169.8 1.5 collective-permute-done.8.refs_7_
  171.8 1.4 multiply_add_fusion
  173.3 11.2 %early_update.3.so_far = bf16[4,5,12,128,128]{4,3,2,1,0:T(8,128)(2,1)} custom-call(s32[8,128]{1,0:T(8,128)S(1)} %get-tuple-element.202.table, s32[2]{0:T(128)S(1)} %get-tuple-element.123.device, s32[1]{0:T(128)} %bitcast.6.first_sec, bf16[1536,128]{1,0:T(8,128)(2,1)S(1)} %collective-permute-done.refs_0_, ...), custom_call_target="tpu_custom_call" | custom-call | flops 1 | bytes 1 | tf_op jit(solution)/shard_map/cond/branch_0_fun/early_update/pallas_call | solution.py:683
  184.6 4.3 %unpack_update.3 = bf16[4,5,12,128,128]{4,3,2,1,0:T(8,128)(2,1)} custom-call(s32[8,128]{1,0:T(8,128)S(1)} %get-tuple-element.202.table, s32[1]{0:T(128)} %bitcast.6.first_sec, bf16[8112,128]{1,0:T(8,128)(2,1)S(1)} %collective-permute-done.2.packed, bf16[4,5,12,128,128]{4,3,2,1,0:T(8,128)(2,1)} %bitcast.69, ...), custom_call_target="tpu_custom_call", output_to_operand_aliasing={{}: (4, {})} | custom-call | flops 1 | bytes 1 | tf_op jit(solution)/shard_map/cond/branch_0_fun/unpack_update/pallas_call | solution.py:698
  189.0 0.7 copy-done.12
  (83 shorter events, 5.0 us)
Async XLA Ops:
  2.8 14.9 %copy-start.2 = (bf16[1536,128]{1,0:T(8,128)(2,1)}, bf16[1536,128]{1,0:T(8,128)(2,1)S(1)}, u32[]{:S(2)}) copy-start(bf16[1536,128]{1,0:T(8,128)(2,1)S(1)} %fusion.3.refs_0_) | copy-start | bytes 1179652
  2.8 5.0 %collective-permute-start.33 = (bf16[1536,128]{1,0:T(8,128)(2,1)S(1)}, bf16[1536,128]{1,0:T(8,128)(2,1)S(1)}, u32[]{:S(2)}, u32[]{:S(2)}) collective-permute-start(bf16[1536,128]{1,0:T(8,128)(2,1)S(1)} %fusion.3.refs_0_), channel_id=1, source_target_pairs={{0,1},{1,0},{2,3},{3,2},{4,5},{5,4},{6,7},{7,6},{8,9},{9,8},{10,11... | collective-permute-start | bytes 1179656 | tf_op jit(solution)/shard_map/ppermute | solution.py:34
  2.9 14.7 %collective-permute-start.34 = (bf16[1536,128]{1,0:T(8,128)(2,1)S(1)}, bf16[1536,128]{1,0:T(8,128)(2,1)S(1)}, u32[]{:S(2)}, u32[]{:S(2)}) collective-permute-start(bf16[1536,128]{1,0:T(8,128)(2,1)S(1)} %fusion.3.refs_0_), channel_id=1, source_target_pairs={{0,2},{1,3},{2,0},{3,1},{4,6},{5,7},{6,4},{7,5},{8,10},{9,11},{10,... | collective-permute-start | bytes 1179656 | tf_op jit(solution)/shard_map/ppermute | solution.py:34
  4.5 13.8 %collective-permute-start.36 = (bf16[1536,128]{1,0:T(8,128)(2,1)S(1)}, bf16[1536,128]{1,0:T(8,128)(2,1)S(1)}, u32[]{:S(2)}, u32[]{:S(2)}) collective-permute-start(bf16[1536,128]{1,0:T(8,128)(2,1)S(1)} %fusion.3.refs_0_), channel_id=1, source_target_pairs={{0,4},{1,5},{2,6},{3,7},{4,0},{5,1},{6,2},{7,3},{8,12},{9,13},{10,... | collective-permute-start | bytes 1179656 | tf_op jit(solution)/shard_map/ppermute | solution.py:34
  7.8 16.3 %copy-start.15 = (s32[1,12,2]{1,2,0:T(2,128)S(1)}, s32[1,12,2]{1,2,0:T(2,128)}, u32[]{:S(2)}) copy-start(s32[1,12,2]{1,2,0:T(2,128)} %param.13) | copy-start | bytes 292
  7.9 18.5 %copy-start = (s32[1,12]{1,0:T(1,128)S(1)}, s32[1,12]{1,0:T(1,128)}, u32[]{:S(2)}) copy-start(s32[1,12]{1,0:T(1,128)} %param.12) | copy-start | bytes 148
  7.9 9.8 %copy-start.5 = (bf16[1536,128]{1,0:T(8,128)(2,1)}, bf16[1536,128]{1,0:T(8,128)(2,1)S(1)}, u32[]{:S(2)}) copy-start(bf16[1536,128]{1,0:T(8,128)(2,1)S(1)} %collective-permute-done.33.refs_1_) | copy-start | bytes 1179652
  7.9 7.7 %collective-permute-start.42 = (f32[8,128]{1,0:T(8,128)S(1)}, f32[8,128]{1,0:T(8,128)S(1)}, u32[]{:S(2)}, u32[]{:S(2)}) collective-permute-start(f32[8,128]{1,0:T(8,128)S(1)} %dynamic_update_slice.3), channel_id=1, source_target_pairs={{0,8},{8,16},{16,24},{24,0},{1,9},{9,17},{17,25},{25,1},{2,10},{10... | collective-permute-start | bytes 12296 | tf_op jit(solution)/shard_map/ppermute | solution.py:588
  9.5 6.1 %collective-permute-start.43 = (f32[8,128]{1,0:T(8,128)S(1)}, f32[8,128]{1,0:T(8,128)S(1)}, u32[]{:S(2)}, u32[]{:S(2)}) collective-permute-start(f32[8,128]{1,0:T(8,128)S(1)} %dynamic_update_slice.3), channel_id=1, source_target_pairs={{0,16},{8,24},{16,0},{24,8},{1,17},{9,25},{17,1},{25,9},{2,18},{10... | collective-permute-start | bytes 12296 | tf_op jit(solution)/shard_map/ppermute | solution.py:588
  10.6 5.0 %collective-permute-start.44 = (f32[8,128]{1,0:T(8,128)S(1)}, f32[8,128]{1,0:T(8,128)S(1)}, u32[]{:S(2)}, u32[]{:S(2)}) collective-permute-start(f32[8,128]{1,0:T(8,128)S(1)} %dynamic_update_slice.3), channel_id=1, source_target_pairs={{0,24},{8,0},{16,8},{24,16},{1,25},{9,1},{17,9},{25,17},{2,26},{10... | collective-permute-start | bytes 12296 | tf_op jit(solution)/shard_map/ppermute | solution.py:588
  15.6 71.3 %collective-permute-start.54 = (bf16[5,12,128,128]{3,2,1,0:T(8,128)(2,1)}, bf16[5,12,128,128]{3,2,1,0:T(8,128)(2,1)}, u32[]{:S(2)}, u32[]{:S(2)}) collective-permute-start(bf16[5,12,128,128]{3,2,1,0:T(8,128)(2,1)} %slice_bitcast_fusion.6), channel_id=1, source_target_pairs={{0,8},{8,16},{16,24},{1,9},{9,17},{17,25},{2,10},{10,18},{18,26},{... | collective-permute-start | bytes 5898248 | tf_op jit(solution)/shard_map/ppermute | solution.py:39
  17.6 7.9 %copy-start.3 = (bf16[1536,128]{1,0:T(8,128)(2,1)}, bf16[1536,128]{1,0:T(8,128)(2,1)S(1)}, u32[]{:S(2)}) copy-start(bf16[1536,128]{1,0:T(8,128)(2,1)S(1)} %collective-permute-done.34.refs_2_) | copy-start | bytes 1179652
  17.7 5.9 %collective-permute-start.38 = (bf16[768,128]{1,0:T(8,128)(2,1)S(1)}, bf16[768,128]{1,0:T(8,128)(2,1)S(1)}, u32[]{:S(2)}, u32[]{:S(2)}) collective-permute-start(bf16[768,128]{1,0:T(8,128)(2,1)S(1)} %slice.126), channel_id=1, source_target_pairs={{0,4},{1,5},{2,6},{3,7},{4,0},{5,1},{6,2},{7,3},{8,12},{9,13},{10,... | collective-permute-start | bytes 589832 | tf_op jit(solution)/shard_map/ppermute | solution.py:34
  18.3 7.2 %copy-start.4 = (bf16[1536,128]{1,0:T(8,128)(2,1)}, bf16[1536,128]{1,0:T(8,128)(2,1)S(1)}, u32[]{:S(2)}) copy-start(bf16[1536,128]{1,0:T(8,128)(2,1)S(1)} %collective-permute-done.36.refs_4_) | copy-start | bytes 1179652
  18.3 5.7 %collective-permute-start.39 = (bf16[768,128]{1,0:T(8,128)(2,1)S(1)}, bf16[768,128]{1,0:T(8,128)(2,1)S(1)}, u32[]{:S(2)}, u32[]{:S(2)}) collective-permute-start(bf16[768,128]{1,0:T(8,128)(2,1)S(1)} %slice.127), channel_id=1, source_target_pairs={{0,2},{1,3},{2,0},{3,1},{4,6},{5,7},{6,4},{7,5},{8,10},{9,11},{10,... | collective-permute-start | bytes 589832 | tf_op jit(solution)/shard_map/ppermute | solution.py:34
  18.9 6.6 %collective-permute-start.35 = (bf16[1536,128]{1,0:T(8,128)(2,1)S(1)}, bf16[1536,128]{1,0:T(8,128)(2,1)S(1)}, u32[]{:S(2)}, u32[]{:S(2)}) collective-permute-start(bf16[1536,128]{1,0:T(8,128)(2,1)S(1)} %collective-permute-done.34.refs_2_), channel_id=1, source_target_pairs={{0,1},{1,0},{2,3},{3,2},{4,5},{5,4},{6,7},{7,6},{8,9},{9,8},{10,11... | collective-permute-start | bytes 1179656 | tf_op jit(solution)/shard_map/ppermute | solution.py:34
  18.9 6.6 %collective-permute-start.37 = (bf16[1536,128]{1,0:T(8,128)(2,1)S(1)}, bf16[1536,128]{1,0:T(8,128)(2,1)S(1)}, u32[]{:S(2)}, u32[]{:S(2)}) collective-permute-start(bf16[1536,128]{1,0:T(8,128)(2,1)S(1)} %collective-permute-done.36.refs_4_), channel_id=1, source_target_pairs={{0,1},{1,0},{2,3},{3,2},{4,5},{5,4},{6,7},{7,6},{8,9},{9,8},{10,11... | collective-permute-start | bytes 1179656 | tf_op jit(solution)/shard_map/ppermute | solution.py:34
  23.6 1.9 %copy-start.8 = (bf16[768,128]{1,0:T(8,128)(2,1)}, bf16[768,128]{1,0:T(8,128)(2,1)S(1)}, u32[]{:S(2)}) copy-start(bf16[768,128]{1,0:T(8,128)(2,1)S(1)} %collective-permute-done.38.refs_6_) | copy-start | bytes 589828
  23.6 1.4 collective-permute-start.40
  24.0 1.5 copy-start.9
  24.0 1.4 collective-permute-start.41
  25.5 0.8 copy-start.6
  25.5 0.9 copy-start.7
  38.6 48.3 %collective-permute-start.55 = (bf16[3,12,128,128]{3,2,1,0:T(8,128)(2,1)}, bf16[3,12,128,128]{3,2,1,0:T(8,128)(2,1)}, u32[]{:S(2)}, u32[]{:S(2)}) collective-permute-start(bf16[3,12,128,128]{3,2,1,0:T(8,128)(2,1)} %get-tuple-element.190), channel_id=1, source_target_pairs={{0,8},{8,16},{16,24},{1,9},{9,17},{17,25},{2,10},{10,18},{18,26},{... | collective-permute-start | bytes 3538952 | tf_op jit(solution)/shard_map/ppermute | solution.py:39
  43.2 11.0 %collective-permute-start.48 = (bf16[1552,128]{1,0:T(8,128)(2,1)S(1)}, bf16[1552,128]{1,0:T(8,128)(2,1)S(1)}, u32[]{:S(2)}, u32[]{:S(2)}) collective-permute-start(bf16[1552,128]{1,0:T(8,128)(2,1)S(1)} %get-tuple-element.182.refs_10_), channel_id=1, source_target_pairs={{0,4},{1,5},{2,6},{3,7},{4,0},{5,1},{6,2},{7,3},{8,12},{9,13},{10,... | collective-permute-start | bytes 1191944 | tf_op jit(solution)/shard_map/ppermute | solution.py:34
  44.8 10.7 %collective-permute-start.46 = (bf16[1552,128]{1,0:T(8,128)(2,1)S(1)}, bf16[1552,128]{1,0:T(8,128)(2,1)S(1)}, u32[]{:S(2)}, u32[]{:S(2)}) collective-permute-start(bf16[1552,128]{1,0:T(8,128)(2,1)S(1)} %get-tuple-element.182.refs_10_), channel_id=1, source_target_pairs={{0,2},{1,3},{2,0},{3,1},{4,6},{5,7},{6,4},{7,5},{8,10},{9,11},{10,... | collective-permute-start | bytes 1191944 | tf_op jit(solution)/shard_map/ppermute | solution.py:34
  45.3 11.1 %collective-permute-start.45 = (bf16[1552,128]{1,0:T(8,128)(2,1)S(1)}, bf16[1552,128]{1,0:T(8,128)(2,1)S(1)}, u32[]{:S(2)}, u32[]{:S(2)}) collective-permute-start(bf16[1552,128]{1,0:T(8,128)(2,1)S(1)} %get-tuple-element.182.refs_10_), channel_id=1, source_target_pairs={{0,1},{1,0},{2,3},{3,2},{4,5},{5,4},{6,7},{7,6},{8,9},{9,8},{10,11... | collective-permute-start | bytes 1191944 | tf_op jit(solution)/shard_map/ppermute | solution.py:34
  54.3 7.0 %collective-permute-start.51 = (bf16[784,128]{1,0:T(8,128)(2,1)S(1)}, bf16[784,128]{1,0:T(8,128)(2,1)S(1)}, u32[]{:S(2)}, u32[]{:S(2)}) collective-permute-start(bf16[784,128]{1,0:T(8,128)(2,1)S(1)} %slice.129), channel_id=1, source_target_pairs={{0,2},{1,3},{2,0},{3,1},{4,6},{5,7},{6,4},{7,5},{8,10},{9,11},{10,... | collective-permute-start | bytes 602120 | tf_op jit(solution)/shard_map/ppermute | solution.py:34
  55.5 5.7 %collective-permute-start.50 = (bf16[768,128]{1,0:T(8,128)(2,1)S(1)}, bf16[768,128]{1,0:T(8,128)(2,1)S(1)}, u32[]{:S(2)}, u32[]{:S(2)}) collective-permute-start(bf16[768,128]{1,0:T(8,128)(2,1)S(1)} %slice.128), channel_id=1, source_target_pairs={{0,4},{1,5},{2,6},{3,7},{4,0},{5,1},{6,2},{7,3},{8,12},{9,13},{10,... | collective-permute-start | bytes 589832 | tf_op jit(solution)/shard_map/ppermute | solution.py:34
  56.5 6.9 %collective-permute-start.47 = (bf16[1552,128]{1,0:T(8,128)(2,1)S(1)}, bf16[1552,128]{1,0:T(8,128)(2,1)S(1)}, u32[]{:S(2)}, u32[]{:S(2)}) collective-permute-start(bf16[1552,128]{1,0:T(8,128)(2,1)S(1)} %collective-permute-done.46.refs_12_), channel_id=1, source_target_pairs={{0,1},{1,0},{2,3},{3,2},{4,5},{5,4},{6,7},{7,6},{8,9},{9,8},{10,11... | collective-permute-start | bytes 1191944 | tf_op jit(solution)/shard_map/ppermute | solution.py:34
  61.2 2.2 %collective-permute-start.49 = (bf16[1552,128]{1,0:T(8,128)(2,1)S(1)}, bf16[1552,128]{1,0:T(8,128)(2,1)S(1)}, u32[]{:S(2)}, u32[]{:S(2)}) collective-permute-start(bf16[1552,128]{1,0:T(8,128)(2,1)S(1)} %collective-permute-done.48.refs_14_), channel_id=1, source_target_pairs={{0,1},{1,0},{2,3},{3,2},{4,5},{5,4},{6,7},{7,6},{8,9},{9,8},{10,11... | collective-permute-start | bytes 1191944 | tf_op jit(solution)/shard_map/ppermute | solution.py:34
  61.2 2.0 %collective-permute-start.52 = (bf16[768,128]{1,0:T(8,128)(2,1)S(1)}, bf16[768,128]{1,0:T(8,128)(2,1)S(1)}, u32[]{:S(2)}, u32[]{:S(2)}) collective-permute-start(bf16[768,128]{1,0:T(8,128)(2,1)S(1)} %collective-permute-done.50.refs_16_), channel_id=1, source_target_pairs={{0,1},{1,0},{2,3},{3,2},{4,5},{5,4},{6,7},{7,6},{8,9},{9,8},{10,11... | collective-permute-start | bytes 589832 | tf_op jit(solution)/shard_map/ppermute | solution.py:34
  63.2 1.4 collective-permute-start.53
  63.4 23.5 %copy-start.1 = (f32[12,128,128]{2,1,0:T(8,128)S(1)}, f32[12,128,128]{2,1,0:T(8,128)}, u32[]{:S(2)}) copy-start(f32[12,128,128]{2,1,0:T(8,128)} %get-tuple-element.186) | copy-start | bytes 2359300
  63.4 23.5 %copy-start.14 = (s32[1,12]{1,0:T(1,128)S(1)}, s32[1,12]{1,0:T(1,128)}, u32[]{:S(2)}) copy-start(s32[1,12]{1,0:T(1,128)} %param.14) | copy-start | bytes 148
  95.8 88.8 %collective-permute-start.2 = (bf16[8112,128]{1,0:T(8,128)(2,1)S(1)}, bf16[8112,128]{1,0:T(8,128)(2,1)S(1)}, u32[]{:S(2)}, u32[]{:S(2)}) collective-permute-start(bf16[8112,128]{1,0:T(8,128)(2,1)S(1)} %pack_update.3), channel_id=1, source_target_pairs={{0,8},{8,16},{16,24},{1,9},{9,17},{17,25},{2,10},{10,18},{18,26},{... | collective-permute-start | bytes 6230024 | tf_op jit(solution)/shard_map/cond/branch_0_fun/ppermute | solution.py:39
  98.4 55.2 %collective-permute-start = (bf16[1536,128]{1,0:T(8,128)(2,1)S(1)}, bf16[1536,128]{1,0:T(8,128)(2,1)S(1)}, u32[]{:S(2)}, u32[]{:S(2)}) collective-permute-start(bf16[1536,128]{1,0:T(8,128)(2,1)S(1)} %get-tuple-element.115), channel_id=1, source_target_pairs={{0,8},{8,16},{16,24},{1,9},{9,17},{17,25},{2,10},{10,18},{18,26},{... | collective-permute-start | bytes 1179656 | tf_op jit(solution)/shard_map/cond/branch_0_fun/ppermute | solution.py:39
  153.6 10.6 %collective-permute-start.1 = (bf16[1536,128]{1,0:T(8,128)(2,1)S(1)}, bf16[1536,128]{1,0:T(8,128)(2,1)S(1)}, u32[]{:S(2)}, u32[]{:S(2)}) collective-permute-start(bf16[1536,128]{1,0:T(8,128)(2,1)S(1)} %collective-permute-done.refs_0_), channel_id=1, source_target_pairs={{0,2},{1,3},{2,0},{3,1},{4,6},{5,7},{6,4},{7,5},{8,10},{9,11},{10,... | collective-permute-start | bytes 1179656 | tf_op jit(solution)/shard_map/cond/branch_0_fun/ppermute | solution.py:34
  155.2 10.4 %collective-permute-start.5 = (bf16[1536,128]{1,0:T(8,128)(2,1)S(1)}, bf16[1536,128]{1,0:T(8,128)(2,1)S(1)}, u32[]{:S(2)}, u32[]{:S(2)}) collective-permute-start(bf16[1536,128]{1,0:T(8,128)(2,1)S(1)} %collective-permute-done.refs_0_), channel_id=1, source_target_pairs={{0,4},{1,5},{2,6},{3,7},{4,0},{5,1},{6,2},{7,3},{8,12},{9,13},{10,... | collective-permute-start | bytes 1179656 | tf_op jit(solution)/shard_map/cond/branch_0_fun/ppermute | solution.py:34
  155.6 12.3 %collective-permute-start.3 = (bf16[1536,128]{1,0:T(8,128)(2,1)S(1)}, bf16[1536,128]{1,0:T(8,128)(2,1)S(1)}, u32[]{:S(2)}, u32[]{:S(2)}) collective-permute-start(bf16[1536,128]{1,0:T(8,128)(2,1)S(1)} %collective-permute-done.refs_0_), channel_id=1, source_target_pairs={{0,1},{1,0},{2,3},{3,2},{4,5},{5,4},{6,7},{7,6},{8,9},{9,8},{10,11... | collective-permute-start | bytes 1179656 | tf_op jit(solution)/shard_map/cond/branch_0_fun/ppermute | solution.py:34
  165.6 5.7 %collective-permute-start.8 = (bf16[768,128]{1,0:T(8,128)(2,1)S(1)}, bf16[768,128]{1,0:T(8,128)(2,1)S(1)}, u32[]{:S(2)}, u32[]{:S(2)}) collective-permute-start(bf16[768,128]{1,0:T(8,128)(2,1)S(1)} %slice.121), channel_id=1, source_target_pairs={{0,2},{1,3},{2,0},{3,1},{4,6},{5,7},{6,4},{7,5},{8,10},{9,11},{10,... | collective-permute-start | bytes 589832 | tf_op jit(solution)/shard_map/cond/branch_0_fun/ppermute | solution.py:34
  166.0 5.7 %collective-permute-start.7 = (bf16[768,128]{1,0:T(8,128)(2,1)S(1)}, bf16[768,128]{1,0:T(8,128)(2,1)S(1)}, u32[]{:S(2)}, u32[]{:S(2)}) collective-permute-start(bf16[768,128]{1,0:T(8,128)(2,1)S(1)} %slice.120), channel_id=1, source_target_pairs={{0,4},{1,5},{2,6},{3,7},{4,0},{5,1},{6,2},{7,3},{8,12},{9,13},{10,... | collective-permute-start | bytes 589832 | tf_op jit(solution)/shard_map/cond/branch_0_fun/ppermute | solution.py:34
  167.4 5.9 %collective-permute-start.4 = (bf16[1536,128]{1,0:T(8,128)(2,1)S(1)}, bf16[1536,128]{1,0:T(8,128)(2,1)S(1)}, u32[]{:S(2)}, u32[]{:S(2)}) collective-permute-start(bf16[1536,128]{1,0:T(8,128)(2,1)S(1)} %collective-permute-done.1.refs_2_), channel_id=1, source_target_pairs={{0,1},{1,0},{2,3},{3,2},{4,5},{5,4},{6,7},{7,6},{8,9},{9,8},{10,11... | collective-permute-start | bytes 1179656 | tf_op jit(solution)/shard_map/cond/branch_0_fun/ppermute | solution.py:34
  167.9 5.4 %collective-permute-start.6 = (bf16[1536,128]{1,0:T(8,128)(2,1)S(1)}, bf16[1536,128]{1,0:T(8,128)(2,1)S(1)}, u32[]{:S(2)}, u32[]{:S(2)}) collective-permute-start(bf16[1536,128]{1,0:T(8,128)(2,1)S(1)} %collective-permute-done.5.refs_4_), channel_id=1, source_target_pairs={{0,1},{1,0},{2,3},{3,2},{4,5},{5,4},{6,7},{7,6},{8,9},{9,8},{10,11... | collective-permute-start | bytes 1179656 | tf_op jit(solution)/shard_map/cond/branch_0_fun/ppermute | solution.py:34
  171.3 2.0 %collective-permute-start.10 = (bf16[768,128]{1,0:T(8,128)(2,1)S(1)}, bf16[768,128]{1,0:T(8,128)(2,1)S(1)}, u32[]{:S(2)}, u32[]{:S(2)}) collective-permute-start(bf16[768,128]{1,0:T(8,128)(2,1)S(1)} %collective-permute-done.8.refs_7_), channel_id=1, source_target_pairs={{0,1},{1,0},{2,3},{3,2},{4,5},{5,4},{6,7},{7,6},{8,9},{9,8},{10,11... | collective-permute-start | bytes 589832 | tf_op jit(solution)/shard_map/cond/branch_0_fun/ppermute | solution.py:34
  171.7 1.6 collective-permute-start.9
  189.0 0.7 copy-start.12
  189.0 0.9 copy-start.13
  (2 other events, 1.4 us)
